TPU v7x, 768 devices: a whole 4x8x12 slice. The times are simulated.
768 devices in a mesh: dp: 12 (over z), fsdp: 64 (over x, y, core).
Axes of the slice: x: 4, y: 8, z: 12, core: 2. Of those that a mesh axis runs over, the one named last changes fastest.
Arguments:
- grads: bfloat16 [12, 12, 512, 16, 1024], P('dp', None, 'fsdp'), may hold values from -50 to 50
- slot_block: int32 [12, 64], replicated, may hold values from 0 to 63, each once within a row
Outputs:
- update: bfloat16 [12, 512, 16, 1024], P('dp', 'fsdp')
- slot_roots: bfloat16 [12, 64, 2, 512, 512], P('dp', 'fsdp')
Inputs may be any that keep to these rules, and one draw needn't show every extreme that they name: `slot_block`: row r is a permutation of 0 to 64 - 1 over the slots of the owners (owner o holds slots o * 1 to o + 1 - 1); a value v below 32 places local block v of index r of dp in that slot, a larger value leaves it empty.
All inputs are finite; a program needn't handle non-finite values.
Results may differ from a plain program's by a relative error of at most 0.033.
Values may be sent and summed in bfloat16 or wider, within the bound.
No kernel may reach another device: no remote copies, remote signals or barrier semaphores. Data moves between devices by JAX's collectives and lax.ppermute only.
A program may use at most 32 MiB of HBM per device.

v0:
```python
import jax
import jax.numpy as jnp
from jax import lax
from jax.sharding import PartitionSpec as P

BLK = 512
ITERS = 2


damping = 0.1


def shortened(x):

    def short(part):
        return part.astype(jnp.bfloat16) if part.dtype == jnp.float32 else part

    return jax.tree.map(short, x)


def left_gram(block_data):
    return jnp.dot(
        block_data,
        block_data.T,
        precision=lax.Precision.HIGHEST,
        preferred_element_type=jnp.float32,
    )


def right_gram(block_data):
    return jnp.dot(
        block_data.T,
        block_data,
        precision=lax.Precision.HIGHEST,
        preferred_element_type=jnp.float32,
    )


def stat_root(statistic):
    order = statistic.shape[0]
    identity = jnp.eye(order, dtype=jnp.float32)
    trace_sum = jnp.trace(statistic)
    damped = statistic + (damping * trace_sum / order + 1e-06) * identity
    norm_scale = jnp.sqrt(jnp.sum(damped * damped)) / 4.0
    matrix = damped / norm_scale
    root_iter = identity
    for iteration in range(ITERS):
        factor = (5.0 * identity - matrix) / 4.0
        factor_low = factor.astype(jnp.bfloat16)
        if iteration == 0:
            root_iter = jnp.power(norm_scale, -0.25) * factor
        else:
            root_iter = jnp.dot(
                root_iter.astype(jnp.bfloat16), factor_low, preferred_element_type=jnp.float32
            )
        if iteration + 1 < ITERS:
            square = jnp.dot(factor_low, factor_low, preferred_element_type=jnp.float32).astype(
                jnp.bfloat16
            )
            fourth = jnp.dot(square, square, preferred_element_type=jnp.float32).astype(
                jnp.bfloat16
            )
            matrix = jnp.dot(
                fourth, matrix.astype(jnp.bfloat16), preferred_element_type=jnp.float32
            )
    return root_iter.astype(jnp.bfloat16)


def graft_step(block_data, left_root, right_root):
    partial_product = jnp.dot(
        left_root, block_data.astype(jnp.bfloat16), preferred_element_type=jnp.float32
    ).astype(jnp.bfloat16)
    direction = jnp.dot(partial_product, right_root, preferred_element_type=jnp.float32)
    grad_rms = jnp.sqrt(jnp.mean(block_data * block_data))
    dir_rms = jnp.sqrt(jnp.mean(direction * direction) + 1e-06)
    return (-(grad_rms / dir_rms) * direction).astype(jnp.bfloat16)


def left_work(block_data):
    return stat_root(left_gram(block_data))


def right_work(block_data):
    return stat_root(right_gram(block_data))


def full_work(block_data):
    left_root = left_work(block_data)
    right_root = right_work(block_data)
    return (jnp.stack([left_root, right_root]), graft_step(block_data, left_root, right_root))


def spare_work(block_data):
    return (
        jnp.zeros((2,) + block_data.shape, jnp.bfloat16),
        jnp.zeros(block_data.shape, jnp.bfloat16),
    )


def owner_slot(packed):
    block_data, active = packed
    return lax.cond(active, full_work, spare_work, block_data)


def local(grads, slot_block):
    fsdp_size = lax.axis_size("fsdp")
    replica_count = lax.axis_size("dp")
    dp_index = lax.axis_index("dp")
    owner = lax.axis_index("fsdp")
    replica_grads = grads[0]
    summed = lax.psum_scatter(
        replica_grads.astype(jnp.float32).astype(jnp.bfloat16),
        "dp",
        scatter_dimension=0,
        tiled=True,
    ).astype(jnp.float32)
    averaged = summed / replica_count
    matrices, row_count, row_blocks, col_count = averaged.shape
    col_blocks = col_count // BLK
    pieces = averaged.reshape(matrices, row_count, row_blocks, col_blocks, BLK)
    pieces = pieces.transpose(0, 2, 3, 1, 4).reshape(
        matrices * row_blocks * col_blocks, row_count, BLK
    )
    group_size = pieces.shape[0]
    table_row = lax.dynamic_slice_in_dim(slot_block, dp_index, 1, 0)[0]
    slot_count = table_row.shape[0]
    capacity = slot_count // fsdp_size
    occupied = table_row < group_size
    chosen = jnp.minimum(table_row, group_size - 1)
    outgoing = jnp.take(pieces, chosen, axis=0) * occupied[:, None, None].astype(jnp.float32)
    outgoing = outgoing.reshape(fsdp_size, capacity, row_count, BLK)
    received = lax.all_to_all(
        outgoing.astype(jnp.bfloat16), "fsdp", split_axis=0, concat_axis=0, tiled=True
    ).astype(outgoing.dtype)
    blocks = received.transpose(1, 0, 2, 3).reshape(capacity, fsdp_size * row_count, BLK)
    my_active = lax.dynamic_slice_in_dim(occupied, owner * capacity, capacity, 0)
    root_pairs, updates = lax.map(owner_slot, (blocks, my_active))
    going_back = updates.reshape(capacity, fsdp_size, row_count, BLK).transpose(1, 0, 2, 3)
    coming_back = lax.all_to_all(
        shortened(going_back), "fsdp", split_axis=0, concat_axis=0, tiled=True
    ).astype(going_back.dtype)
    coming_back = coming_back.reshape(slot_count, row_count, BLK)
    placement = (
        jnp.zeros((slot_count,), jnp.int32)
        .at[table_row]
        .set(jnp.arange(slot_count, dtype=jnp.int32))
    )
    mine = jnp.take(coming_back, placement[:group_size], axis=0)
    update = mine.reshape(matrices, row_blocks, col_blocks, row_count, BLK)
    update = update.transpose(0, 3, 1, 2, 4).reshape(matrices, row_count, row_blocks, col_count)
    return (update, root_pairs.reshape(1, capacity, 2, BLK, BLK))


def solution(mesh):
    return jax.shard_map(
        local,
        mesh=mesh,
        in_specs=(P("dp", None, "fsdp", None, None), P()),
        out_specs=(P("dp", "fsdp", None, None), P("dp", "fsdp", None, None, None)),
        check_vma=False,
    )
```

profile of v0, /device:TPU:1, one launch (start us, length us, event | category | flops | bytes accessed | tf_op | source)
XLA Modules:
  0.0 168.7 jit_solution(7291626492271544533)
XLA Ops:
  7.2 0.7 reduce-scatter.2.cloned.1.call-update
  7.9 0.7 fusion.66
  8.6 67.8 %reduce-scatter.2.cloned.1.call-done = bf16[1,8,16,1024]{3,2,1,0:T(8,128)(2,1)} async-done(((bf16[12,8,16,1024]{3,2,1,0:T(8,128)(2,1)}), bf16[1,8,16,1024]{3,2,1,0:T(8,128)(2,1)}) %reduce-scatter.2.cloned.1.call-update) | async-done | bytes 262160 | tf_op jit(solution)/shard_map/reduce_scatter | solution.py:111
  76.4 1.0 convert_multiply_fusion
  78.8 1.0 fusion.65
  79.8 17.4 %all-to-all-start = ((bf16[64,1,8,512]{3,2,1,0:T(8,128)(2,1)}), bf16[64,1,8,512]{3,2,1,0:T(8,128)(2,1)S(1)}, u32[]{:S(2)}, u32[]{:S(2)}) async-start(bf16[64,1,8,512]{3,2,1,0:T(8,128)(2,1)} %fusion.65), calls=%async_computation.1 | async-start | bytes 1048576 | tf_op jit(solution)/shard_map/all_to_all | solution.py:132
  97.9 16.7 %all-to-all-done = bf16[64,1,8,512]{3,2,1,0:T(8,128)(2,1)S(1)} async-done(((bf16[64,1,8,512]{3,2,1,0:T(8,128)(2,1)}), bf16[64,1,8,512]{3,2,1,0:T(8,128)(2,1)S(1)}, u32[]{:S(2)}, u32[]{:S(2)}) %all-to-all-start) | async-done | bytes 524320 | tf_op jit(solution)/shard_map/all_to_all | solution.py:132
  114.7 21.8 %conditional.1 = (bf16[512,512]{1,0:T(8,128)(2,1)}, bf16[1,1,2,512,512]{4,3,2,1,0:T(8,128)(2,1)}) conditional(s32[]{:T(128)} %bitcast.10, () %tuple.21, f32[64,1,8,512]{3,2,1,0:T(8,128)S(1)} %convert_element_type.98), branch_computations={%region_2.3_spmd, %region_3.10_spmd} | conditional | flops 5927075840 | bytes 21496108 | solution.py:102
  115.4 2.5 %select_reduce_fusion = (f32[]{:T(128)}, f32[512,512]{1,0:T(8,128)S(1)}) fusion(f32[64,1,8,512]{3,2,1,0:T(8,128)S(1)} %param.1), kind=kOutput, calls=%fused_computation.33 | convolution fusion | flops 1611399168 | bytes 2097156 | tf_op jit(solution)/shard_map/while/body/eval_jaxpr/cond/branch_1_fun/dot_general | solution.py:31
  118.6 0.9 multiply_reduce_fusion.1
  120.1 1.1 convolution_convert_fusion.1
  121.4 0.8 convolution_convert_fusion
  122.2 2.5 %select_reduce_fusion.1 = (f32[]{:T(128)}, f32[512,512]{1,0:T(8,128)S(1)}) fusion(f32[64,1,8,512]{3,2,1,0:T(8,128)S(1)} %param.1), kind=kOutput, calls=%fused_computation.38 | convolution fusion | flops 1611399168 | bytes 2097156 | tf_op jit(solution)/shard_map/while/body/eval_jaxpr/cond/branch_1_fun/dot_general | solution.py:22
  125.3 0.9 multiply_reduce_fusion.2
  126.9 1.9 %convolution_convert_fusion.5 = bf16[512,512]{1,0:T(8,128)(2,1)} fusion(f32[512,512]{1,0:T(8,128)S(1)} %get-tuple-element.29, f32[]{:T(128)S(6)} %div.36, f32[]{:T(128)S(6)} %add.56), kind=kOutput, calls=%fused_computation.15 | convolution fusion | flops 539492352 | bytes 1572872 | tf_op jit(solution)/shard_map/while/body/eval_jaxpr/cond/branch_1_fun/dot_general | solution.py:60
  128.9 1.9 %convolution_convert_fusion.4 = bf16[512,512]{1,0:T(8,128)(2,1)S(1)} fusion(bf16[512,512]{1,0:T(8,128)(2,1)} %convolution_convert_fusion.5, f32[]{:T(128)S(6)} %mul.59, f32[512,512]{1,0:T(8,128)S(1)} %get-tuple-element.29, f32[]{:T(128)S(6)} %div.36, f32[]{:T(128)S(6)} %add.56), kind=kOutput, calls=%fused_computation.14 | convolution fusion | flops 541851648 | bytes 2097164 | tf_op jit(solution)/shard_map/while/body/eval_jaxpr/cond/branch_1_fun/dot_general | solution.py:53
  130.7 1.4 multiply_reduce_fusion
  132.2 0.9 fusion.8
  134.5 0.9 multiply_convert_fusion
  135.5 1.1 maximum_bitcast_fusion
  136.5 6.3 %all-to-all-start.1 = ((bf16[64,1,8,512]{3,2,1,0:T(8,128)(2,1)}), bf16[64,1,8,512]{3,2,1,0:T(8,128)(2,1)S(1)}, u32[]{:S(2)}, u32[]{:S(2)}) async-start(bf16[64,1,8,512]{3,2,1,0:T(8,128)(2,1)} %bitcast.19), calls=%async_computation.2 | async-start | bytes 1048576 | tf_op jit(solution)/shard_map/all_to_all | solution.py:139
  142.8 0.8 scatter_custom_fusion
  143.7 16.4 %all-to-all-done.1 = bf16[64,1,8,512]{3,2,1,0:T(8,128)(2,1)S(1)} async-done(((bf16[64,1,8,512]{3,2,1,0:T(8,128)(2,1)}), bf16[64,1,8,512]{3,2,1,0:T(8,128)(2,1)S(1)}, u32[]{:S(2)}, u32[]{:S(2)}) %all-to-all-start.1) | async-done | bytes 524320 | tf_op jit(solution)/shard_map/all_to_all | solution.py:139
  161.0 0.9 reshape.143
  (18 shorter events, 3.1 us)
Async XLA Ops:
  7.2 69.2 %reduce-scatter.2.cloned.1.call-start = ((), (), s32[]{:S(2)}) async-start(), calls=%async_computation.3 | async-start | bytes 3407872 | tf_op jit(solution)/shard_map/reduce_scatter | solution.py:111
  79.8 34.8 %all-to-all-start = ((bf16[64,1,8,512]{3,2,1,0:T(8,128)(2,1)}), bf16[64,1,8,512]{3,2,1,0:T(8,128)(2,1)S(1)}, u32[]{:S(2)}, u32[]{:S(2)}) async-start(bf16[64,1,8,512]{3,2,1,0:T(8,128)(2,1)} %fusion.65), calls=%async_computation.1 | async-start | bytes 1048576 | tf_op jit(solution)/shard_map/all_to_all | solution.py:132
  136.5 23.6 %all-to-all-start.1 = ((bf16[64,1,8,512]{3,2,1,0:T(8,128)(2,1)}), bf16[64,1,8,512]{3,2,1,0:T(8,128)(2,1)S(1)}, u32[]{:S(2)}, u32[]{:S(2)}) async-start(bf16[64,1,8,512]{3,2,1,0:T(8,128)(2,1)} %bitcast.19), calls=%async_computation.2 | async-start | bytes 1048576 | tf_op jit(solution)/shard_map/all_to_all | solution.py:139
Sparse Core Ops, SparseCore 0:
  11.1 65.2 reduce-scatter.1
where the time goes:
time: 169 us
  waiting for transfers between devices  102 us (60%)
  starting transfers between devices  23.8 us (14%)
  between operations  14.2 us (8%)
  matrix products  12.2 us (7%)
  other arithmetic  8.22 us (5%)
  loops' own time  4.93 us (3%)
  local copies, waits for them, and re-layouts  3.88 us (2%)
    reduce_scatter x1, waiting for transfers between devices, local(): lax.psum_scatter(replica_grads.astype(jnp.float32).astype(jnp.bfloat16),...  67.8 us
    all_to_all x1, starting transfers between devices, local(): lax.all_to_all(outgoing.astype(jnp.bfloat16), 'fsdp', split_axis=0, conca...  17.4 us
    all_to_all x1, waiting for transfers between devices, local(): lax.all_to_all(outgoing.astype(jnp.bfloat16), 'fsdp', split_axis=0, conca...  16.7 us
    all_to_all x1, waiting for transfers between devices, local(): lax.all_to_all(shortened(going_back), 'fsdp', split_axis=0, concat_axis=0...  16.4 us
    all_to_all x1, starting transfers between devices, local(): lax.all_to_all(shortened(going_back), 'fsdp', split_axis=0, concat_axis=0...  6.27 us
    another operation x1, loops' own time, owner_slot(): return lax.cond(active, full_work, spare_work, block_data)  4.93 us
  transfers between devices with their start and end apart: 3, of which 3 were waited for; matrix products, arithmetic and copies ran while one was open for 1% of the time, Pallas kernels for 0%

commit v1 on v0

v1 whole, which is shorter than its diff:
```python
import jax
import jax.numpy as jnp
from jax import lax
from jax.experimental import pallas as pl
from jax.experimental.pallas import tpu as pltpu
from jax.sharding import PartitionSpec as P

BLK = 512
LANES = 128
PER_BLK = BLK // LANES
ITERS = 2
DAMPING = 0.1
F32 = jnp.float32
BF16 = jnp.bfloat16
VMEM_LIMIT = 48 * 1024 * 1024


def cost(flops, nbytes):
    return pl.CostEstimate(flops=flops, bytes_accessed=nbytes, transcendentals=0)


def vmem():
    return pl.BlockSpec(memory_space=pltpu.VMEM)


def smem():
    return pl.BlockSpec(memory_space=pltpu.SMEM)


def params():
    return pltpu.CompilerParams(vmem_limit_bytes=VMEM_LIMIT)


def outgoing_pieces(table, summed):
    rows, row_blocks, cols = summed.shape
    col_blocks = cols // BLK
    group = row_blocks * col_blocks
    slots = table.shape[0]

    def kernel(table_ref, x_ref, out_ref, wide, pieces):
        for k in range(cols // LANES):
            lanes = x_ref[:, :, k * LANES : (k + 1) * LANES].astype(F32)
            wide[k] = lanes.reshape(rows * row_blocks, LANES)
        for rb in range(row_blocks):
            for k in range(cols // LANES):
                v, at = rb * col_blocks + k // PER_BLK, k % PER_BLK * LANES
                part = wide[k, pl.ds(rb, rows, stride=row_blocks), :]
                pieces[v, :, at : at + LANES] = part.astype(BF16)
        pieces[group:] = jnp.zeros((slots - group, rows, BLK), BF16)

        def place(s, carry):
            out_ref[s] = pieces[table_ref[s]]
            return carry

        lax.fori_loop(0, slots, place, 0, unroll=8)

    return pl.pallas_call(
        kernel,
        out_shape=jax.ShapeDtypeStruct((slots, rows, BLK), BF16),
        in_specs=[smem(), vmem()],
        out_specs=vmem(),
        scratch_shapes=[
            pltpu.VMEM((cols // LANES, rows * row_blocks, LANES), F32),
            pltpu.VMEM((slots, rows, BLK), BF16),
        ],
        compiler_params=params(),
        cost_estimate=cost(0, 3 * slots * rows * BLK * 2),
        name="outgoing",
    )(table, summed)


def incoming_update(table, returned, row_blocks, col_blocks):
    slots, rows, _ = returned.shape
    cols = col_blocks * BLK

    def kernel(table_ref, x_ref, out_ref, wide, pieces):
        def place(s, carry):
            pieces[table_ref[s]] = x_ref[s]
            return carry

        lax.fori_loop(0, slots, place, 0, unroll=8)
        for rb in range(row_blocks):
            for k in range(cols // LANES):
                v, at = rb * col_blocks + k // PER_BLK, k % PER_BLK * LANES
                part = pieces[v, :, at : at + LANES].astype(F32)
                wide[k, pl.ds(rb, rows, stride=row_blocks), :] = part
        for k in range(cols // LANES):
            lanes = wide[k].reshape(rows, row_blocks, LANES)
            out_ref[:, :, k * LANES : (k + 1) * LANES] = lanes.astype(BF16)

    return pl.pallas_call(
        kernel,
        out_shape=jax.ShapeDtypeStruct((rows, row_blocks, cols), BF16),
        in_specs=[smem(), vmem()],
        out_specs=vmem(),
        scratch_shapes=[
            pltpu.VMEM((cols // LANES, rows * row_blocks, LANES), F32),
            pltpu.VMEM((slots, rows, BLK), BF16),
        ],
        compiler_params=params(),
        cost_estimate=cost(0, 3 * slots * rows * BLK * 2),
        name="incoming",
    )(table, returned)


def dot(a, b, contract=((1,), (0,))):
    return lax.dot_general(a, b, (contract, ((), ())), preferred_element_type=F32)


def newton_root(stat, total, eye):
    damped = stat + (DAMPING * total / BLK + 1e-06) * eye
    scale = jnp.sqrt(jnp.sum(damped * damped)) / 4.0
    matrix = damped * (1.0 / scale)
    root = None
    for iteration in range(ITERS):
        factor = 1.25 * eye - 0.25 * matrix
        factor_low = factor.astype(BF16)
        if iteration == 0:
            root = (lax.rsqrt(jnp.sqrt(scale)) * factor).astype(BF16)
        else:
            root = dot(root, factor_low).astype(BF16)
        if iteration + 1 < ITERS:
            square = dot(factor_low, factor_low).astype(BF16)
            fourth = dot(square, square).astype(BF16)
            matrix = dot(fourth, matrix.astype(BF16))
    return root


def owner_work(active, block, replicas):
    def kernel(active_ref, x_ref, roots_ref, update_ref):
        @pl.when(active_ref[0] == 0)
        def _():
            roots_ref[...] = jnp.zeros_like(roots_ref)
            update_ref[...] = jnp.zeros_like(update_ref)

        @pl.when(active_ref[0] != 0)
        def _():
            eye = (
                lax.broadcasted_iota(jnp.int32, (BLK, BLK), 0)
                == lax.broadcasted_iota(jnp.int32, (BLK, BLK), 1)
            ).astype(F32)
            x = x_ref[...]
            wide = x.astype(F32)
            scale = 1.0 / (replicas * replicas)
            total = jnp.sum(wide * wide) * scale
            left = newton_root(dot(x, x, ((1,), (1,))) * scale, total, eye)
            roots_ref[0] = left
            right = newton_root(dot(x, x, ((0,), (0,))) * scale, total, eye)
            roots_ref[1] = right
            partial = (dot(left, x) * (1.0 / replicas)).astype(BF16)
            direction = dot(partial, right)
            count = BLK * BLK
            grad_rms = jnp.sqrt(total / count)
            dir_rms = jnp.sqrt(jnp.sum(direction * direction) / count + 1e-06)
            update_ref[...] = (-(grad_rms / dir_rms) * direction).astype(BF16)

    return pl.pallas_call(
        kernel,
        out_shape=(
            jax.ShapeDtypeStruct((2, BLK, BLK), BF16),
            jax.ShapeDtypeStruct((BLK, BLK), BF16),
        ),
        in_specs=[smem(), vmem()],
        out_specs=(vmem(), vmem()),
        compiler_params=params(),
        cost_estimate=cost(24 * BLK**3, 8 * BLK * BLK),
        name="owner",
    )(active, block)


def local(grads, slot_block):
    replicas = lax.axis_size("dp")
    table = lax.dynamic_index_in_dim(slot_block, lax.axis_index("dp"), 0, keepdims=False)
    slots = table.shape[0]
    summed = lax.psum_scatter(grads[0], "dp", scatter_dimension=0, tiled=True)[0]
    rows, row_blocks, cols = summed.shape
    col_blocks = cols // BLK
    group = row_blocks * col_blocks
    active = lax.dynamic_slice_in_dim(table, lax.axis_index("fsdp"), 1, 0) < group
    pieces = outgoing_pieces(table, summed)
    received = lax.all_to_all(pieces, "fsdp", split_axis=0, concat_axis=0, tiled=True)
    roots, update = owner_work(active.astype(jnp.int32), received.reshape(BLK, BLK), replicas)
    returned = lax.all_to_all(
        update.reshape(slots, rows, BLK), "fsdp", split_axis=0, concat_axis=0, tiled=True
    )
    result = incoming_update(table, returned, row_blocks, col_blocks)
    return result[None], roots[None, None]


def solution(mesh):
    return jax.shard_map(
        local,
        mesh=mesh,
        in_specs=(P("dp", None, "fsdp", None, None), P()),
        out_specs=(P("dp", "fsdp", None, None), P("dp", "fsdp", None, None, None)),
        check_vma=False,
    )
```

time: 169 us -> 152 us (0.90)
  blocking collectives: 0 us -> 28.8 us
  waiting for transfers between devices: 102 us -> 83.9 us
  matrix products: 12.2 us -> 0 us
  other arithmetic: 8.22 us -> 0 us
  starting transfers between devices: 23.8 us -> 17.5 us
  loops' own time: 4.93 us -> 0 us
  Pallas kernels: 0 us -> 4.37 us
    all_to_all x0 -> x1, blocking collectives: none -> 28.8 us  [local(): lax.all_to_all(update.reshape(slots, rows, BLK), 'fsdp', split_axis=0, co...]
    all_to_all x2 -> x1, waiting for transfers between devices: 33.1 us -> 15.4 us  [local(): lax.all_to_all(pieces, 'fsdp', split_axis=0, concat_axis=0, tiled=True)]
    dot_general x7 -> x0, matrix products: 12.2 us -> none  [the longest x2 3.09 us: stat_root(): jnp.dot(square, square, preferred_element_type=jnp.float32)]
    all_to_all x2 -> x1, starting transfers between devices: 23.7 us -> 17.4 us  [local(): lax.all_to_all(pieces, 'fsdp', split_axis=0, concat_axis=0, tiled=True)]
    another operation x1 -> x0, loops' own time: 4.93 us -> none  [owner_slot(): return lax.cond(active, full_work, spare_work, block_data)]
    pallas_call x0 -> x3, Pallas kernels: none -> 4.37 us  [the longest x1 1.65 us: outgoing_pieces(): pl.pallas_call(kernel, out_shape=jax.ShapeDtypeStruct((slots, rows, BLK),...]
    reduce_sum x3 -> x0, other arithmetic: 2.69 us -> none  [the longest x2 1.74 us: stat_root(): norm_scale = jnp.sqrt(jnp.sum(damped * damped)) / 4.0]
    convert_element_type x5 -> x0, other arithmetic: 2.62 us -> none  [the longest x1 1 us: local(): outgoing.astype(jnp.bfloat16)]
  transfers between devices with their start and end apart: 3 -> 2, of which waited for: 3 -> 2; matrix products, arithmetic and copies ran while one was open for 1% -> 1% of each run, Pallas kernels for 0% -> 0%
where the time goes in v1:
time: 152 us
  waiting for transfers between devices  83.9 us (55%)
  blocking collectives  28.8 us (19%)
  starting transfers between devices  17.5 us (12%)
  between operations  14.7 us (10%)
  Pallas kernels  4.37 us (3%)
  local copies, waits for them, and re-layouts  2.92 us (2%)
    reduce_scatter x1, waiting for transfers between devices, local(): lax.psum_scatter(grads[0], 'dp', scatter_dimension=0, tiled=True)[0]  67.8 us
    all_to_all x1, blocking collectives, local(): lax.all_to_all(update.reshape(slots, rows, BLK), 'fsdp', split_axis=0, co...  28.8 us
    all_to_all x1, starting transfers between devices, local(): lax.all_to_all(pieces, 'fsdp', split_axis=0, concat_axis=0, tiled=True)  17.4 us
    all_to_all x1, waiting for transfers between devices, local(): lax.all_to_all(pieces, 'fsdp', split_axis=0, concat_axis=0, tiled=True)  15.4 us
  transfers between devices with their start and end apart: 2, of which 2 were waited for; matrix products, arithmetic and copies ran while one was open for 1% of the time, Pallas kernels for 0%

profile of v1, /device:TPU:1, one launch (start us, length us, event | category | flops | bytes accessed | tf_op | source)
XLA Modules:
  0.0 152.2 jit_solution(13417999384303752741)
XLA Ops:
  7.2 0.0 reduce-scatter.2.cloned.1.call-start
  7.2 0.7 reduce-scatter.2.cloned.1.call-update
  7.9 0.7 dynamic-slice_bitcast_fusion.table_ref
  8.6 67.8 %reduce-scatter.2.cloned.1.call-done = bf16[1,8,16,1024]{3,2,1,0:T(8,128)(2,1)} async-done(((bf16[12,8,16,1024]{3,2,1,0:T(8,128)(2,1)}), bf16[1,8,16,1024]{3,2,1,0:T(8,128)(2,1)}) %reduce-scatter.2.cloned.1.call-update) | async-done | bytes 262160 | tf_op jit(solution)/shard_map/reduce_scatter | solution.py:175
  76.4 0.0 copy-start
  76.4 0.9 copy-done
  77.4 1.6 %outgoing.1 = bf16[64,8,512]{2,1,0:T(8,128)(2,1)} custom-call(s32[64]{0:T(128)S(1)} %dynamic-slice_bitcast_fusion.table_ref, bf16[8,16,1024]{2,1,0:T(8,128)(2,1)S(1)} %bitcast.11), custom_call_target="tpu_custom_call" | custom-call | bytes 1572864 | tf_op jit(solution)/shard_map/outgoing/pallas_call | solution.py:57
  79.0 17.4 %all-to-all-start = ((bf16[64,8,512]{2,1,0:T(8,128)(2,1)}), bf16[64,8,512]{2,1,0:T(8,128)(2,1)S(1)}, u32[]{:S(2)}, u32[]{:S(2)}) async-start(bf16[64,8,512]{2,1,0:T(8,128)(2,1)} %outgoing.1), calls=%async_computation.1 | async-start | bytes 1048576 | tf_op jit(solution)/shard_map/all_to_all | solution.py:181
  96.5 1.3 dynamic_slice.8
  98.4 15.4 %all-to-all-done = bf16[64,8,512]{2,1,0:T(8,128)(2,1)S(1)} async-done(((bf16[64,8,512]{2,1,0:T(8,128)(2,1)}), bf16[64,8,512]{2,1,0:T(8,128)(2,1)S(1)}, u32[]{:S(2)}, u32[]{:S(2)}) %all-to-all-start) | async-done | bytes 524320 | tf_op jit(solution)/shard_map/all_to_all | solution.py:181
  113.8 1.1 owner.1
  114.9 28.8 %all_to_all.10.x_ref = bf16[64,8,512]{2,1,0:T(8,128)(2,1)S(1)} all-to-all(bf16[64,8,512]{2,1,0:T(8,128)(2,1)S(1)} %bitcast.10), channel_id=1, replica_groups=mesh['dp'=12,'fsdp'=64] {'fsdp'}, dimensions={0} | all-to-all | bytes 1048576 | tf_op jit(solution)/shard_map/all_to_all | solution.py:183
  143.7 1.6 %incoming.1 = bf16[8,16,1024]{2,1,0:T(8,128)(2,1)} custom-call(s32[64]{0:T(128)S(1)} %dynamic-slice_bitcast_fusion.table_ref, bf16[64,8,512]{2,1,0:T(8,128)(2,1)S(1)} %all_to_all.10.x_ref), custom_call_target="tpu_custom_call" | custom-call | bytes 1572864 | tf_op jit(solution)/shard_map/incoming/pallas_call | solution.py:91
Async XLA Ops:
  7.2 69.2 %reduce-scatter.2.cloned.1.call-start = ((), (), s32[]{:S(2)}) async-start(), calls=%async_computation.3 | async-start | bytes 3407872 | tf_op jit(solution)/shard_map/reduce_scatter | solution.py:175
  76.4 0.9 copy-start
  79.0 34.8 %all-to-all-start = ((bf16[64,8,512]{2,1,0:T(8,128)(2,1)}), bf16[64,8,512]{2,1,0:T(8,128)(2,1)S(1)}, u32[]{:S(2)}, u32[]{:S(2)}) async-start(bf16[64,8,512]{2,1,0:T(8,128)(2,1)} %outgoing.1), calls=%async_computation.1 | async-start | bytes 1048576 | tf_op jit(solution)/shard_map/all_to_all | solution.py:181
Sparse Core Ops, SparseCore 0:
  11.1 65.2 reduce-scatter.1

commit v2 on v1

--- a/solution.py
+++ b/solution.py
@@ -31,15 +31,16 @@
     return pltpu.CompilerParams(vmem_limit_bytes=VMEM_LIMIT)
 
 
-def outgoing_pieces(table, summed):
-    rows, row_blocks, cols = summed.shape
+def outgoing_pieces(table, terms):
+    rows, row_blocks, cols = terms[0].shape
     col_blocks = cols // BLK
     group = row_blocks * col_blocks
     slots = table.shape[0]
 
-    def kernel(table_ref, x_ref, out_ref, wide, pieces):
+    def kernel(table_ref, *refs):
+        x_refs, (out_ref, wide, pieces) = refs[: len(terms)], refs[len(terms) :]
         for k in range(cols // LANES):
-            lanes = x_ref[:, :, k * LANES : (k + 1) * LANES].astype(F32)
+            lanes = sum(x[:, :, k * LANES : (k + 1) * LANES].astype(F32) for x in x_refs)
             wide[k] = lanes.reshape(rows * row_blocks, LANES)
         for rb in range(row_blocks):
             for k in range(cols // LANES):
@@ -57,7 +58,7 @@
     return pl.pallas_call(
         kernel,
         out_shape=jax.ShapeDtypeStruct((slots, rows, BLK), BF16),
-        in_specs=[smem(), vmem()],
+        in_specs=[smem()] + [vmem()] * len(terms),
         out_specs=vmem(),
         scratch_shapes=[
             pltpu.VMEM((cols // LANES, rows * row_blocks, LANES), F32),
@@ -66,7 +67,7 @@
         compiler_params=params(),
         cost_estimate=cost(0, 3 * slots * rows * BLK * 2),
         name="outgoing",
-    )(table, summed)
+    )(table, *terms)
 
 
 def incoming_update(table, returned, row_blocks, col_blocks):
@@ -168,16 +169,39 @@
     )(active, block)
 
 
+def ring_terms(parts, axis):
+    n = parts.shape[0]
+    here = lax.axis_index(axis)
+    raising = [(i, (i + 1) % n) for i in range(n)]
+    lowering = [(i, (i - 1) % n) for i in range(n)]
+    hops = n // 2
+
+    def own(offset):
+        return lax.dynamic_index_in_dim(parts, (here + offset + n) % n, 0, keepdims=False)
+
+    def plus(total, offset):
+        if total is None:
+            return own(offset)
+        return (total.astype(F32) + own(offset).astype(F32)).astype(BF16)
+
+    below = above = None
+    for step in range(hops):
+        below = lax.ppermute(plus(below, hops - step), axis, raising)
+        if step >= 2 * hops + 1 - n:
+            above = lax.ppermute(plus(above, step - hops), axis, lowering)
+    return below, above, own(0)
+
+
 def local(grads, slot_block):
     replicas = lax.axis_size("dp")
     table = lax.dynamic_index_in_dim(slot_block, lax.axis_index("dp"), 0, keepdims=False)
     slots = table.shape[0]
-    summed = lax.psum_scatter(grads[0], "dp", scatter_dimension=0, tiled=True)[0]
-    rows, row_blocks, cols = summed.shape
+    terms = ring_terms(grads[0], "dp")
+    rows, row_blocks, cols = terms[0].shape
     col_blocks = cols // BLK
     group = row_blocks * col_blocks
     active = lax.dynamic_slice_in_dim(table, lax.axis_index("fsdp"), 1, 0) < group
-    pieces = outgoing_pieces(table, summed)
+    pieces = outgoing_pieces(table, terms)
     received = lax.all_to_all(pieces, "fsdp", split_axis=0, concat_axis=0, tiled=True)
     roots, update = owner_work(active.astype(jnp.int32), received.reshape(BLK, BLK), replicas)
     returned = lax.all_to_all(

time: 152 us -> 155 us (1.020)
  starting transfers between devices: 17.5 us -> 57.5 us
  waiting for transfers between devices: 83.9 us -> 47.9 us
  between operations: 14.7 us -> 1.67 us
  other arithmetic: 0 us -> 10 us
    reduce_scatter x1 -> x0, waiting for transfers between devices: 67.8 us -> none  [local(): lax.psum_scatter(grads[0], 'dp', scatter_dimension=0, tiled=True)[0]]
    ppermute x0 -> x11, starting transfers between devices: none -> 40 us  [the longest x6 20.2 us: ring_terms(): below = lax.ppermute(plus(below, hops - step), axis, raising)]
    ppermute x0 -> x11, waiting for transfers between devices: none -> 32.6 us  [the longest x6 24.5 us: ring_terms(): below = lax.ppermute(plus(below, hops - step), axis, raising)]
    convert_element_type x0 -> x5, other arithmetic: none -> 10 us  [plus(): return (total.astype(F32) + own(offset).astype(F32)).astype(BF16)]
    squeeze x0 -> x1, local copies, waits for them, and re-layouts: none -> 2.13 us  [own(): lax.dynamic_index_in_dim(parts, (here + offset + n) % n, 0, keepdims=False)]
  transfers between devices with their start and end apart: 2 -> 12, of which waited for: 2 -> 11; matrix products, arithmetic and copies ran while one was open for 1% -> 2% of each run, Pallas kernels for 0% -> 0%
where the time goes in v2:
time: 155 us
  starting transfers between devices  57.5 us (37%)
  waiting for transfers between devices  47.9 us (31%)
  blocking collectives  28.8 us (19%)
  other arithmetic  10 us (6%)
  Pallas kernels  4.47 us (3%)
  local copies, waits for them, and re-layouts  4.1 us (3%)
  between operations  1.67 us (1%)
    all_to_all x1, blocking collectives, local(): lax.all_to_all(update.reshape(slots, rows, BLK), 'fsdp', split_axis=0, co...  28.8 us
    ppermute x6, waiting for transfers between devices, ring_terms(): below = lax.ppermute(plus(below, hops - step), axis, raising)  24.5 us
    ppermute x6, starting transfers between devices, ring_terms(): below = lax.ppermute(plus(below, hops - step), axis, raising)  20.2 us
    ppermute x5, starting transfers between devices, ring_terms(): above = lax.ppermute(plus(above, step - hops), axis, lowering)  19.9 us
    all_to_all x1, starting transfers between devices, local(): lax.all_to_all(pieces, 'fsdp', split_axis=0, concat_axis=0, tiled=True)  17.5 us
    all_to_all x1, waiting for transfers between devices, local(): lax.all_to_all(pieces, 'fsdp', split_axis=0, concat_axis=0, tiled=True)  15.4 us
    convert_element_type x5, other arithmetic, plus(): return (total.astype(F32) + own(offset).astype(F32)).astype(BF16)  10 us
    ppermute x5, waiting for transfers between devices, ring_terms(): above = lax.ppermute(plus(above, step - hops), axis, lowering)  8.03 us
  transfers between devices with their start and end apart: 12, of which 11 were waited for; matrix products, arithmetic and copies ran while one was open for 2% of the time, Pallas kernels for 0%

profile of v2, /device:TPU:1, one launch (start us, length us, event | category | flops | bytes accessed | tf_op | source)
XLA Modules:
  0.0 154.5 jit_solution(4581408485104556649)
XLA Ops:
  0.7 2.1 %dynamic-slice_bitcast_fusion = (bf16[8,16,1024]{2,1,0:T(8,128)(2,1)S(1)}, bf16[8,16,1024]{2,1,0:T(8,128)(2,1)}, bf16[8,16,1024]{2,1,0:T(8,128)(2,1)}) fusion(bf16[1,12,8,16,1024]{4,3,2,1,0:T(8,128)(2,1)} %param.2, s32[]{:T(128)S(6)} %select_n.126, s32[]{:T(128)S(6)} %select_n.116, s32[]{:T(128)S(6)} %select_n.104), kind=kLoop, calls=%fused_computation.18 | loop fusion | bytes 1572876 | tf_op jit(solution)/shard_map/jit(dynamic_index_in_dim)/squeeze | solution.py:180
  2.8 4.8 %collective-permute-start = (bf16[8,16,1024]{2,1,0:T(8,128)(2,1)}, bf16[8,16,1024]{2,1,0:T(8,128)(2,1)}, u32[]{:S(2)}, u32[]{:S(2)}) collective-permute-start(bf16[8,16,1024]{2,1,0:T(8,128)(2,1)} %get-tuple-element.8), channel_id=1, source_target_pairs={{0,64},{64,128},{128,192},{192,256},{256,320},{320,384},{384,448},... | collective-permute-start | bytes 786440 | tf_op jit(solution)/shard_map/ppermute | solution.py:189
  7.7 12.2 %collective-permute-start.6 = (bf16[8,16,1024]{2,1,0:T(8,128)(2,1)}, bf16[8,16,1024]{2,1,0:T(8,128)(2,1)}, u32[]{:S(2)}, u32[]{:S(2)}) collective-permute-start(bf16[8,16,1024]{2,1,0:T(8,128)(2,1)} %get-tuple-element.7), channel_id=1, source_target_pairs={{0,704},{64,0},{128,64},{192,128},{256,192},{320,256},{384,320},{4... | collective-permute-start | bytes 786440 | tf_op jit(solution)/shard_map/ppermute | solution.py:191
  19.9 4.4 %collective-permute-done = bf16[8,16,1024]{2,1,0:T(8,128)(2,1)} collective-permute-done((bf16[8,16,1024]{2,1,0:T(8,128)(2,1)}, bf16[8,16,1024]{2,1,0:T(8,128)(2,1)}, u32[]{:S(2)}, u32[]{:S(2)}) %collective-permute-start) | collective-permute-done | bytes 262176 | tf_op jit(solution)/shard_map/ppermute | solution.py:189
  26.1 1.9 %collective-permute-start.1 = (bf16[8,16,1024]{2,1,0:T(8,128)(2,1)}, bf16[8,16,1024]{2,1,0:T(8,128)(2,1)}, u32[]{:S(2)}, u32[]{:S(2)}) collective-permute-start(bf16[8,16,1024]{2,1,0:T(8,128)(2,1)} %fusion.8), channel_id=1, source_target_pairs={{0,64},{64,128},{128,192},{192,256},{256,320},{320,384},{384,448},... | collective-permute-start | bytes 786440 | tf_op jit(solution)/shard_map/ppermute | solution.py:189
  28.1 8.0 %collective-permute-done.1 = bf16[8,16,1024]{2,1,0:T(8,128)(2,1)} collective-permute-done((bf16[8,16,1024]{2,1,0:T(8,128)(2,1)}, bf16[8,16,1024]{2,1,0:T(8,128)(2,1)}, u32[]{:S(2)}, u32[]{:S(2)}) %collective-permute-start.1) | collective-permute-done | bytes 262176 | tf_op jit(solution)/shard_map/ppermute | solution.py:189
  36.1 2.2 %fusion.3 = (bf16[8,16,1024]{2,1,0:T(8,128)(2,1)}, bf16[8,16,1024]{2,1,0:T(8,128)(2,1)}) fusion(bf16[8,16,1024]{2,1,0:T(8,128)(2,1)} %collective-permute-done.6, bf16[1,12,8,16,1024]{4,3,2,1,0:T(8,128)(2,1)} %param.2, s32[]{:T(128)S(6)} %select_n.118, s32[]{:T(128)S(6)} %select_n.108, bf16[8,16,1024]{2,1,0:T(8,128)(2,1)} %collective-permute-done.1), kind=kLoop, calls=%fused_computation.7 | loop fusion | flops 1048576 | bytes 1572872 | tf_op jit(solution)/shard_map/convert_element_type | solution.py:185
  40.2 3.4 %collective-permute-start.2 = (bf16[8,16,1024]{2,1,0:T(8,128)(2,1)}, bf16[8,16,1024]{2,1,0:T(8,128)(2,1)}, u32[]{:S(2)}, u32[]{:S(2)}) collective-permute-start(bf16[8,16,1024]{2,1,0:T(8,128)(2,1)} %get-tuple-element.16), channel_id=1, source_target_pairs={{0,64},{64,128},{128,192},{192,256},{256,320},{320,384},{384,448},... | collective-permute-start | bytes 786440 | tf_op jit(solution)/shard_map/ppermute | solution.py:189
  43.6 2.5 %collective-permute-done.7 = bf16[8,16,1024]{2,1,0:T(8,128)(2,1)} collective-permute-done((bf16[8,16,1024]{2,1,0:T(8,128)(2,1)}, bf16[8,16,1024]{2,1,0:T(8,128)(2,1)}, u32[]{:S(2)}, u32[]{:S(2)}) %collective-permute-start.7) | collective-permute-done | bytes 262176 | tf_op jit(solution)/shard_map/ppermute | solution.py:191
  46.1 2.7 %collective-permute-done.2 = bf16[8,16,1024]{2,1,0:T(8,128)(2,1)} collective-permute-done((bf16[8,16,1024]{2,1,0:T(8,128)(2,1)}, bf16[8,16,1024]{2,1,0:T(8,128)(2,1)}, u32[]{:S(2)}, u32[]{:S(2)}) %collective-permute-start.2) | collective-permute-done | bytes 262176 | tf_op jit(solution)/shard_map/ppermute | solution.py:189
  48.8 2.0 %fusion.2 = (bf16[8,16,1024]{2,1,0:T(8,128)(2,1)}, bf16[8,16,1024]{2,1,0:T(8,128)(2,1)}) fusion(bf16[8,16,1024]{2,1,0:T(8,128)(2,1)} %collective-permute-done.7, bf16[1,12,8,16,1024]{4,3,2,1,0:T(8,128)(2,1)S(1)} %copy-done, s32[]{:T(128)S(6)} %select_n.120, s32[]{:T(128)S(6)} %select_n.110, bf16[8,16,1024]{2,1,0:T(8,128)(2,1)} %collective-permute-done.2), kind=kLoop, calls=%fused_computation.5 | loop fusion | flops 1048576 | bytes 1572872 | tf_op jit(solution)/shard_map/convert_element_type | solution.py:185
  52.8 3.4 %collective-permute-start.3 = (bf16[8,16,1024]{2,1,0:T(8,128)(2,1)}, bf16[8,16,1024]{2,1,0:T(8,128)(2,1)}, u32[]{:S(2)}, u32[]{:S(2)}) collective-permute-start(bf16[8,16,1024]{2,1,0:T(8,128)(2,1)} %get-tuple-element.14), channel_id=1, source_target_pairs={{0,64},{64,128},{128,192},{192,256},{256,320},{320,384},{384,448},... | collective-permute-start | bytes 786440 | tf_op jit(solution)/shard_map/ppermute | solution.py:189
  56.2 2.1 %collective-permute-done.8 = bf16[8,16,1024]{2,1,0:T(8,128)(2,1)} collective-permute-done((bf16[8,16,1024]{2,1,0:T(8,128)(2,1)}, bf16[8,16,1024]{2,1,0:T(8,128)(2,1)}, u32[]{:S(2)}, u32[]{:S(2)}) %collective-permute-start.8) | collective-permute-done | bytes 262176 | tf_op jit(solution)/shard_map/ppermute | solution.py:191
  58.3 3.1 %collective-permute-done.3 = bf16[8,16,1024]{2,1,0:T(8,128)(2,1)} collective-permute-done((bf16[8,16,1024]{2,1,0:T(8,128)(2,1)}, bf16[8,16,1024]{2,1,0:T(8,128)(2,1)}, u32[]{:S(2)}, u32[]{:S(2)}) %collective-permute-start.3) | collective-permute-done | bytes 262176 | tf_op jit(solution)/shard_map/ppermute | solution.py:189
  61.4 2.0 %fusion.1 = (bf16[8,16,1024]{2,1,0:T(8,128)(2,1)}, bf16[8,16,1024]{2,1,0:T(8,128)(2,1)}) fusion(bf16[8,16,1024]{2,1,0:T(8,128)(2,1)} %collective-permute-done.8, bf16[1,12,8,16,1024]{4,3,2,1,0:T(8,128)(2,1)S(1)} %copy-done, s32[]{:T(128)S(6)} %select_n.122, s32[]{:T(128)S(6)} %select_n.112, bf16[8,16,1024]{2,1,0:T(8,128)(2,1)} %collective-permute-done.3), kind=kLoop, calls=%fused_computation.3 | loop fusion | flops 1048576 | bytes 1572872 | tf_op jit(solution)/shard_map/convert_element_type | solution.py:185
  65.3 3.4 %collective-permute-start.4 = (bf16[8,16,1024]{2,1,0:T(8,128)(2,1)}, bf16[8,16,1024]{2,1,0:T(8,128)(2,1)}, u32[]{:S(2)}, u32[]{:S(2)}) collective-permute-start(bf16[8,16,1024]{2,1,0:T(8,128)(2,1)} %get-tuple-element.12), channel_id=1, source_target_pairs={{0,64},{64,128},{128,192},{192,256},{256,320},{320,384},{384,448},... | collective-permute-start | bytes 786440 | tf_op jit(solution)/shard_map/ppermute | solution.py:189
  68.7 2.1 %collective-permute-done.9 = bf16[8,16,1024]{2,1,0:T(8,128)(2,1)} collective-permute-done((bf16[8,16,1024]{2,1,0:T(8,128)(2,1)}, bf16[8,16,1024]{2,1,0:T(8,128)(2,1)}, u32[]{:S(2)}, u32[]{:S(2)}) %collective-permute-start.9) | collective-permute-done | bytes 262176 | tf_op jit(solution)/shard_map/ppermute | solution.py:191
  70.8 3.1 %collective-permute-done.4 = bf16[8,16,1024]{2,1,0:T(8,128)(2,1)} collective-permute-done((bf16[8,16,1024]{2,1,0:T(8,128)(2,1)}, bf16[8,16,1024]{2,1,0:T(8,128)(2,1)}, u32[]{:S(2)}, u32[]{:S(2)}) %collective-permute-start.4) | collective-permute-done | bytes 262176 | tf_op jit(solution)/shard_map/ppermute | solution.py:189
  74.0 2.0 %fusion = (bf16[8,16,1024]{2,1,0:T(8,128)(2,1)}, bf16[8,16,1024]{2,1,0:T(8,128)(2,1)}) fusion(bf16[8,16,1024]{2,1,0:T(8,128)(2,1)} %collective-permute-done.9, bf16[1,12,8,16,1024]{4,3,2,1,0:T(8,128)(2,1)S(1)} %copy-done, s32[]{:T(128)S(6)} %select_n.124, s32[]{:T(128)S(6)} %select_n.114, bf16[8,16,1024]{2,1,0:T(8,128)(2,1)} %collective-permute-done.4), kind=kLoop, calls=%fused_computation.1 | loop fusion | flops 1048576 | bytes 1572872 | tf_op jit(solution)/shard_map/convert_element_type | solution.py:185
  77.9 3.4 %collective-permute-start.5 = (bf16[8,16,1024]{2,1,0:T(8,128)(2,1)}, bf16[8,16,1024]{2,1,0:T(8,128)(2,1)S(1)}, u32[]{:S(2)}, u32[]{:S(2)}) collective-permute-start(bf16[8,16,1024]{2,1,0:T(8,128)(2,1)} %get-tuple-element.10), channel_id=1, source_target_pairs={{0,64},{64,128},{128,192},{192,256},{256,320},{320,384},{384,448},... | collective-permute-start | bytes 786440 | tf_op jit(solution)/shard_map/ppermute | solution.py:189
  83.3 3.1 %collective-permute-done.5.refs_0_ = bf16[8,16,1024]{2,1,0:T(8,128)(2,1)S(1)} collective-permute-done((bf16[8,16,1024]{2,1,0:T(8,128)(2,1)}, bf16[8,16,1024]{2,1,0:T(8,128)(2,1)S(1)}, u32[]{:S(2)}, u32[]{:S(2)}) %collective-permute-start.5) | collective-permute-done | bytes 262176 | tf_op jit(solution)/shard_map/ppermute | solution.py:189
  88.2 17.5 %all-to-all-start = ((bf16[64,8,512]{2,1,0:T(8,128)(2,1)}), bf16[64,8,512]{2,1,0:T(8,128)(2,1)S(1)}, u32[]{:S(2)}, u32[]{:S(2)}) async-start(bf16[64,8,512]{2,1,0:T(8,128)(2,1)} %outgoing.1), calls=%async_computation | async-start | bytes 1048576 | tf_op jit(solution)/shard_map/all_to_all | solution.py:205
  107.6 15.4 %all-to-all-done = bf16[64,8,512]{2,1,0:T(8,128)(2,1)S(1)} async-done(((bf16[64,8,512]{2,1,0:T(8,128)(2,1)}), bf16[64,8,512]{2,1,0:T(8,128)(2,1)S(1)}, u32[]{:S(2)}, u32[]{:S(2)}) %all-to-all-start) | async-done | bytes 524320 | tf_op jit(solution)/shard_map/all_to_all | solution.py:205
  124.1 28.8 %all_to_all.10.x_ref = bf16[64,8,512]{2,1,0:T(8,128)(2,1)S(1)} all-to-all(bf16[64,8,512]{2,1,0:T(8,128)(2,1)S(1)} %bitcast.41), channel_id=1, replica_groups=mesh['dp'=12,'fsdp'=64] {'fsdp'}, dimensions={0} | all-to-all | bytes 1048576 | tf_op jit(solution)/shard_map/all_to_all | solution.py:207
  (14 shorter events, 17.2 us)
Async XLA Ops:
  0.6 48.2 %copy-start = (bf16[1,12,8,16,1024]{4,3,2,1,0:T(8,128)(2,1)S(1)}, bf16[1,12,8,16,1024]{4,3,2,1,0:T(8,128)(2,1)}, u32[]{:S(2)}) copy-start(bf16[1,12,8,16,1024]{4,3,2,1,0:T(8,128)(2,1)} %param.2) | copy-start | bytes 9437188
  2.8 21.5 %collective-permute-start = (bf16[8,16,1024]{2,1,0:T(8,128)(2,1)}, bf16[8,16,1024]{2,1,0:T(8,128)(2,1)}, u32[]{:S(2)}, u32[]{:S(2)}) collective-permute-start(bf16[8,16,1024]{2,1,0:T(8,128)(2,1)} %get-tuple-element.8), channel_id=1, source_target_pairs={{0,64},{64,128},{128,192},{192,256},{256,320},{320,384},{384,448},... | collective-permute-start | bytes 786440 | tf_op jit(solution)/shard_map/ppermute | solution.py:189
  7.7 20.4 %collective-permute-start.6 = (bf16[8,16,1024]{2,1,0:T(8,128)(2,1)}, bf16[8,16,1024]{2,1,0:T(8,128)(2,1)}, u32[]{:S(2)}, u32[]{:S(2)}) collective-permute-start(bf16[8,16,1024]{2,1,0:T(8,128)(2,1)} %get-tuple-element.7), channel_id=1, source_target_pairs={{0,704},{64,0},{128,64},{192,128},{256,192},{320,256},{384,320},{4... | collective-permute-start | bytes 786440 | tf_op jit(solution)/shard_map/ppermute | solution.py:191
  26.1 10.0 %collective-permute-start.1 = (bf16[8,16,1024]{2,1,0:T(8,128)(2,1)}, bf16[8,16,1024]{2,1,0:T(8,128)(2,1)}, u32[]{:S(2)}, u32[]{:S(2)}) collective-permute-start(bf16[8,16,1024]{2,1,0:T(8,128)(2,1)} %fusion.8), channel_id=1, source_target_pairs={{0,64},{64,128},{128,192},{192,256},{256,320},{320,384},{384,448},... | collective-permute-start | bytes 786440 | tf_op jit(solution)/shard_map/ppermute | solution.py:189
  38.3 7.8 %collective-permute-start.7 = (bf16[8,16,1024]{2,1,0:T(8,128)(2,1)}, bf16[8,16,1024]{2,1,0:T(8,128)(2,1)}, u32[]{:S(2)}, u32[]{:S(2)}) collective-permute-start(bf16[8,16,1024]{2,1,0:T(8,128)(2,1)} %get-tuple-element.15), channel_id=1, source_target_pairs={{0,704},{64,0},{128,64},{192,128},{256,192},{320,256},{384,320},{4... | collective-permute-start | bytes 786440 | tf_op jit(solution)/shard_map/ppermute | solution.py:191
  40.2 8.6 %collective-permute-start.2 = (bf16[8,16,1024]{2,1,0:T(8,128)(2,1)}, bf16[8,16,1024]{2,1,0:T(8,128)(2,1)}, u32[]{:S(2)}, u32[]{:S(2)}) collective-permute-start(bf16[8,16,1024]{2,1,0:T(8,128)(2,1)} %get-tuple-element.16), channel_id=1, source_target_pairs={{0,64},{64,128},{128,192},{192,256},{256,320},{320,384},{384,448},... | collective-permute-start | bytes 786440 | tf_op jit(solution)/shard_map/ppermute | solution.py:189
  50.8 7.4 %collective-permute-start.8 = (bf16[8,16,1024]{2,1,0:T(8,128)(2,1)}, bf16[8,16,1024]{2,1,0:T(8,128)(2,1)}, u32[]{:S(2)}, u32[]{:S(2)}) collective-permute-start(bf16[8,16,1024]{2,1,0:T(8,128)(2,1)} %get-tuple-element.13), channel_id=1, source_target_pairs={{0,704},{64,0},{128,64},{192,128},{256,192},{320,256},{384,320},{4... | collective-permute-start | bytes 786440 | tf_op jit(solution)/shard_map/ppermute | solution.py:191
  52.8 8.6 %collective-permute-start.3 = (bf16[8,16,1024]{2,1,0:T(8,128)(2,1)}, bf16[8,16,1024]{2,1,0:T(8,128)(2,1)}, u32[]{:S(2)}, u32[]{:S(2)}) collective-permute-start(bf16[8,16,1024]{2,1,0:T(8,128)(2,1)} %get-tuple-element.14), channel_id=1, source_target_pairs={{0,64},{64,128},{128,192},{192,256},{256,320},{320,384},{384,448},... | collective-permute-start | bytes 786440 | tf_op jit(solution)/shard_map/ppermute | solution.py:189
  63.4 7.4 %collective-permute-start.9 = (bf16[8,16,1024]{2,1,0:T(8,128)(2,1)}, bf16[8,16,1024]{2,1,0:T(8,128)(2,1)}, u32[]{:S(2)}, u32[]{:S(2)}) collective-permute-start(bf16[8,16,1024]{2,1,0:T(8,128)(2,1)} %get-tuple-element.11), channel_id=1, source_target_pairs={{0,704},{64,0},{128,64},{192,128},{256,192},{320,256},{384,320},{4... | collective-permute-start | bytes 786440 | tf_op jit(solution)/shard_map/ppermute | solution.py:191
  65.3 8.6 %collective-permute-start.4 = (bf16[8,16,1024]{2,1,0:T(8,128)(2,1)}, bf16[8,16,1024]{2,1,0:T(8,128)(2,1)}, u32[]{:S(2)}, u32[]{:S(2)}) collective-permute-start(bf16[8,16,1024]{2,1,0:T(8,128)(2,1)} %get-tuple-element.12), channel_id=1, source_target_pairs={{0,64},{64,128},{128,192},{192,256},{256,320},{320,384},{384,448},... | collective-permute-start | bytes 786440 | tf_op jit(solution)/shard_map/ppermute | solution.py:189
  76.0 7.3 %collective-permute-start.10 = (bf16[8,16,1024]{2,1,0:T(8,128)(2,1)}, bf16[8,16,1024]{2,1,0:T(8,128)(2,1)S(1)}, u32[]{:S(2)}, u32[]{:S(2)}) collective-permute-start(bf16[8,16,1024]{2,1,0:T(8,128)(2,1)} %get-tuple-element.9), channel_id=1, source_target_pairs={{0,704},{64,0},{128,64},{192,128},{256,192},{320,256},{384,320},{4... | collective-permute-start | bytes 786440 | tf_op jit(solution)/shard_map/ppermute | solution.py:191
  77.9 8.5 %collective-permute-start.5 = (bf16[8,16,1024]{2,1,0:T(8,128)(2,1)}, bf16[8,16,1024]{2,1,0:T(8,128)(2,1)S(1)}, u32[]{:S(2)}, u32[]{:S(2)}) collective-permute-start(bf16[8,16,1024]{2,1,0:T(8,128)(2,1)} %get-tuple-element.10), channel_id=1, source_target_pairs={{0,64},{64,128},{128,192},{192,256},{256,320},{320,384},{384,448},... | collective-permute-start | bytes 786440 | tf_op jit(solution)/shard_map/ppermute | solution.py:189
  88.2 34.8 %all-to-all-start = ((bf16[64,8,512]{2,1,0:T(8,128)(2,1)}), bf16[64,8,512]{2,1,0:T(8,128)(2,1)S(1)}, u32[]{:S(2)}, u32[]{:S(2)}) async-start(bf16[64,8,512]{2,1,0:T(8,128)(2,1)} %outgoing.1), calls=%async_computation | async-start | bytes 1048576 | tf_op jit(solution)/shard_map/all_to_all | solution.py:205

commit v3 on v1

--- a/solution.py
+++ b/solution.py
@@ -12,7 +12,7 @@
 DAMPING = 0.1
 F32 = jnp.float32
 BF16 = jnp.bfloat16
-VMEM_LIMIT = 48 * 1024 * 1024
+VMEM_LIMIT = 24 * 1024 * 1024
 
 
 def cost(flops, nbytes):
@@ -31,15 +31,17 @@
     return pltpu.CompilerParams(vmem_limit_bytes=VMEM_LIMIT)
 
 
-def outgoing_pieces(table, summed):
-    rows, row_blocks, cols = summed.shape
+def outgoing_pieces(here, table, terms, parts):
+    rows, row_blocks, cols = terms[0].shape
     col_blocks = cols // BLK
     group = row_blocks * col_blocks
     slots = table.shape[0]
 
-    def kernel(table_ref, x_ref, out_ref, wide, pieces):
+    def kernel(here_ref, table_ref, below_ref, above_ref, parts_ref, out_ref, wide, pieces):
         for k in range(cols // LANES):
-            lanes = x_ref[:, :, k * LANES : (k + 1) * LANES].astype(F32)
+            at = (slice(None), slice(None), slice(k * LANES, (k + 1) * LANES))
+            lanes = below_ref[at].astype(F32) + above_ref[at].astype(F32)
+            lanes = lanes + parts_ref[(here_ref[0], *at)].astype(F32)
             wide[k] = lanes.reshape(rows * row_blocks, LANES)
         for rb in range(row_blocks):
             for k in range(cols // LANES):
@@ -57,7 +59,7 @@
     return pl.pallas_call(
         kernel,
         out_shape=jax.ShapeDtypeStruct((slots, rows, BLK), BF16),
-        in_specs=[smem(), vmem()],
+        in_specs=[smem(), smem(), vmem(), vmem(), vmem()],
         out_specs=vmem(),
         scratch_shapes=[
             pltpu.VMEM((cols // LANES, rows * row_blocks, LANES), F32),
@@ -66,7 +68,7 @@
         compiler_params=params(),
         cost_estimate=cost(0, 3 * slots * rows * BLK * 2),
         name="outgoing",
-    )(table, summed)
+    )(here, table, *terms, parts)
 
 
 def incoming_update(table, returned, row_blocks, col_blocks):
@@ -168,16 +170,71 @@
     )(active, block)
 
 
+def part_at(parts_ref, here_ref, offset):
+    return parts_ref[lax.rem(here_ref[0] + offset, parts_ref.shape[0])]
+
+
+def picked(here, parts, offsets):
+    def kernel(here_ref, parts_ref, *out_refs):
+        for offset, out_ref in zip(offsets, out_refs):
+            out_ref[...] = part_at(parts_ref, here_ref, offset)
+
+    return pl.pallas_call(
+        kernel,
+        out_shape=[jax.ShapeDtypeStruct(parts.shape[1:], BF16)] * len(offsets),
+        in_specs=[smem(), vmem()],
+        out_specs=[vmem()] * len(offsets),
+        compiler_params=params(),
+        cost_estimate=cost(0, 4 * parts[0].size * len(offsets)),
+        name="picked",
+    )(here, parts)
+
+
+def added(here, total, parts, offset):
+    def kernel(here_ref, total_ref, parts_ref, out_ref):
+        own = part_at(parts_ref, here_ref, offset).astype(F32)
+        out_ref[...] = (total_ref[...].astype(F32) + own).astype(BF16)
+
+    return pl.pallas_call(
+        kernel,
+        out_shape=jax.ShapeDtypeStruct(total.shape, BF16),
+        in_specs=[smem(), vmem(), vmem()],
+        out_specs=vmem(),
+        compiler_params=params(),
+        cost_estimate=cost(total.size, 6 * total.size),
+        name="added",
+    )(here, total, parts)
+
+
+def ring_terms(here, parts, axis):
+    n = parts.shape[0]
+    raising = [(i, (i + 1) % n) for i in range(n)]
+    lowering = [(i, (i - 1) % n) for i in range(n)]
+    hops = n // 2
+    first = 2 * hops + 1 - n
+    below, above = picked(here, parts, (hops, (first - hops) % n))
+    for step in range(hops):
+        if step > 0:
+            below = added(here, below, parts, hops - step)
+        below = lax.ppermute(below, axis, raising)
+        if step > first:
+            above = added(here, above, parts, (step - hops) % n)
+        if step >= first:
+            above = lax.ppermute(above, axis, lowering)
+    return below, above
+
+
 def local(grads, slot_block):
     replicas = lax.axis_size("dp")
     table = lax.dynamic_index_in_dim(slot_block, lax.axis_index("dp"), 0, keepdims=False)
     slots = table.shape[0]
-    summed = lax.psum_scatter(grads[0], "dp", scatter_dimension=0, tiled=True)[0]
-    rows, row_blocks, cols = summed.shape
+    here = lax.axis_index("dp")[None]
+    terms = ring_terms(here, grads[0], "dp")
+    rows, row_blocks, cols = terms[0].shape
     col_blocks = cols // BLK
     group = row_blocks * col_blocks
     active = lax.dynamic_slice_in_dim(table, lax.axis_index("fsdp"), 1, 0) < group
-    pieces = outgoing_pieces(table, summed)
+    pieces = outgoing_pieces(here, table, terms, grads[0])
     received = lax.all_to_all(pieces, "fsdp", split_axis=0, concat_axis=0, tiled=True)
     roots, update = owner_work(active.astype(jnp.int32), received.reshape(BLK, BLK), replicas)
     returned = lax.all_to_all(

time: 152 us -> 137 us (0.901)
  waiting for transfers between devices: 83.9 us -> 33.5 us
  starting transfers between devices: 17.5 us -> 61.8 us
  between operations: 14.7 us -> 1.5 us
  Pallas kernels: 4.37 us -> 11.6 us
  blocking collectives: 28.8 us -> 23.3 us
  local copies, waits for them, and re-layouts: 2.92 us -> 4.65 us
    reduce_scatter x1 -> x0, waiting for transfers between devices: 67.8 us -> none  [local(): lax.psum_scatter(grads[0], 'dp', scatter_dimension=0, tiled=True)[0]]
    ppermute x0 -> x11, starting transfers between devices: none -> 45.2 us  [the longest x5 30.5 us: ring_terms(): above = lax.ppermute(above, axis, lowering)]
    ppermute x0 -> x11, waiting for transfers between devices: none -> 18.1 us  [the longest x6 18.1 us: ring_terms(): below = lax.ppermute(below, axis, raising)]
    all_to_all x1, blocking collectives: 28.8 us -> 23.3 us  [local(): lax.all_to_all(update.reshape(slots, rows, BLK), 'fsdp', split_axis=0, co...]
    pallas_call x1, Pallas kernels: 1.08 us -> 6.49 us  [owner_work(): pl.pallas_call(kernel, out_shape=(jax.ShapeDtypeStruct((2, BLK, BLK), BF1...]
    pallas_call x0 -> x10, Pallas kernels: none -> 2.1 us  [the longest x9 2.07 us: added(): pl.pallas_call(kernel, out_shape=jax.ShapeDtypeStruct(total.shape, BF16),...]
    unnamed x2 -> x6, local copies, waits for them, and re-layouts: 0.95 us -> 2.68 us
  transfers between devices with their start and end apart: 2 -> 12, of which waited for: 2 -> 7; matrix products, arithmetic and copies ran while one was open for 1% -> 1% of each run, Pallas kernels for 0% -> 2%
where the time goes in v3:
time: 137 us; the launch traced here: 136 us
  starting transfers between devices  61.8 us (45%)
  waiting for transfers between devices  33.5 us (24%)
  blocking collectives  23.3 us (17%)
  Pallas kernels  11.6 us (8%)
  local copies, waits for them, and re-layouts  4.65 us (3%)
  between operations  1.5 us (1%)
    ppermute x5, starting transfers between devices, ring_terms(): above = lax.ppermute(above, axis, lowering)  30.5 us
    all_to_all x1, blocking collectives, local(): lax.all_to_all(update.reshape(slots, rows, BLK), 'fsdp', split_axis=0, co...  23.3 us
    ppermute x6, waiting for transfers between devices, ring_terms(): below = lax.ppermute(below, axis, raising)  18.1 us
    all_to_all x1, starting transfers between devices, local(): lax.all_to_all(pieces, 'fsdp', split_axis=0, concat_axis=0, tiled=True)  16.6 us
    all_to_all x1, waiting for transfers between devices, local(): lax.all_to_all(pieces, 'fsdp', split_axis=0, concat_axis=0, tiled=True)  15.4 us
    ppermute x6, starting transfers between devices, ring_terms(): below = lax.ppermute(below, axis, raising)  14.7 us
    pallas_call x1, Pallas kernels, owner_work(): pl.pallas_call(kernel, out_shape=(jax.ShapeDtypeStruct((2, BLK, BLK), BF1...  6.49 us
  transfers between devices with their start and end apart: 12, of which 7 were waited for; matrix products, arithmetic and copies ran while one was open for 1% of the time, Pallas kernels for 2%

profile of v3, /device:TPU:1, one launch (start us, length us, event | category | flops | bytes accessed | tf_op | source)
XLA Modules:
  0.0 136.4 jit_solution(2169475477108709430)
XLA Ops:
  0.7 1.9 %copy-done = bf16[1,12,8,16,1024]{4,3,2,1,0:T(8,128)(2,1)S(1)} copy-done((bf16[1,12,8,16,1024]{4,3,2,1,0:T(8,128)(2,1)S(1)}, bf16[1,12,8,16,1024]{4,3,2,1,0:T(8,128)(2,1)}, u32[]{:S(2)}) %copy-start) | copy-done | bytes 3145752
  2.6 4.8 %collective-permute-start = (bf16[8,16,1024]{2,1,0:T(8,128)(2,1)S(1)}, bf16[8,16,1024]{2,1,0:T(8,128)(2,1)S(1)}, u32[]{:S(2)}, u32[]{:S(2)}) collective-permute-start(bf16[8,16,1024]{2,1,0:T(8,128)(2,1)S(1)} %get-tuple-element.6), channel_id=1, source_target_pairs={{0,64},{64,128},{128,192},{192,256},{256,320},{320,384},{384,448},... | collective-permute-start | bytes 786440 | tf_op jit(solution)/shard_map/ppermute | solution.py:219
  7.4 12.2 %collective-permute-start.6 = (bf16[8,16,1024]{2,1,0:T(8,128)(2,1)S(1)}, bf16[8,16,1024]{2,1,0:T(8,128)(2,1)S(1)}, u32[]{:S(2)}, u32[]{:S(2)}) collective-permute-start(bf16[8,16,1024]{2,1,0:T(8,128)(2,1)S(1)} %get-tuple-element.7), channel_id=1, source_target_pairs={{0,704},{64,0},{128,64},{192,128},{256,192},{320,256},{384,320},{4... | collective-permute-start | bytes 786440 | tf_op jit(solution)/shard_map/ppermute | solution.py:223
  19.6 4.1 %collective-permute-done.total_ref = bf16[8,16,1024]{2,1,0:T(8,128)(2,1)S(1)} collective-permute-done((bf16[8,16,1024]{2,1,0:T(8,128)(2,1)S(1)}, bf16[8,16,1024]{2,1,0:T(8,128)(2,1)S(1)}, u32[]{:S(2)}, u32[]{:S(2)}) %collective-permute-start) | collective-permute-done | bytes 262176 | tf_op jit(solution)/shard_map/ppermute | solution.py:219
  23.8 1.9 %collective-permute-start.1 = (bf16[8,16,1024]{2,1,0:T(8,128)(2,1)S(1)}, bf16[8,16,1024]{2,1,0:T(8,128)(2,1)S(1)}, u32[]{:S(2)}, u32[]{:S(2)}) collective-permute-start(bf16[8,16,1024]{2,1,0:T(8,128)(2,1)S(1)} %added.9), channel_id=1, source_target_pairs={{0,64},{64,128},{128,192},{192,256},{256,320},{320,384},{384,448},... | collective-permute-start | bytes 786440 | tf_op jit(solution)/shard_map/ppermute | solution.py:219
  25.8 4.6 %collective-permute-start.7 = (bf16[8,16,1024]{2,1,0:T(8,128)(2,1)S(1)}, bf16[8,16,1024]{2,1,0:T(8,128)(2,1)S(1)}, u32[]{:S(2)}, u32[]{:S(2)}) collective-permute-start(bf16[8,16,1024]{2,1,0:T(8,128)(2,1)S(1)} %added.14), channel_id=1, source_target_pairs={{0,704},{64,0},{128,64},{192,128},{256,192},{320,256},{384,320},{4... | collective-permute-start | bytes 786440 | tf_op jit(solution)/shard_map/ppermute | solution.py:223
  30.4 3.1 %collective-permute-done.1.total_ref = bf16[8,16,1024]{2,1,0:T(8,128)(2,1)S(1)} collective-permute-done((bf16[8,16,1024]{2,1,0:T(8,128)(2,1)S(1)}, bf16[8,16,1024]{2,1,0:T(8,128)(2,1)S(1)}, u32[]{:S(2)}, u32[]{:S(2)}) %collective-permute-start.1) | collective-permute-done | bytes 262176 | tf_op jit(solution)/shard_map/ppermute | solution.py:219
  33.5 1.9 %collective-permute-start.2 = (bf16[8,16,1024]{2,1,0:T(8,128)(2,1)S(1)}, bf16[8,16,1024]{2,1,0:T(8,128)(2,1)S(1)}, u32[]{:S(2)}, u32[]{:S(2)}) collective-permute-start(bf16[8,16,1024]{2,1,0:T(8,128)(2,1)S(1)} %added.10), channel_id=1, source_target_pairs={{0,64},{64,128},{128,192},{192,256},{256,320},{320,384},{384,448},... | collective-permute-start | bytes 786440 | tf_op jit(solution)/shard_map/ppermute | solution.py:219
  35.6 4.6 %collective-permute-start.8 = (bf16[8,16,1024]{2,1,0:T(8,128)(2,1)S(1)}, bf16[8,16,1024]{2,1,0:T(8,128)(2,1)S(1)}, u32[]{:S(2)}, u32[]{:S(2)}) collective-permute-start(bf16[8,16,1024]{2,1,0:T(8,128)(2,1)S(1)} %added.15), channel_id=1, source_target_pairs={{0,704},{64,0},{128,64},{192,128},{256,192},{320,256},{384,320},{4... | collective-permute-start | bytes 786440 | tf_op jit(solution)/shard_map/ppermute | solution.py:223
  40.2 2.2 %collective-permute-done.2.total_ref = bf16[8,16,1024]{2,1,0:T(8,128)(2,1)S(1)} collective-permute-done((bf16[8,16,1024]{2,1,0:T(8,128)(2,1)S(1)}, bf16[8,16,1024]{2,1,0:T(8,128)(2,1)S(1)}, u32[]{:S(2)}, u32[]{:S(2)}) %collective-permute-start.2) | collective-permute-done | bytes 262176 | tf_op jit(solution)/shard_map/ppermute | solution.py:219
  42.4 1.9 %collective-permute-start.3 = (bf16[8,16,1024]{2,1,0:T(8,128)(2,1)S(1)}, bf16[8,16,1024]{2,1,0:T(8,128)(2,1)S(1)}, u32[]{:S(2)}, u32[]{:S(2)}) collective-permute-start(bf16[8,16,1024]{2,1,0:T(8,128)(2,1)S(1)} %added.11), channel_id=1, source_target_pairs={{0,64},{64,128},{128,192},{192,256},{256,320},{320,384},{384,448},... | collective-permute-start | bytes 786440 | tf_op jit(solution)/shard_map/ppermute | solution.py:219
  44.4 4.6 %collective-permute-start.9 = (bf16[8,16,1024]{2,1,0:T(8,128)(2,1)S(1)}, bf16[8,16,1024]{2,1,0:T(8,128)(2,1)S(1)}, u32[]{:S(2)}, u32[]{:S(2)}) collective-permute-start(bf16[8,16,1024]{2,1,0:T(8,128)(2,1)S(1)} %added.16), channel_id=1, source_target_pairs={{0,704},{64,0},{128,64},{192,128},{256,192},{320,256},{384,320},{4... | collective-permute-start | bytes 786440 | tf_op jit(solution)/shard_map/ppermute | solution.py:223
  49.0 1.7 %collective-permute-done.3.total_ref = bf16[8,16,1024]{2,1,0:T(8,128)(2,1)S(1)} collective-permute-done((bf16[8,16,1024]{2,1,0:T(8,128)(2,1)S(1)}, bf16[8,16,1024]{2,1,0:T(8,128)(2,1)S(1)}, u32[]{:S(2)}, u32[]{:S(2)}) %collective-permute-start.3) | collective-permute-done | bytes 262176 | tf_op jit(solution)/shard_map/ppermute | solution.py:219
  50.8 2.2 %collective-permute-start.4 = (bf16[8,16,1024]{2,1,0:T(8,128)(2,1)S(1)}, bf16[8,16,1024]{2,1,0:T(8,128)(2,1)S(1)}, u32[]{:S(2)}, u32[]{:S(2)}) collective-permute-start(bf16[8,16,1024]{2,1,0:T(8,128)(2,1)S(1)} %added.12), channel_id=1, source_target_pairs={{0,64},{64,128},{128,192},{192,256},{256,320},{320,384},{384,448},... | collective-permute-start | bytes 786440 | tf_op jit(solution)/shard_map/ppermute | solution.py:219
  53.8 4.6 %collective-permute-start.10 = (bf16[8,16,1024]{2,1,0:T(8,128)(2,1)}, bf16[8,16,1024]{2,1,0:T(8,128)(2,1)S(1)}, u32[]{:S(2)}, u32[]{:S(2)}) collective-permute-start(bf16[8,16,1024]{2,1,0:T(8,128)(2,1)} %added.17), channel_id=1, source_target_pairs={{0,704},{64,0},{128,64},{192,128},{256,192},{320,256},{384,320},{4... | collective-permute-start | bytes 786440 | tf_op jit(solution)/shard_map/ppermute | solution.py:223
  60.2 1.9 %collective-permute-start.5 = (bf16[8,16,1024]{2,1,0:T(8,128)(2,1)}, bf16[8,16,1024]{2,1,0:T(8,128)(2,1)}, u32[]{:S(2)}, u32[]{:S(2)}) collective-permute-start(bf16[8,16,1024]{2,1,0:T(8,128)(2,1)} %added.13), channel_id=1, source_target_pairs={{0,64},{64,128},{128,192},{192,256},{256,320},{320,384},{384,448},... | collective-permute-start | bytes 786440 | tf_op jit(solution)/shard_map/ppermute | solution.py:219
  62.8 6.0 %collective-permute-done.5.below_ref = bf16[8,16,1024]{2,1,0:T(8,128)(2,1)} collective-permute-done((bf16[8,16,1024]{2,1,0:T(8,128)(2,1)}, bf16[8,16,1024]{2,1,0:T(8,128)(2,1)}, u32[]{:S(2)}, u32[]{:S(2)}) %collective-permute-start.5) | collective-permute-done | bytes 262176 | tf_op jit(solution)/shard_map/ppermute | solution.py:219
  68.8 1.4 %outgoing.1 = bf16[64,8,512]{2,1,0:T(8,128)(2,1)S(1)} custom-call(s32[1]{0:T(128)} %bitcast.2.here_ref, s32[64]{0:T(128)S(1)} %dynamic-slice_bitcast_fusion.table_ref, bf16[8,16,1024]{2,1,0:T(8,128)(2,1)} %collective-permute-done.5.below_ref, bf16[8,16,1024]{2,1,0:T(8,128)(2,1)S(1)} %collective-permute-done.10.above_ref, bf16[12,8,16,1024]{3,2,1,0:T(8,128)(2,1)S(1)} %bitcast.19), custom_call_target="tpu_custom_call" | custom-call | bytes 1572864 | tf_op jit(solution)/shard_map/outgoing/pallas_call | solution.py:59
  71.0 16.6 %all-to-all-start = ((bf16[64,8,512]{2,1,0:T(8,128)(2,1)}), bf16[64,8,512]{2,1,0:T(8,128)(2,1)S(1)}, u32[]{:S(2)}, u32[]{:S(2)}) async-start(bf16[64,8,512]{2,1,0:T(8,128)(2,1)} %copy-done.2), calls=%async_computation | async-start | bytes 1048576 | tf_op jit(solution)/shard_map/all_to_all | solution.py:238
  87.6 1.3 dynamic_slice.8
  89.5 15.4 %all-to-all-done = bf16[64,8,512]{2,1,0:T(8,128)(2,1)S(1)} async-done(((bf16[64,8,512]{2,1,0:T(8,128)(2,1)}), bf16[64,8,512]{2,1,0:T(8,128)(2,1)S(1)}, u32[]{:S(2)}, u32[]{:S(2)}) %all-to-all-start) | async-done | bytes 524320 | tf_op jit(solution)/shard_map/all_to_all | solution.py:238
  104.9 6.5 %owner.1 = (bf16[2,512,512]{2,1,0:T(8,128)(2,1)}, bf16[512,512]{1,0:T(8,128)(2,1)S(1)}) custom-call(s32[1]{0:T(128)} %bitcast.1.active_ref, bf16[512,512]{1,0:T(8,128)(2,1)S(1)} %bitcast.20), custom_call_target="tpu_custom_call" | custom-call | flops 3221225472 | bytes 2097152 | tf_op jit(solution)/shard_map/owner/pallas_call | solution.py:159
  111.4 23.3 %all_to_all.10.x_ref = bf16[64,8,512]{2,1,0:T(8,128)(2,1)S(1)} all-to-all(bf16[64,8,512]{2,1,0:T(8,128)(2,1)S(1)} %bitcast.21), channel_id=1, replica_groups=mesh['dp'=12,'fsdp'=64] {'fsdp'}, dimensions={0} | all-to-all | bytes 1048576 | tf_op jit(solution)/shard_map/all_to_all | solution.py:240
  134.7 1.6 %incoming.1 = bf16[8,16,1024]{2,1,0:T(8,128)(2,1)} custom-call(s32[64]{0:T(128)S(1)} %dynamic-slice_bitcast_fusion.table_ref, bf16[64,8,512]{2,1,0:T(8,128)(2,1)S(1)} %all_to_all.10.x_ref), custom_call_target="tpu_custom_call" | custom-call | bytes 1572864 | tf_op jit(solution)/shard_map/incoming/pallas_call | solution.py:93
  (22 shorter events, 4.6 us)
Async XLA Ops:
  0.6 1.9 %copy-start = (bf16[1,12,8,16,1024]{4,3,2,1,0:T(8,128)(2,1)S(1)}, bf16[1,12,8,16,1024]{4,3,2,1,0:T(8,128)(2,1)}, u32[]{:S(2)}) copy-start(bf16[1,12,8,16,1024]{4,3,2,1,0:T(8,128)(2,1)} %param.2) | copy-start | bytes 9437188
  2.6 21.2 %collective-permute-start = (bf16[8,16,1024]{2,1,0:T(8,128)(2,1)S(1)}, bf16[8,16,1024]{2,1,0:T(8,128)(2,1)S(1)}, u32[]{:S(2)}, u32[]{:S(2)}) collective-permute-start(bf16[8,16,1024]{2,1,0:T(8,128)(2,1)S(1)} %get-tuple-element.6), channel_id=1, source_target_pairs={{0,64},{64,128},{128,192},{192,256},{256,320},{320,384},{384,448},... | collective-permute-start | bytes 786440 | tf_op jit(solution)/shard_map/ppermute | solution.py:219
  7.4 18.3 %collective-permute-start.6 = (bf16[8,16,1024]{2,1,0:T(8,128)(2,1)S(1)}, bf16[8,16,1024]{2,1,0:T(8,128)(2,1)S(1)}, u32[]{:S(2)}, u32[]{:S(2)}) collective-permute-start(bf16[8,16,1024]{2,1,0:T(8,128)(2,1)S(1)} %get-tuple-element.7), channel_id=1, source_target_pairs={{0,704},{64,0},{128,64},{192,128},{256,192},{320,256},{384,320},{4... | collective-permute-start | bytes 786440 | tf_op jit(solution)/shard_map/ppermute | solution.py:223
  23.8 9.7 %collective-permute-start.1 = (bf16[8,16,1024]{2,1,0:T(8,128)(2,1)S(1)}, bf16[8,16,1024]{2,1,0:T(8,128)(2,1)S(1)}, u32[]{:S(2)}, u32[]{:S(2)}) collective-permute-start(bf16[8,16,1024]{2,1,0:T(8,128)(2,1)S(1)} %added.9), channel_id=1, source_target_pairs={{0,64},{64,128},{128,192},{192,256},{256,320},{320,384},{384,448},... | collective-permute-start | bytes 786440 | tf_op jit(solution)/shard_map/ppermute | solution.py:219
  25.8 9.7 %collective-permute-start.7 = (bf16[8,16,1024]{2,1,0:T(8,128)(2,1)S(1)}, bf16[8,16,1024]{2,1,0:T(8,128)(2,1)S(1)}, u32[]{:S(2)}, u32[]{:S(2)}) collective-permute-start(bf16[8,16,1024]{2,1,0:T(8,128)(2,1)S(1)} %added.14), channel_id=1, source_target_pairs={{0,704},{64,0},{128,64},{192,128},{256,192},{320,256},{384,320},{4... | collective-permute-start | bytes 786440 | tf_op jit(solution)/shard_map/ppermute | solution.py:223
  33.5 8.8 %collective-permute-start.2 = (bf16[8,16,1024]{2,1,0:T(8,128)(2,1)S(1)}, bf16[8,16,1024]{2,1,0:T(8,128)(2,1)S(1)}, u32[]{:S(2)}, u32[]{:S(2)}) collective-permute-start(bf16[8,16,1024]{2,1,0:T(8,128)(2,1)S(1)} %added.10), channel_id=1, source_target_pairs={{0,64},{64,128},{128,192},{192,256},{256,320},{320,384},{384,448},... | collective-permute-start | bytes 786440 | tf_op jit(solution)/shard_map/ppermute | solution.py:219
  35.6 8.7 %collective-permute-start.8 = (bf16[8,16,1024]{2,1,0:T(8,128)(2,1)S(1)}, bf16[8,16,1024]{2,1,0:T(8,128)(2,1)S(1)}, u32[]{:S(2)}, u32[]{:S(2)}) collective-permute-start(bf16[8,16,1024]{2,1,0:T(8,128)(2,1)S(1)} %added.15), channel_id=1, source_target_pairs={{0,704},{64,0},{128,64},{192,128},{256,192},{320,256},{384,320},{4... | collective-permute-start | bytes 786440 | tf_op jit(solution)/shard_map/ppermute | solution.py:223
  42.4 8.3 %collective-permute-start.3 = (bf16[8,16,1024]{2,1,0:T(8,128)(2,1)S(1)}, bf16[8,16,1024]{2,1,0:T(8,128)(2,1)S(1)}, u32[]{:S(2)}, u32[]{:S(2)}) collective-permute-start(bf16[8,16,1024]{2,1,0:T(8,128)(2,1)S(1)} %added.11), channel_id=1, source_target_pairs={{0,64},{64,128},{128,192},{192,256},{256,320},{320,384},{384,448},... | collective-permute-start | bytes 786440 | tf_op jit(solution)/shard_map/ppermute | solution.py:219
  44.4 8.6 %collective-permute-start.9 = (bf16[8,16,1024]{2,1,0:T(8,128)(2,1)S(1)}, bf16[8,16,1024]{2,1,0:T(8,128)(2,1)S(1)}, u32[]{:S(2)}, u32[]{:S(2)}) collective-permute-start(bf16[8,16,1024]{2,1,0:T(8,128)(2,1)S(1)} %added.16), channel_id=1, source_target_pairs={{0,704},{64,0},{128,64},{192,128},{256,192},{320,256},{384,320},{4... | collective-permute-start | bytes 786440 | tf_op jit(solution)/shard_map/ppermute | solution.py:223
  50.8 18.0 %copy-start.1 = (bf16[1,12,8,16,1024]{4,3,2,1,0:T(8,128)(2,1)S(1)}, bf16[1,12,8,16,1024]{4,3,2,1,0:T(8,128)(2,1)}, u32[]{:S(2)}) copy-start(bf16[1,12,8,16,1024]{4,3,2,1,0:T(8,128)(2,1)} %param.2) | copy-start | bytes 9437188
  50.8 8.6 %collective-permute-start.4 = (bf16[8,16,1024]{2,1,0:T(8,128)(2,1)S(1)}, bf16[8,16,1024]{2,1,0:T(8,128)(2,1)S(1)}, u32[]{:S(2)}, u32[]{:S(2)}) collective-permute-start(bf16[8,16,1024]{2,1,0:T(8,128)(2,1)S(1)} %added.12), channel_id=1, source_target_pairs={{0,64},{64,128},{128,192},{192,256},{256,320},{320,384},{384,448},... | collective-permute-start | bytes 786440 | tf_op jit(solution)/shard_map/ppermute | solution.py:219
  53.8 9.0 %collective-permute-start.10 = (bf16[8,16,1024]{2,1,0:T(8,128)(2,1)}, bf16[8,16,1024]{2,1,0:T(8,128)(2,1)S(1)}, u32[]{:S(2)}, u32[]{:S(2)}) collective-permute-start(bf16[8,16,1024]{2,1,0:T(8,128)(2,1)} %added.17), channel_id=1, source_target_pairs={{0,704},{64,0},{128,64},{192,128},{256,192},{320,256},{384,320},{4... | collective-permute-start | bytes 786440 | tf_op jit(solution)/shard_map/ppermute | solution.py:223
  60.2 8.6 %collective-permute-start.5 = (bf16[8,16,1024]{2,1,0:T(8,128)(2,1)}, bf16[8,16,1024]{2,1,0:T(8,128)(2,1)}, u32[]{:S(2)}, u32[]{:S(2)}) collective-permute-start(bf16[8,16,1024]{2,1,0:T(8,128)(2,1)} %added.13), channel_id=1, source_target_pairs={{0,64},{64,128},{128,192},{192,256},{256,320},{320,384},{384,448},... | collective-permute-start | bytes 786440 | tf_op jit(solution)/shard_map/ppermute | solution.py:219
  70.2 0.8 copy-start.2
  71.0 34.0 %all-to-all-start = ((bf16[64,8,512]{2,1,0:T(8,128)(2,1)}), bf16[64,8,512]{2,1,0:T(8,128)(2,1)S(1)}, u32[]{:S(2)}, u32[]{:S(2)}) async-start(bf16[64,8,512]{2,1,0:T(8,128)(2,1)} %copy-done.2), calls=%async_computation | async-start | bytes 1048576 | tf_op jit(solution)/shard_map/all_to_all | solution.py:238

commit v4 on v3

--- a/solution.py
+++ b/solution.py
@@ -31,13 +31,48 @@
     return pltpu.CompilerParams(vmem_limit_bytes=VMEM_LIMIT)
 
 
-def outgoing_pieces(here, table, terms, parts):
+def assigned(table):
+    slots = table.shape[0]
+    chips = slots // 2
+
+    def kernel(table_ref, first_ref, second_ref, spare):
+        def collect(p, count):
+            low, high = table_ref[2 * p], table_ref[2 * p + 1]
+            two = jnp.logical_and(low < chips, high < chips)
+            first_ref[p] = jnp.minimum(jnp.where(low < chips, low, high), chips)
+            second_ref[p] = jnp.where(two, high, chips)
+            spare[count] = high
+            return count + two.astype(jnp.int32)
+
+        def fill(p, count):
+            empty = first_ref[p] == chips
+            first_ref[p] = jnp.where(empty, spare[count], first_ref[p])
+            return count + empty.astype(jnp.int32)
+
+        lax.fori_loop(0, chips, collect, jnp.int32(0))
+        lax.fori_loop(0, chips, fill, jnp.int32(0))
+
+    return pl.pallas_call(
+        kernel,
+        out_shape=[jax.ShapeDtypeStruct((chips,), jnp.int32)] * 2,
+        in_specs=[smem()],
+        out_specs=[smem(), smem()],
+        scratch_shapes=[pltpu.SMEM((chips + 1,), jnp.int32)],
+        compiler_params=params(),
+        cost_estimate=cost(0, 1024),
+        name="assigned",
+    )(table)
+
+
+def outgoing_pieces(here, first, second, terms, parts):
     rows, row_blocks, cols = terms[0].shape
     col_blocks = cols // BLK
     group = row_blocks * col_blocks
-    slots = table.shape[0]
-
-    def kernel(here_ref, table_ref, below_ref, above_ref, parts_ref, out_ref, wide, pieces):
+    chips = first.shape[0]
+
+    def kernel(
+        here_ref, first_ref, second_ref, below_ref, above_ref, parts_ref, one_ref, two_ref, wide, pieces
+    ):
         for k in range(cols // LANES):
             at = (slice(None), slice(None), slice(k * LANES, (k + 1) * LANES))
             lanes = below_ref[at].astype(F32) + above_ref[at].astype(F32)
@@ -48,39 +83,40 @@
                 v, at = rb * col_blocks + k // PER_BLK, k % PER_BLK * LANES
                 part = wide[k, pl.ds(rb, rows, stride=row_blocks), :]
                 pieces[v, :, at : at + LANES] = part.astype(BF16)
-        pieces[group:] = jnp.zeros((slots - group, rows, BLK), BF16)
-
-        def place(s, carry):
-            out_ref[s] = pieces[table_ref[s]]
+        pieces[group] = jnp.zeros((rows, BLK), BF16)
+
+        def place(p, carry):
+            one_ref[p] = pieces[first_ref[p]]
+            two_ref[p] = pieces[second_ref[p]]
             return carry
 
-        lax.fori_loop(0, slots, place, 0, unroll=8)
-
-    return pl.pallas_call(
-        kernel,
-        out_shape=jax.ShapeDtypeStruct((slots, rows, BLK), BF16),
-        in_specs=[smem(), smem(), vmem(), vmem(), vmem()],
-        out_specs=vmem(),
+        lax.fori_loop(0, chips, place, 0, unroll=4)
+
+    return pl.pallas_call(
+        kernel,
+        out_shape=[jax.ShapeDtypeStruct((chips, rows, BLK), BF16)] * 2,
+        in_specs=[smem(), smem(), smem(), vmem(), vmem(), vmem()],
+        out_specs=[vmem(), vmem()],
         scratch_shapes=[
             pltpu.VMEM((cols // LANES, rows * row_blocks, LANES), F32),
-            pltpu.VMEM((slots, rows, BLK), BF16),
+            pltpu.VMEM((group + 1, rows, BLK), BF16),
         ],
         compiler_params=params(),
-        cost_estimate=cost(0, 3 * slots * rows * BLK * 2),
+        cost_estimate=cost(0, 6 * chips * rows * BLK * 2),
         name="outgoing",
-    )(here, table, *terms, parts)
-
-
-def incoming_update(table, returned, row_blocks, col_blocks):
-    slots, rows, _ = returned.shape
+    )(here, first, second, *terms, parts)
+
+
+def incoming_update(first, returned, row_blocks, col_blocks):
+    chips, rows, _ = returned.shape
     cols = col_blocks * BLK
 
-    def kernel(table_ref, x_ref, out_ref, wide, pieces):
+    def kernel(first_ref, x_ref, out_ref, wide, pieces):
         def place(s, carry):
-            pieces[table_ref[s]] = x_ref[s]
+            pieces[first_ref[s]] = x_ref[s]
             return carry
 
-        lax.fori_loop(0, slots, place, 0, unroll=8)
+        lax.fori_loop(0, chips, place, 0, unroll=4)
         for rb in range(row_blocks):
             for k in range(cols // LANES):
                 v, at = rb * col_blocks + k // PER_BLK, k % PER_BLK * LANES
@@ -97,12 +133,12 @@
         out_specs=vmem(),
         scratch_shapes=[
             pltpu.VMEM((cols // LANES, rows * row_blocks, LANES), F32),
-            pltpu.VMEM((slots, rows, BLK), BF16),
+            pltpu.VMEM((chips, rows, BLK), BF16),
         ],
         compiler_params=params(),
-        cost_estimate=cost(0, 3 * slots * rows * BLK * 2),
+        cost_estimate=cost(0, 3 * chips * rows * BLK * 2),
         name="incoming",
-    )(table, returned)
+    )(first, returned)
 
 
 def dot(a, b, contract=((1,), (0,))):
@@ -128,46 +164,85 @@
     return root
 
 
-def owner_work(active, block, replicas):
-    def kernel(active_ref, x_ref, roots_ref, update_ref):
-        @pl.when(active_ref[0] == 0)
-        def _():
-            roots_ref[...] = jnp.zeros_like(roots_ref)
-            update_ref[...] = jnp.zeros_like(update_ref)
-
-        @pl.when(active_ref[0] != 0)
-        def _():
-            eye = (
-                lax.broadcasted_iota(jnp.int32, (BLK, BLK), 0)
-                == lax.broadcasted_iota(jnp.int32, (BLK, BLK), 1)
-            ).astype(F32)
-            x = x_ref[...]
-            wide = x.astype(F32)
-            scale = 1.0 / (replicas * replicas)
-            total = jnp.sum(wide * wide) * scale
-            left = newton_root(dot(x, x, ((1,), (1,))) * scale, total, eye)
-            roots_ref[0] = left
-            right = newton_root(dot(x, x, ((0,), (0,))) * scale, total, eye)
-            roots_ref[1] = right
-            partial = (dot(left, x) * (1.0 / replicas)).astype(BF16)
-            direction = dot(partial, right)
-            count = BLK * BLK
-            grad_rms = jnp.sqrt(total / count)
-            dir_rms = jnp.sqrt(jnp.sum(direction * direction) / count + 1e-06)
-            update_ref[...] = (-(grad_rms / dir_rms) * direction).astype(BF16)
+def whole_block(core_ref, mine_ref, other_ref, halves):
+    halves[:, core_ref[0]] = mine_ref[...].astype(F32)
+    halves[:, 1 - core_ref[0]] = other_ref[...].astype(F32)
+    return halves[...].reshape(BLK, BLK)
+
+
+def both_roots(wide, replicas):
+    eye = (
+        lax.broadcasted_iota(jnp.int32, (BLK, BLK), 0)
+        == lax.broadcasted_iota(jnp.int32, (BLK, BLK), 1)
+    ).astype(F32)
+    x = wide.astype(BF16)
+    scale = 1.0 / (replicas * replicas)
+    total = jnp.sum(wide * wide) * scale
+    left = newton_root(dot(x, x, ((1,), (1,))) * scale, total, eye)
+    right = newton_root(dot(x, x, ((0,), (0,))) * scale, total, eye)
+    return x, total, left, right
+
+
+def first_work(core, mine, other, replicas):
+    chips, rows, _ = mine.shape
+
+    def kernel(core_ref, mine_ref, other_ref, roots_ref, update_ref, halves):
+        wide = whole_block(core_ref, mine_ref, other_ref, halves)
+        x, total, left, right = both_roots(wide, replicas)
+        roots_ref[0] = left
+        roots_ref[1] = right
+        partial = (dot(left, x) * (1.0 / replicas)).astype(BF16)
+        direction = dot(partial, right)
+        count = BLK * BLK
+        grad_rms = jnp.sqrt(total / count)
+        dir_rms = jnp.sqrt(jnp.sum(direction * direction) / count + 1e-06)
+        halves[...] = (-(grad_rms / dir_rms) * direction).reshape(chips, 2, rows, BLK)
+        update_ref[...] = halves[:, core_ref[0]].astype(BF16)
 
     return pl.pallas_call(
         kernel,
         out_shape=(
             jax.ShapeDtypeStruct((2, BLK, BLK), BF16),
-            jax.ShapeDtypeStruct((BLK, BLK), BF16),
+            jax.ShapeDtypeStruct((chips, rows, BLK), BF16),
         ),
-        in_specs=[smem(), vmem()],
+        in_specs=[smem(), vmem(), vmem()],
         out_specs=(vmem(), vmem()),
+        scratch_shapes=[pltpu.VMEM((chips, 2, rows, BLK), F32)],
         compiler_params=params(),
         cost_estimate=cost(24 * BLK**3, 8 * BLK * BLK),
-        name="owner",
-    )(active, block)
+        name="first_work",
+    )(core, mine, other)
+
+
+def second_work(mode, core, mine, other, roots, replicas):
+    chips, rows, _ = mine.shape
+
+    def kernel(mode_ref, core_ref, mine_ref, other_ref, roots_ref, out_ref, halves):
+        @pl.when(mode_ref[0] == 0)
+        def _():
+            out_ref[...] = jnp.zeros_like(out_ref)
+
+        @pl.when(mode_ref[0] == 1)
+        def _():
+            out_ref[...] = roots_ref[...]
+
+        @pl.when(mode_ref[0] == 2)
+        def _():
+            wide = whole_block(core_ref, mine_ref, other_ref, halves)
+            _, _, left, right = both_roots(wide, replicas)
+            out_ref[0] = left
+            out_ref[1] = right
+
+    return pl.pallas_call(
+        kernel,
+        out_shape=jax.ShapeDtypeStruct((2, BLK, BLK), BF16),
+        in_specs=[smem(), smem(), vmem(), vmem(), vmem()],
+        out_specs=vmem(),
+        scratch_shapes=[pltpu.VMEM((chips, 2, rows, BLK), F32)],
+        compiler_params=params(),
+        cost_estimate=cost(20 * BLK**3, 8 * BLK * BLK),
+        name="second_work",
+    )(mode, core, mine, other, roots)
 
 
 def part_at(parts_ref, here_ref, offset):
@@ -226,21 +301,36 @@
 
 def local(grads, slot_block):
     replicas = lax.axis_size("dp")
+    slot = lax.axis_index("fsdp")
     table = lax.dynamic_index_in_dim(slot_block, lax.axis_index("dp"), 0, keepdims=False)
-    slots = table.shape[0]
+    chips = table.shape[0] // 2
+    same_core = [[2 * p + c for p in range(chips)] for c in range(2)]
+    across = [(i, i ^ 1) for i in range(2 * chips)]
+
+    def exchanged(x):
+        return lax.all_to_all(
+            x, "fsdp", split_axis=0, concat_axis=0, axis_index_groups=same_core, tiled=True
+        )
+
+    first, second = assigned(table)
+    core = (slot % 2)[None]
+    kept = lax.dynamic_slice_in_dim(table, slot, 1, 0)
+    worked = lax.dynamic_slice_in_dim(first, slot // 2, 1, 0)
+    mode = jnp.where(kept >= chips, 0, jnp.where(kept == worked, 1, 2)).astype(jnp.int32)
     here = lax.axis_index("dp")[None]
     terms = ring_terms(here, grads[0], "dp")
-    rows, row_blocks, cols = terms[0].shape
-    col_blocks = cols // BLK
-    group = row_blocks * col_blocks
-    active = lax.dynamic_slice_in_dim(table, lax.axis_index("fsdp"), 1, 0) < group
-    pieces = outgoing_pieces(here, table, terms, grads[0])
-    received = lax.all_to_all(pieces, "fsdp", split_axis=0, concat_axis=0, tiled=True)
-    roots, update = owner_work(active.astype(jnp.int32), received.reshape(BLK, BLK), replicas)
-    returned = lax.all_to_all(
-        update.reshape(slots, rows, BLK), "fsdp", split_axis=0, concat_axis=0, tiled=True
-    )
-    result = incoming_update(table, returned, row_blocks, col_blocks)
+    _, row_blocks, cols = terms[0].shape
+    one, two = outgoing_pieces(here, first, second, terms, grads[0])
+    one_mine = exchanged(one)
+    one_mine, two = lax.optimization_barrier((one_mine, two))
+    two_mine = exchanged(two)
+    one_other = lax.ppermute(one_mine, "fsdp", across)
+    roots, update = first_work(core, one_mine, one_other, replicas)
+    update, two_mine = lax.optimization_barrier((update, two_mine))
+    returned = exchanged(update)
+    two_other = lax.ppermute(two_mine, "fsdp", across)
+    roots = second_work(mode, core, two_mine, two_other, roots, replicas)
+    result = incoming_update(first, returned, row_blocks, cols // BLK)
     return result[None], roots[None, None]
 
 

time: 137 us -> 137 us (level)
  the two profiles are of different devices: /device:TPU:1 before, /device:TPU:8 now
where the time goes in v4:
time: 137 us; the launch traced here: 136 us
  starting transfers between devices  59.8 us (44%)
  waiting for transfers between devices  34.4 us (25%)
  blocking collectives  20.9 us (15%)
  Pallas kernels  14 us (10%)
  local copies, waits for them, and re-layouts  4.46 us (3%)
  between operations  2.85 us (2%)
    ppermute x5, starting transfers between devices, ring_terms(): above = lax.ppermute(above, axis, lowering)  32.7 us
    all_to_all x1, blocking collectives, exchanged(): lax.all_to_all(x, 'fsdp', split_axis=0, concat_axis=0, axis_index_groups=...  20.9 us
    ppermute x6, waiting for transfers between devices, ring_terms(): below = lax.ppermute(below, axis, raising)  19.7 us
    all_to_all x2, waiting for transfers between devices, exchanged(): lax.all_to_all(x, 'fsdp', split_axis=0, concat_axis=0, axis_index_groups=...  14.6 us
    ppermute x6, starting transfers between devices, ring_terms(): below = lax.ppermute(below, axis, raising)  14.1 us
    all_to_all x2, starting transfers between devices, exchanged(): lax.all_to_all(x, 'fsdp', split_axis=0, concat_axis=0, axis_index_groups=...  9.1 us
    pallas_call x1, Pallas kernels, first_work(): pl.pallas_call(kernel, out_shape=(jax.ShapeDtypeStruct((2, BLK, BLK), BF1...  6.28 us
  transfers between devices with their start and end apart: 15, of which 8 were waited for; matrix products, arithmetic and copies ran while one was open for 2% of the time, Pallas kernels for 8%

profile of v4, /device:TPU:8, one launch (start us, length us, event | category | flops | bytes accessed | tf_op | source)
XLA Modules:
  0.0 136.5 jit_solution(11300128440176018568)
XLA Ops:
  2.6 4.3 %collective-permute-start = (bf16[8,16,1024]{2,1,0:T(8,128)(2,1)S(1)}, bf16[8,16,1024]{2,1,0:T(8,128)(2,1)S(1)}, u32[]{:S(2)}, u32[]{:S(2)}) collective-permute-start(bf16[8,16,1024]{2,1,0:T(8,128)(2,1)S(1)} %get-tuple-element.16), channel_id=1, source_target_pairs={{0,64},{64,128},{128,192},{192,256},{256,320},{320,384},{384,448},... | collective-permute-start | bytes 786440 | tf_op jit(solution)/shard_map/ppermute | solution.py:294
  6.9 12.2 %collective-permute-start.6 = (bf16[8,16,1024]{2,1,0:T(8,128)(2,1)S(1)}, bf16[8,16,1024]{2,1,0:T(8,128)(2,1)S(1)}, u32[]{:S(2)}, u32[]{:S(2)}) collective-permute-start(bf16[8,16,1024]{2,1,0:T(8,128)(2,1)S(1)} %get-tuple-element.17), channel_id=1, source_target_pairs={{0,704},{64,0},{128,64},{192,128},{256,192},{320,256},{384,320},{4... | collective-permute-start | bytes 786440 | tf_op jit(solution)/shard_map/ppermute | solution.py:298
  19.1 4.4 %collective-permute-done.total_ref = bf16[8,16,1024]{2,1,0:T(8,128)(2,1)S(1)} collective-permute-done((bf16[8,16,1024]{2,1,0:T(8,128)(2,1)S(1)}, bf16[8,16,1024]{2,1,0:T(8,128)(2,1)S(1)}, u32[]{:S(2)}, u32[]{:S(2)}) %collective-permute-start) | collective-permute-done | bytes 262176 | tf_op jit(solution)/shard_map/ppermute | solution.py:294
  23.5 1.9 %collective-permute-start.1 = (bf16[8,16,1024]{2,1,0:T(8,128)(2,1)S(1)}, bf16[8,16,1024]{2,1,0:T(8,128)(2,1)S(1)}, u32[]{:S(2)}, u32[]{:S(2)}) collective-permute-start(bf16[8,16,1024]{2,1,0:T(8,128)(2,1)S(1)} %added.9), channel_id=1, source_target_pairs={{0,64},{64,128},{128,192},{192,256},{256,320},{320,384},{384,448},... | collective-permute-start | bytes 786440 | tf_op jit(solution)/shard_map/ppermute | solution.py:294
  25.5 5.1 %collective-permute-start.7 = (bf16[8,16,1024]{2,1,0:T(8,128)(2,1)S(1)}, bf16[8,16,1024]{2,1,0:T(8,128)(2,1)S(1)}, u32[]{:S(2)}, u32[]{:S(2)}) collective-permute-start(bf16[8,16,1024]{2,1,0:T(8,128)(2,1)S(1)} %added.14), channel_id=1, source_target_pairs={{0,704},{64,0},{128,64},{192,128},{256,192},{320,256},{384,320},{4... | collective-permute-start | bytes 786440 | tf_op jit(solution)/shard_map/ppermute | solution.py:298
  30.7 3.4 %collective-permute-done.1.total_ref = bf16[8,16,1024]{2,1,0:T(8,128)(2,1)S(1)} collective-permute-done((bf16[8,16,1024]{2,1,0:T(8,128)(2,1)S(1)}, bf16[8,16,1024]{2,1,0:T(8,128)(2,1)S(1)}, u32[]{:S(2)}, u32[]{:S(2)}) %collective-permute-start.1) | collective-permute-done | bytes 262176 | tf_op jit(solution)/shard_map/ppermute | solution.py:294
  34.2 1.9 %collective-permute-start.2 = (bf16[8,16,1024]{2,1,0:T(8,128)(2,1)S(1)}, bf16[8,16,1024]{2,1,0:T(8,128)(2,1)S(1)}, u32[]{:S(2)}, u32[]{:S(2)}) collective-permute-start(bf16[8,16,1024]{2,1,0:T(8,128)(2,1)S(1)} %added.10), channel_id=1, source_target_pairs={{0,64},{64,128},{128,192},{192,256},{256,320},{320,384},{384,448},... | collective-permute-start | bytes 786440 | tf_op jit(solution)/shard_map/ppermute | solution.py:294
  36.2 5.1 %collective-permute-start.8 = (bf16[8,16,1024]{2,1,0:T(8,128)(2,1)S(1)}, bf16[8,16,1024]{2,1,0:T(8,128)(2,1)S(1)}, u32[]{:S(2)}, u32[]{:S(2)}) collective-permute-start(bf16[8,16,1024]{2,1,0:T(8,128)(2,1)S(1)} %added.15), channel_id=1, source_target_pairs={{0,704},{64,0},{128,64},{192,128},{256,192},{320,256},{384,320},{4... | collective-permute-start | bytes 786440 | tf_op jit(solution)/shard_map/ppermute | solution.py:298
  41.4 2.5 %collective-permute-done.2.total_ref = bf16[8,16,1024]{2,1,0:T(8,128)(2,1)S(1)} collective-permute-done((bf16[8,16,1024]{2,1,0:T(8,128)(2,1)S(1)}, bf16[8,16,1024]{2,1,0:T(8,128)(2,1)S(1)}, u32[]{:S(2)}, u32[]{:S(2)}) %collective-permute-start.2) | collective-permute-done | bytes 262176 | tf_op jit(solution)/shard_map/ppermute | solution.py:294
  43.9 1.9 %collective-permute-start.3 = (bf16[8,16,1024]{2,1,0:T(8,128)(2,1)S(1)}, bf16[8,16,1024]{2,1,0:T(8,128)(2,1)S(1)}, u32[]{:S(2)}, u32[]{:S(2)}) collective-permute-start(bf16[8,16,1024]{2,1,0:T(8,128)(2,1)S(1)} %added.11), channel_id=1, source_target_pairs={{0,64},{64,128},{128,192},{192,256},{256,320},{320,384},{384,448},... | collective-permute-start | bytes 786440 | tf_op jit(solution)/shard_map/ppermute | solution.py:294
  46.0 5.1 %collective-permute-start.9 = (bf16[8,16,1024]{2,1,0:T(8,128)(2,1)S(1)}, bf16[8,16,1024]{2,1,0:T(8,128)(2,1)S(1)}, u32[]{:S(2)}, u32[]{:S(2)}) collective-permute-start(bf16[8,16,1024]{2,1,0:T(8,128)(2,1)S(1)} %added.16), channel_id=1, source_target_pairs={{0,704},{64,0},{128,64},{192,128},{256,192},{320,256},{384,320},{4... | collective-permute-start | bytes 786440 | tf_op jit(solution)/shard_map/ppermute | solution.py:298
  51.1 2.3 %collective-permute-done.3.total_ref = bf16[8,16,1024]{2,1,0:T(8,128)(2,1)S(1)} collective-permute-done((bf16[8,16,1024]{2,1,0:T(8,128)(2,1)S(1)}, bf16[8,16,1024]{2,1,0:T(8,128)(2,1)S(1)}, u32[]{:S(2)}, u32[]{:S(2)}) %collective-permute-start.3) | collective-permute-done | bytes 262176 | tf_op jit(solution)/shard_map/ppermute | solution.py:294
  53.5 2.2 %collective-permute-start.4 = (bf16[8,16,1024]{2,1,0:T(8,128)(2,1)S(1)}, bf16[8,16,1024]{2,1,0:T(8,128)(2,1)S(1)}, u32[]{:S(2)}, u32[]{:S(2)}) collective-permute-start(bf16[8,16,1024]{2,1,0:T(8,128)(2,1)S(1)} %added.12), channel_id=1, source_target_pairs={{0,64},{64,128},{128,192},{192,256},{256,320},{320,384},{384,448},... | collective-permute-start | bytes 786440 | tf_op jit(solution)/shard_map/ppermute | solution.py:294
  56.5 5.1 %collective-permute-start.10 = (bf16[8,16,1024]{2,1,0:T(8,128)(2,1)}, bf16[8,16,1024]{2,1,0:T(8,128)(2,1)S(1)}, u32[]{:S(2)}, u32[]{:S(2)}) collective-permute-start(bf16[8,16,1024]{2,1,0:T(8,128)(2,1)} %added.17), channel_id=1, source_target_pairs={{0,704},{64,0},{128,64},{192,128},{256,192},{320,256},{384,320},{4... | collective-permute-start | bytes 786440 | tf_op jit(solution)/shard_map/ppermute | solution.py:298
  64.0 1.9 %collective-permute-start.5 = (bf16[8,16,1024]{2,1,0:T(8,128)(2,1)}, bf16[8,16,1024]{2,1,0:T(8,128)(2,1)}, u32[]{:S(2)}, u32[]{:S(2)}) collective-permute-start(bf16[8,16,1024]{2,1,0:T(8,128)(2,1)} %added.13), channel_id=1, source_target_pairs={{0,64},{64,128},{128,192},{192,256},{256,320},{320,384},{384,448},... | collective-permute-start | bytes 786440 | tf_op jit(solution)/shard_map/ppermute | solution.py:294
  68.3 5.5 %collective-permute-done.5.below_ref = bf16[8,16,1024]{2,1,0:T(8,128)(2,1)} collective-permute-done((bf16[8,16,1024]{2,1,0:T(8,128)(2,1)}, bf16[8,16,1024]{2,1,0:T(8,128)(2,1)}, u32[]{:S(2)}, u32[]{:S(2)}) %collective-permute-start.5) | collective-permute-done | bytes 262176 | tf_op jit(solution)/shard_map/ppermute | solution.py:294
  75.2 20.9 %all_to_all.15.mine_ref = bf16[32,8,512]{2,1,0:T(8,128)(2,1)S(1)} all-to-all(bf16[32,8,512]{2,1,0:T(8,128)(2,1)S(1)} %get-tuple-element.18), channel_id=1, replica_groups={{0,2,4,6,8,10,12,14,16,18,20,22,24,26,28,30,32,34,36,38,40,42,44,46,48,..., dimensions={0} | all-to-all | bytes 524288 | tf_op jit(solution)/shard_map/all_to_all | solution.py:311
  96.1 1.9 %collective-permute-start.11 = (bf16[32,8,512]{2,1,0:T(8,128)(2,1)S(1)}, bf16[32,8,512]{2,1,0:T(8,128)(2,1)S(1)}, u32[]{:S(2)}, u32[]{:S(2)}) collective-permute-start(bf16[32,8,512]{2,1,0:T(8,128)(2,1)S(1)} %all_to_all.15.mine_ref), channel_id=1, source_target_pairs={{0,1},{1,0},{2,3},{3,2},{4,5},{5,4},{6,7},{7,6},{8,9},{9,8},{10,11... | collective-permute-start | bytes 786440 | tf_op jit(solution)/shard_map/ppermute | solution.py:327
  98.0 4.5 %all-to-all-start.1 = ((bf16[32,8,512]{2,1,0:T(8,128)(2,1)}), bf16[32,8,512]{2,1,0:T(8,128)(2,1)S(1)}, u32[]{:S(2)}, u32[]{:S(2)}) async-start(bf16[32,8,512]{2,1,0:T(8,128)(2,1)} %copy-done.2), calls=%async_computation.1 | async-start | bytes 524288 | tf_op jit(solution)/shard_map/all_to_all | solution.py:311
  102.5 6.3 %first_work.1 = (bf16[2,512,512]{2,1,0:T(8,128)(2,1)S(1)}, bf16[32,8,512]{2,1,0:T(8,128)(2,1)}) custom-call(s32[1]{0:T(128)} %bitcast.1.core_ref, bf16[32,8,512]{2,1,0:T(8,128)(2,1)S(1)} %all_to_all.15.mine_ref, bf16[32,8,512]{2,1,0:T(8,128)(2,1)S(1)} %collective-permute-done.11.other_ref), custom_call_target="tpu_custom_call" | custom-call | flops 3221225472 | bytes 2097152 | tf_op jit(solution)/shard_map/first_work/pallas_call | solution.py:202
  108.8 6.6 %all-to-all-done.1.mine_ref = bf16[32,8,512]{2,1,0:T(8,128)(2,1)S(1)} async-done(((bf16[32,8,512]{2,1,0:T(8,128)(2,1)}), bf16[32,8,512]{2,1,0:T(8,128)(2,1)S(1)}, u32[]{:S(2)}, u32[]{:S(2)}) %all-to-all-start.1) | async-done | bytes 262176 | tf_op jit(solution)/shard_map/all_to_all | solution.py:311
  115.4 1.9 %collective-permute-start.12 = (bf16[32,8,512]{2,1,0:T(8,128)(2,1)S(1)}, bf16[32,8,512]{2,1,0:T(8,128)(2,1)S(1)}, u32[]{:S(2)}, u32[]{:S(2)}) collective-permute-start(bf16[32,8,512]{2,1,0:T(8,128)(2,1)S(1)} %all-to-all-done.1.mine_ref), channel_id=1, source_target_pairs={{0,1},{1,0},{2,3},{3,2},{4,5},{5,4},{6,7},{7,6},{8,9},{9,8},{10,11... | collective-permute-start | bytes 786440 | tf_op jit(solution)/shard_map/ppermute | solution.py:331
  117.3 4.6 %all-to-all-start.2 = ((bf16[32,8,512]{2,1,0:T(8,128)(2,1)}), bf16[32,8,512]{2,1,0:T(8,128)(2,1)S(1)}, u32[]{:S(2)}, u32[]{:S(2)}) async-start(bf16[32,8,512]{2,1,0:T(8,128)(2,1)} %get-tuple-element.23), calls=%async_computation.2 | async-start | bytes 524288 | tf_op jit(solution)/shard_map/all_to_all | solution.py:311
  126.9 8.0 %all-to-all-done.2.x_ref = bf16[32,8,512]{2,1,0:T(8,128)(2,1)S(1)} async-done(((bf16[32,8,512]{2,1,0:T(8,128)(2,1)}), bf16[32,8,512]{2,1,0:T(8,128)(2,1)S(1)}, u32[]{:S(2)}, u32[]{:S(2)}) %all-to-all-start.2) | async-done | bytes 262176 | tf_op jit(solution)/shard_map/all_to_all | solution.py:311
  (31 shorter events, 13.9 us)
Async XLA Ops:
  0.6 1.9 %copy-start = (bf16[1,12,8,16,1024]{4,3,2,1,0:T(8,128)(2,1)S(1)}, bf16[1,12,8,16,1024]{4,3,2,1,0:T(8,128)(2,1)}, u32[]{:S(2)}) copy-start(bf16[1,12,8,16,1024]{4,3,2,1,0:T(8,128)(2,1)} %param.2) | copy-start | bytes 9437188
  2.6 20.9 %collective-permute-start = (bf16[8,16,1024]{2,1,0:T(8,128)(2,1)S(1)}, bf16[8,16,1024]{2,1,0:T(8,128)(2,1)S(1)}, u32[]{:S(2)}, u32[]{:S(2)}) collective-permute-start(bf16[8,16,1024]{2,1,0:T(8,128)(2,1)S(1)} %get-tuple-element.16), channel_id=1, source_target_pairs={{0,64},{64,128},{128,192},{192,256},{256,320},{320,384},{384,448},... | collective-permute-start | bytes 786440 | tf_op jit(solution)/shard_map/ppermute | solution.py:294
  6.9 18.6 %collective-permute-start.6 = (bf16[8,16,1024]{2,1,0:T(8,128)(2,1)S(1)}, bf16[8,16,1024]{2,1,0:T(8,128)(2,1)S(1)}, u32[]{:S(2)}, u32[]{:S(2)}) collective-permute-start(bf16[8,16,1024]{2,1,0:T(8,128)(2,1)S(1)} %get-tuple-element.17), channel_id=1, source_target_pairs={{0,704},{64,0},{128,64},{192,128},{256,192},{320,256},{384,320},{4... | collective-permute-start | bytes 786440 | tf_op jit(solution)/shard_map/ppermute | solution.py:298
  23.5 10.6 %collective-permute-start.1 = (bf16[8,16,1024]{2,1,0:T(8,128)(2,1)S(1)}, bf16[8,16,1024]{2,1,0:T(8,128)(2,1)S(1)}, u32[]{:S(2)}, u32[]{:S(2)}) collective-permute-start(bf16[8,16,1024]{2,1,0:T(8,128)(2,1)S(1)} %added.9), channel_id=1, source_target_pairs={{0,64},{64,128},{128,192},{192,256},{256,320},{320,384},{384,448},... | collective-permute-start | bytes 786440 | tf_op jit(solution)/shard_map/ppermute | solution.py:294
  25.5 10.6 %collective-permute-start.7 = (bf16[8,16,1024]{2,1,0:T(8,128)(2,1)S(1)}, bf16[8,16,1024]{2,1,0:T(8,128)(2,1)S(1)}, u32[]{:S(2)}, u32[]{:S(2)}) collective-permute-start(bf16[8,16,1024]{2,1,0:T(8,128)(2,1)S(1)} %added.14), channel_id=1, source_target_pairs={{0,704},{64,0},{128,64},{192,128},{256,192},{320,256},{384,320},{4... | collective-permute-start | bytes 786440 | tf_op jit(solution)/shard_map/ppermute | solution.py:298
  34.2 9.7 %collective-permute-start.2 = (bf16[8,16,1024]{2,1,0:T(8,128)(2,1)S(1)}, bf16[8,16,1024]{2,1,0:T(8,128)(2,1)S(1)}, u32[]{:S(2)}, u32[]{:S(2)}) collective-permute-start(bf16[8,16,1024]{2,1,0:T(8,128)(2,1)S(1)} %added.10), channel_id=1, source_target_pairs={{0,64},{64,128},{128,192},{192,256},{256,320},{320,384},{384,448},... | collective-permute-start | bytes 786440 | tf_op jit(solution)/shard_map/ppermute | solution.py:294
  36.2 9.7 %collective-permute-start.8 = (bf16[8,16,1024]{2,1,0:T(8,128)(2,1)S(1)}, bf16[8,16,1024]{2,1,0:T(8,128)(2,1)S(1)}, u32[]{:S(2)}, u32[]{:S(2)}) collective-permute-start(bf16[8,16,1024]{2,1,0:T(8,128)(2,1)S(1)} %added.15), channel_id=1, source_target_pairs={{0,704},{64,0},{128,64},{192,128},{256,192},{320,256},{384,320},{4... | collective-permute-start | bytes 786440 | tf_op jit(solution)/shard_map/ppermute | solution.py:298
  43.9 9.5 %collective-permute-start.3 = (bf16[8,16,1024]{2,1,0:T(8,128)(2,1)S(1)}, bf16[8,16,1024]{2,1,0:T(8,128)(2,1)S(1)}, u32[]{:S(2)}, u32[]{:S(2)}) collective-permute-start(bf16[8,16,1024]{2,1,0:T(8,128)(2,1)S(1)} %added.11), channel_id=1, source_target_pairs={{0,64},{64,128},{128,192},{192,256},{256,320},{320,384},{384,448},... | collective-permute-start | bytes 786440 | tf_op jit(solution)/shard_map/ppermute | solution.py:294
  46.0 9.7 %collective-permute-start.9 = (bf16[8,16,1024]{2,1,0:T(8,128)(2,1)S(1)}, bf16[8,16,1024]{2,1,0:T(8,128)(2,1)S(1)}, u32[]{:S(2)}, u32[]{:S(2)}) collective-permute-start(bf16[8,16,1024]{2,1,0:T(8,128)(2,1)S(1)} %added.16), channel_id=1, source_target_pairs={{0,704},{64,0},{128,64},{192,128},{256,192},{320,256},{384,320},{4... | collective-permute-start | bytes 786440 | tf_op jit(solution)/shard_map/ppermute | solution.py:298
  53.5 20.3 %copy-start.1 = (bf16[1,12,8,16,1024]{4,3,2,1,0:T(8,128)(2,1)S(1)}, bf16[1,12,8,16,1024]{4,3,2,1,0:T(8,128)(2,1)}, u32[]{:S(2)}) copy-start(bf16[1,12,8,16,1024]{4,3,2,1,0:T(8,128)(2,1)} %param.2) | copy-start | bytes 9437188
  53.5 9.7 %collective-permute-start.4 = (bf16[8,16,1024]{2,1,0:T(8,128)(2,1)S(1)}, bf16[8,16,1024]{2,1,0:T(8,128)(2,1)S(1)}, u32[]{:S(2)}, u32[]{:S(2)}) collective-permute-start(bf16[8,16,1024]{2,1,0:T(8,128)(2,1)S(1)} %added.12), channel_id=1, source_target_pairs={{0,64},{64,128},{128,192},{192,256},{256,320},{320,384},{384,448},... | collective-permute-start | bytes 786440 | tf_op jit(solution)/shard_map/ppermute | solution.py:294
  56.5 11.8 %collective-permute-start.10 = (bf16[8,16,1024]{2,1,0:T(8,128)(2,1)}, bf16[8,16,1024]{2,1,0:T(8,128)(2,1)S(1)}, u32[]{:S(2)}, u32[]{:S(2)}) collective-permute-start(bf16[8,16,1024]{2,1,0:T(8,128)(2,1)} %added.17), channel_id=1, source_target_pairs={{0,704},{64,0},{128,64},{192,128},{256,192},{320,256},{384,320},{4... | collective-permute-start | bytes 786440 | tf_op jit(solution)/shard_map/ppermute | solution.py:298
  64.0 9.8 %collective-permute-start.5 = (bf16[8,16,1024]{2,1,0:T(8,128)(2,1)}, bf16[8,16,1024]{2,1,0:T(8,128)(2,1)}, u32[]{:S(2)}, u32[]{:S(2)}) collective-permute-start(bf16[8,16,1024]{2,1,0:T(8,128)(2,1)} %added.13), channel_id=1, source_target_pairs={{0,64},{64,128},{128,192},{192,256},{256,320},{320,384},{384,448},... | collective-permute-start | bytes 786440 | tf_op jit(solution)/shard_map/ppermute | solution.py:294
  75.1 21.0 %copy-start.2 = (bf16[32,8,512]{2,1,0:T(8,128)(2,1)}, bf16[32,8,512]{2,1,0:T(8,128)(2,1)S(1)}, u32[]{:S(2)}) copy-start(bf16[32,8,512]{2,1,0:T(8,128)(2,1)S(1)} %get-tuple-element.22) | copy-start | bytes 786436
  96.1 6.4 %collective-permute-start.11 = (bf16[32,8,512]{2,1,0:T(8,128)(2,1)S(1)}, bf16[32,8,512]{2,1,0:T(8,128)(2,1)S(1)}, u32[]{:S(2)}, u32[]{:S(2)}) collective-permute-start(bf16[32,8,512]{2,1,0:T(8,128)(2,1)S(1)} %all_to_all.15.mine_ref), channel_id=1, source_target_pairs={{0,1},{1,0},{2,3},{3,2},{4,5},{5,4},{6,7},{7,6},{8,9},{9,8},{10,11... | collective-permute-start | bytes 786440 | tf_op jit(solution)/shard_map/ppermute | solution.py:327
  98.0 17.4 %all-to-all-start.1 = ((bf16[32,8,512]{2,1,0:T(8,128)(2,1)}), bf16[32,8,512]{2,1,0:T(8,128)(2,1)S(1)}, u32[]{:S(2)}, u32[]{:S(2)}) async-start(bf16[32,8,512]{2,1,0:T(8,128)(2,1)} %copy-done.2), calls=%async_computation.1 | async-start | bytes 524288 | tf_op jit(solution)/shard_map/all_to_all | solution.py:311
  115.4 10.4 %collective-permute-start.12 = (bf16[32,8,512]{2,1,0:T(8,128)(2,1)S(1)}, bf16[32,8,512]{2,1,0:T(8,128)(2,1)S(1)}, u32[]{:S(2)}, u32[]{:S(2)}) collective-permute-start(bf16[32,8,512]{2,1,0:T(8,128)(2,1)S(1)} %all-to-all-done.1.mine_ref), channel_id=1, source_target_pairs={{0,1},{1,0},{2,3},{3,2},{4,5},{5,4},{6,7},{7,6},{8,9},{9,8},{10,11... | collective-permute-start | bytes 786440 | tf_op jit(solution)/shard_map/ppermute | solution.py:331
  117.3 17.5 %all-to-all-start.2 = ((bf16[32,8,512]{2,1,0:T(8,128)(2,1)}), bf16[32,8,512]{2,1,0:T(8,128)(2,1)S(1)}, u32[]{:S(2)}, u32[]{:S(2)}) async-start(bf16[32,8,512]{2,1,0:T(8,128)(2,1)} %get-tuple-element.23), calls=%async_computation.2 | async-start | bytes 524288 | tf_op jit(solution)/shard_map/all_to_all | solution.py:311

commit v5 on v4

--- a/solution.py
+++ b/solution.py
@@ -71,7 +71,7 @@
     chips = first.shape[0]
 
     def kernel(
-        here_ref, first_ref, second_ref, below_ref, above_ref, parts_ref, one_ref, two_ref, wide, pieces
+        here_ref, first_ref, second_ref, below_ref, above_ref, parts_ref, out_ref, wide, pieces
     ):
         for k in range(cols // LANES):
             at = (slice(None), slice(None), slice(k * LANES, (k + 1) * LANES))
@@ -86,17 +86,17 @@
         pieces[group] = jnp.zeros((rows, BLK), BF16)
 
         def place(p, carry):
-            one_ref[p] = pieces[first_ref[p]]
-            two_ref[p] = pieces[second_ref[p]]
+            out_ref[p, 0] = pieces[first_ref[p]]
+            out_ref[p, 1] = pieces[second_ref[p]]
             return carry
 
         lax.fori_loop(0, chips, place, 0, unroll=4)
 
     return pl.pallas_call(
         kernel,
-        out_shape=[jax.ShapeDtypeStruct((chips, rows, BLK), BF16)] * 2,
+        out_shape=jax.ShapeDtypeStruct((chips, 2, rows, BLK), BF16),
         in_specs=[smem(), smem(), smem(), vmem(), vmem(), vmem()],
-        out_specs=[vmem(), vmem()],
+        out_specs=vmem(),
         scratch_shapes=[
             pltpu.VMEM((cols // LANES, rows * row_blocks, LANES), F32),
             pltpu.VMEM((group + 1, rows, BLK), BF16),
@@ -164,9 +164,9 @@
     return root
 
 
-def whole_block(core_ref, mine_ref, other_ref, halves):
-    halves[:, core_ref[0]] = mine_ref[...].astype(F32)
-    halves[:, 1 - core_ref[0]] = other_ref[...].astype(F32)
+def whole_block(core_ref, mine_ref, other_ref, which, halves):
+    halves[:, core_ref[0]] = mine_ref[:, which].astype(F32)
+    halves[:, 1 - core_ref[0]] = other_ref[:, which].astype(F32)
     return halves[...].reshape(BLK, BLK)
 
 
@@ -184,10 +184,10 @@
 
 
 def first_work(core, mine, other, replicas):
-    chips, rows, _ = mine.shape
+    chips, _, rows, _ = mine.shape
 
     def kernel(core_ref, mine_ref, other_ref, roots_ref, update_ref, halves):
-        wide = whole_block(core_ref, mine_ref, other_ref, halves)
+        wide = whole_block(core_ref, mine_ref, other_ref, 0, halves)
         x, total, left, right = both_roots(wide, replicas)
         roots_ref[0] = left
         roots_ref[1] = right
@@ -215,7 +215,7 @@
 
 
 def second_work(mode, core, mine, other, roots, replicas):
-    chips, rows, _ = mine.shape
+    chips, _, rows, _ = mine.shape
 
     def kernel(mode_ref, core_ref, mine_ref, other_ref, roots_ref, out_ref, halves):
         @pl.when(mode_ref[0] == 0)
@@ -228,7 +228,7 @@
 
         @pl.when(mode_ref[0] == 2)
         def _():
-            wide = whole_block(core_ref, mine_ref, other_ref, halves)
+            wide = whole_block(core_ref, mine_ref, other_ref, 1, halves)
             _, _, left, right = both_roots(wide, replicas)
             out_ref[0] = left
             out_ref[1] = right
@@ -320,16 +320,11 @@
     here = lax.axis_index("dp")[None]
     terms = ring_terms(here, grads[0], "dp")
     _, row_blocks, cols = terms[0].shape
-    one, two = outgoing_pieces(here, first, second, terms, grads[0])
-    one_mine = exchanged(one)
-    one_mine, two = lax.optimization_barrier((one_mine, two))
-    two_mine = exchanged(two)
-    one_other = lax.ppermute(one_mine, "fsdp", across)
-    roots, update = first_work(core, one_mine, one_other, replicas)
-    update, two_mine = lax.optimization_barrier((update, two_mine))
+    mine = exchanged(outgoing_pieces(here, first, second, terms, grads[0]))
+    other = lax.ppermute(mine, "fsdp", across)
+    roots, update = first_work(core, mine, other, replicas)
     returned = exchanged(update)
-    two_other = lax.ppermute(two_mine, "fsdp", across)
-    roots = second_work(mode, core, two_mine, two_other, roots, replicas)
+    roots = second_work(mode, core, mine, other, roots, replicas)
     result = incoming_update(first, returned, row_blocks, cols // BLK)
     return result[None], roots[None, None]
 

time: 137 us -> 128 us (0.934)
  starting transfers between devices: 59.8 us -> 53.5 us
  waiting for transfers between devices: 34.4 us -> 29.2 us
  blocking collectives: 20.9 us -> 23.6 us
    all_to_all x2 -> x1, waiting for transfers between devices: 14.6 us -> 7.56 us  [exchanged(): lax.all_to_all(x, 'fsdp', split_axis=0, concat_axis=0, axis_index_groups=...]
    all_to_all x2 -> x1, starting transfers between devices: 9.1 us -> 4.67 us  [exchanged(): lax.all_to_all(x, 'fsdp', split_axis=0, concat_axis=0, axis_index_groups=...]
    all_to_all x1, blocking collectives: 20.9 us -> 23.6 us  [exchanged(): lax.all_to_all(x, 'fsdp', split_axis=0, concat_axis=0, axis_index_groups=...]
    ppermute x2 -> x1, starting transfers between devices: 3.82 us -> 1.91 us  [local(): other = lax.ppermute(mine, 'fsdp', across)]
    ppermute x2 -> x1, waiting for transfers between devices: 0.01 us -> 1.86 us  [local(): other = lax.ppermute(mine, 'fsdp', across)]
  transfers between devices with their start and end apart: 15 -> 13, of which waited for: 8 -> 8; matrix products, arithmetic and copies ran while one was open for 2% -> 2% of each run, Pallas kernels for 8% -> 4%
where the time goes in v5:
time: 128 us
  starting transfers between devices  53.5 us (42%)
  waiting for transfers between devices  29.2 us (23%)
  blocking collectives  23.6 us (18%)
  Pallas kernels  14 us (11%)
  local copies, waits for them, and re-layouts  4.52 us (4%)
  between operations  2.89 us (2%)
    ppermute x5, starting transfers between devices, ring_terms(): above = lax.ppermute(above, axis, lowering)  32.7 us
    all_to_all x1, blocking collectives, exchanged(): lax.all_to_all(x, 'fsdp', split_axis=0, concat_axis=0, axis_index_groups=...  23.6 us
    ppermute x6, waiting for transfers between devices, ring_terms(): below = lax.ppermute(below, axis, raising)  19.7 us
    ppermute x6, starting transfers between devices, ring_terms(): below = lax.ppermute(below, axis, raising)  14.1 us
    all_to_all x1, waiting for transfers between devices, exchanged(): lax.all_to_all(x, 'fsdp', split_axis=0, concat_axis=0, axis_index_groups=...  7.56 us
    pallas_call x1, Pallas kernels, first_work(): pl.pallas_call(kernel, out_shape=(jax.ShapeDtypeStruct((2, BLK, BLK), BF1...  6.27 us
    all_to_all x1, starting transfers between devices, exchanged(): lax.all_to_all(x, 'fsdp', split_axis=0, concat_axis=0, axis_index_groups=...  4.67 us
  transfers between devices with their start and end apart: 13, of which 8 were waited for; matrix products, arithmetic and copies ran while one was open for 2% of the time, Pallas kernels for 4%

profile of v5, /device:TPU:8, one launch (start us, length us, event | category | flops | bytes accessed | tf_op | source)
XLA Modules:
  0.0 127.6 jit_solution(16636858153962502393)
XLA Ops:
  0.7 1.9 %copy-done = bf16[1,12,8,16,1024]{4,3,2,1,0:T(8,128)(2,1)S(1)} copy-done((bf16[1,12,8,16,1024]{4,3,2,1,0:T(8,128)(2,1)S(1)}, bf16[1,12,8,16,1024]{4,3,2,1,0:T(8,128)(2,1)}, u32[]{:S(2)}) %copy-start) | copy-done | bytes 3145752
  2.6 4.3 %collective-permute-start = (bf16[8,16,1024]{2,1,0:T(8,128)(2,1)S(1)}, bf16[8,16,1024]{2,1,0:T(8,128)(2,1)S(1)}, u32[]{:S(2)}, u32[]{:S(2)}) collective-permute-start(bf16[8,16,1024]{2,1,0:T(8,128)(2,1)S(1)} %get-tuple-element.10), channel_id=1, source_target_pairs={{0,64},{64,128},{128,192},{192,256},{256,320},{320,384},{384,448},... | collective-permute-start | bytes 786440 | tf_op jit(solution)/shard_map/ppermute | solution.py:294
  6.9 12.2 %collective-permute-start.6 = (bf16[8,16,1024]{2,1,0:T(8,128)(2,1)S(1)}, bf16[8,16,1024]{2,1,0:T(8,128)(2,1)S(1)}, u32[]{:S(2)}, u32[]{:S(2)}) collective-permute-start(bf16[8,16,1024]{2,1,0:T(8,128)(2,1)S(1)} %get-tuple-element.11), channel_id=1, source_target_pairs={{0,704},{64,0},{128,64},{192,128},{256,192},{320,256},{384,320},{4... | collective-permute-start | bytes 786440 | tf_op jit(solution)/shard_map/ppermute | solution.py:298
  19.1 4.4 %collective-permute-done.total_ref = bf16[8,16,1024]{2,1,0:T(8,128)(2,1)S(1)} collective-permute-done((bf16[8,16,1024]{2,1,0:T(8,128)(2,1)S(1)}, bf16[8,16,1024]{2,1,0:T(8,128)(2,1)S(1)}, u32[]{:S(2)}, u32[]{:S(2)}) %collective-permute-start) | collective-permute-done | bytes 262176 | tf_op jit(solution)/shard_map/ppermute | solution.py:294
  23.5 1.9 %collective-permute-start.1 = (bf16[8,16,1024]{2,1,0:T(8,128)(2,1)S(1)}, bf16[8,16,1024]{2,1,0:T(8,128)(2,1)S(1)}, u32[]{:S(2)}, u32[]{:S(2)}) collective-permute-start(bf16[8,16,1024]{2,1,0:T(8,128)(2,1)S(1)} %added.9), channel_id=1, source_target_pairs={{0,64},{64,128},{128,192},{192,256},{256,320},{320,384},{384,448},... | collective-permute-start | bytes 786440 | tf_op jit(solution)/shard_map/ppermute | solution.py:294
  25.5 5.1 %collective-permute-start.7 = (bf16[8,16,1024]{2,1,0:T(8,128)(2,1)S(1)}, bf16[8,16,1024]{2,1,0:T(8,128)(2,1)S(1)}, u32[]{:S(2)}, u32[]{:S(2)}) collective-permute-start(bf16[8,16,1024]{2,1,0:T(8,128)(2,1)S(1)} %added.14), channel_id=1, source_target_pairs={{0,704},{64,0},{128,64},{192,128},{256,192},{320,256},{384,320},{4... | collective-permute-start | bytes 786440 | tf_op jit(solution)/shard_map/ppermute | solution.py:298
  30.7 3.4 %collective-permute-done.1.total_ref = bf16[8,16,1024]{2,1,0:T(8,128)(2,1)S(1)} collective-permute-done((bf16[8,16,1024]{2,1,0:T(8,128)(2,1)S(1)}, bf16[8,16,1024]{2,1,0:T(8,128)(2,1)S(1)}, u32[]{:S(2)}, u32[]{:S(2)}) %collective-permute-start.1) | collective-permute-done | bytes 262176 | tf_op jit(solution)/shard_map/ppermute | solution.py:294
  34.2 1.9 %collective-permute-start.2 = (bf16[8,16,1024]{2,1,0:T(8,128)(2,1)S(1)}, bf16[8,16,1024]{2,1,0:T(8,128)(2,1)S(1)}, u32[]{:S(2)}, u32[]{:S(2)}) collective-permute-start(bf16[8,16,1024]{2,1,0:T(8,128)(2,1)S(1)} %added.10), channel_id=1, source_target_pairs={{0,64},{64,128},{128,192},{192,256},{256,320},{320,384},{384,448},... | collective-permute-start | bytes 786440 | tf_op jit(solution)/shard_map/ppermute | solution.py:294
  36.2 5.1 %collective-permute-start.8 = (bf16[8,16,1024]{2,1,0:T(8,128)(2,1)S(1)}, bf16[8,16,1024]{2,1,0:T(8,128)(2,1)S(1)}, u32[]{:S(2)}, u32[]{:S(2)}) collective-permute-start(bf16[8,16,1024]{2,1,0:T(8,128)(2,1)S(1)} %added.15), channel_id=1, source_target_pairs={{0,704},{64,0},{128,64},{192,128},{256,192},{320,256},{384,320},{4... | collective-permute-start | bytes 786440 | tf_op jit(solution)/shard_map/ppermute | solution.py:298
  41.4 2.5 %collective-permute-done.2.total_ref = bf16[8,16,1024]{2,1,0:T(8,128)(2,1)S(1)} collective-permute-done((bf16[8,16,1024]{2,1,0:T(8,128)(2,1)S(1)}, bf16[8,16,1024]{2,1,0:T(8,128)(2,1)S(1)}, u32[]{:S(2)}, u32[]{:S(2)}) %collective-permute-start.2) | collective-permute-done | bytes 262176 | tf_op jit(solution)/shard_map/ppermute | solution.py:294
  43.9 1.9 %collective-permute-start.3 = (bf16[8,16,1024]{2,1,0:T(8,128)(2,1)S(1)}, bf16[8,16,1024]{2,1,0:T(8,128)(2,1)S(1)}, u32[]{:S(2)}, u32[]{:S(2)}) collective-permute-start(bf16[8,16,1024]{2,1,0:T(8,128)(2,1)S(1)} %added.11), channel_id=1, source_target_pairs={{0,64},{64,128},{128,192},{192,256},{256,320},{320,384},{384,448},... | collective-permute-start | bytes 786440 | tf_op jit(solution)/shard_map/ppermute | solution.py:294
  46.0 5.1 %collective-permute-start.9 = (bf16[8,16,1024]{2,1,0:T(8,128)(2,1)S(1)}, bf16[8,16,1024]{2,1,0:T(8,128)(2,1)S(1)}, u32[]{:S(2)}, u32[]{:S(2)}) collective-permute-start(bf16[8,16,1024]{2,1,0:T(8,128)(2,1)S(1)} %added.16), channel_id=1, source_target_pairs={{0,704},{64,0},{128,64},{192,128},{256,192},{320,256},{384,320},{4... | collective-permute-start | bytes 786440 | tf_op jit(solution)/shard_map/ppermute | solution.py:298
  51.1 2.3 %collective-permute-done.3.total_ref = bf16[8,16,1024]{2,1,0:T(8,128)(2,1)S(1)} collective-permute-done((bf16[8,16,1024]{2,1,0:T(8,128)(2,1)S(1)}, bf16[8,16,1024]{2,1,0:T(8,128)(2,1)S(1)}, u32[]{:S(2)}, u32[]{:S(2)}) %collective-permute-start.3) | collective-permute-done | bytes 262176 | tf_op jit(solution)/shard_map/ppermute | solution.py:294
  53.5 2.2 %collective-permute-start.4 = (bf16[8,16,1024]{2,1,0:T(8,128)(2,1)S(1)}, bf16[8,16,1024]{2,1,0:T(8,128)(2,1)S(1)}, u32[]{:S(2)}, u32[]{:S(2)}) collective-permute-start(bf16[8,16,1024]{2,1,0:T(8,128)(2,1)S(1)} %added.12), channel_id=1, source_target_pairs={{0,64},{64,128},{128,192},{192,256},{256,320},{320,384},{384,448},... | collective-permute-start | bytes 786440 | tf_op jit(solution)/shard_map/ppermute | solution.py:294
  56.5 5.1 %collective-permute-start.10 = (bf16[8,16,1024]{2,1,0:T(8,128)(2,1)}, bf16[8,16,1024]{2,1,0:T(8,128)(2,1)S(1)}, u32[]{:S(2)}, u32[]{:S(2)}) collective-permute-start(bf16[8,16,1024]{2,1,0:T(8,128)(2,1)} %added.17), channel_id=1, source_target_pairs={{0,704},{64,0},{128,64},{192,128},{256,192},{320,256},{384,320},{4... | collective-permute-start | bytes 786440 | tf_op jit(solution)/shard_map/ppermute | solution.py:298
  64.0 1.9 %collective-permute-start.5 = (bf16[8,16,1024]{2,1,0:T(8,128)(2,1)}, bf16[8,16,1024]{2,1,0:T(8,128)(2,1)}, u32[]{:S(2)}, u32[]{:S(2)}) collective-permute-start(bf16[8,16,1024]{2,1,0:T(8,128)(2,1)} %added.13), channel_id=1, source_target_pairs={{0,64},{64,128},{128,192},{192,256},{256,320},{320,384},{384,448},... | collective-permute-start | bytes 786440 | tf_op jit(solution)/shard_map/ppermute | solution.py:294
  66.6 1.7 %assigned.1 = (s32[32]{0:T(128)S(1)}, s32[32]{0:T(128)S(1)}) custom-call(s32[64]{0:T(128)S(1)} %dynamic-slice_bitcast_fusion.table_ref), custom_call_target="tpu_custom_call" | custom-call | bytes 1024 | tf_op jit(solution)/shard_map/assigned/pallas_call | solution.py:55
  68.3 5.5 %collective-permute-done.5.below_ref = bf16[8,16,1024]{2,1,0:T(8,128)(2,1)} collective-permute-done((bf16[8,16,1024]{2,1,0:T(8,128)(2,1)}, bf16[8,16,1024]{2,1,0:T(8,128)(2,1)}, u32[]{:S(2)}, u32[]{:S(2)}) %collective-permute-start.5) | collective-permute-done | bytes 262176 | tf_op jit(solution)/shard_map/ppermute | solution.py:294
  75.1 23.6 %all_to_all.10.mine_ref = bf16[32,2,8,512]{3,2,1,0:T(8,128)(2,1)S(1)} all-to-all(bf16[32,2,8,512]{3,2,1,0:T(8,128)(2,1)S(1)} %outgoing.1), channel_id=1, replica_groups={{0,2,4,6,8,10,12,14,16,18,20,22,24,26,28,30,32,34,36,38,40,42,44,46,48,..., dimensions={0} | all-to-all | bytes 1048576 | tf_op jit(solution)/shard_map/all_to_all | solution.py:311
  98.7 1.9 %collective-permute-start.11 = (bf16[32,2,8,512]{3,2,1,0:T(8,128)(2,1)S(1)}, bf16[32,2,8,512]{3,2,1,0:T(8,128)(2,1)S(1)}, u32[]{:S(2)}, u32[]{:S(2)}) collective-permute-start(bf16[32,2,8,512]{3,2,1,0:T(8,128)(2,1)S(1)} %all_to_all.10.mine_ref), channel_id=1, source_target_pairs={{0,1},{1,0},{2,3},{3,2},{4,5},{5,4},{6,7},{7,6},{8,9},{9,8},{10,11... | collective-permute-start | bytes 1572872 | tf_op jit(solution)/shard_map/ppermute | solution.py:324
  100.6 1.9 %collective-permute-done.11.other_ref = bf16[32,2,8,512]{3,2,1,0:T(8,128)(2,1)S(1)} collective-permute-done((bf16[32,2,8,512]{3,2,1,0:T(8,128)(2,1)S(1)}, bf16[32,2,8,512]{3,2,1,0:T(8,128)(2,1)S(1)}, u32[]{:S(2)}, u32[]{:S(2)}) %collective-permute-start.11) | collective-permute-done | bytes 524320 | tf_op jit(solution)/shard_map/ppermute | solution.py:324
  102.5 6.3 %first_work.1 = (bf16[2,512,512]{2,1,0:T(8,128)(2,1)S(1)}, bf16[32,8,512]{2,1,0:T(8,128)(2,1)}) custom-call(s32[1]{0:T(128)} %bitcast.1.core_ref, bf16[32,2,8,512]{3,2,1,0:T(8,128)(2,1)S(1)} %all_to_all.10.mine_ref, bf16[32,2,8,512]{3,2,1,0:T(8,128)(2,1)S(1)} %collective-permute-done.11.other_ref), custom_call_target="tpu_custom_call" | custom-call | flops 3221225472 | bytes 2097152 | tf_op jit(solution)/shard_map/first_work/pallas_call | solution.py:202
  108.8 4.7 %all-to-all-start.1 = ((bf16[32,8,512]{2,1,0:T(8,128)(2,1)}), bf16[32,8,512]{2,1,0:T(8,128)(2,1)S(1)}, u32[]{:S(2)}, u32[]{:S(2)}) async-start(bf16[32,8,512]{2,1,0:T(8,128)(2,1)} %get-tuple-element.12), calls=%async_computation.1 | async-start | bytes 524288 | tf_op jit(solution)/shard_map/all_to_all | solution.py:311
  118.5 7.6 %all-to-all-done.1.x_ref = bf16[32,8,512]{2,1,0:T(8,128)(2,1)S(1)} async-done(((bf16[32,8,512]{2,1,0:T(8,128)(2,1)}), bf16[32,8,512]{2,1,0:T(8,128)(2,1)S(1)}, u32[]{:S(2)}, u32[]{:S(2)}) %all-to-all-start.1) | async-done | bytes 262176 | tf_op jit(solution)/shard_map/all_to_all | solution.py:311
  (25 shorter events, 10.3 us)
Async XLA Ops:
  0.6 1.9 %copy-start = (bf16[1,12,8,16,1024]{4,3,2,1,0:T(8,128)(2,1)S(1)}, bf16[1,12,8,16,1024]{4,3,2,1,0:T(8,128)(2,1)}, u32[]{:S(2)}) copy-start(bf16[1,12,8,16,1024]{4,3,2,1,0:T(8,128)(2,1)} %param.2) | copy-start | bytes 9437188
  2.6 20.9 %collective-permute-start = (bf16[8,16,1024]{2,1,0:T(8,128)(2,1)S(1)}, bf16[8,16,1024]{2,1,0:T(8,128)(2,1)S(1)}, u32[]{:S(2)}, u32[]{:S(2)}) collective-permute-start(bf16[8,16,1024]{2,1,0:T(8,128)(2,1)S(1)} %get-tuple-element.10), channel_id=1, source_target_pairs={{0,64},{64,128},{128,192},{192,256},{256,320},{320,384},{384,448},... | collective-permute-start | bytes 786440 | tf_op jit(solution)/shard_map/ppermute | solution.py:294
  6.9 18.6 %collective-permute-start.6 = (bf16[8,16,1024]{2,1,0:T(8,128)(2,1)S(1)}, bf16[8,16,1024]{2,1,0:T(8,128)(2,1)S(1)}, u32[]{:S(2)}, u32[]{:S(2)}) collective-permute-start(bf16[8,16,1024]{2,1,0:T(8,128)(2,1)S(1)} %get-tuple-element.11), channel_id=1, source_target_pairs={{0,704},{64,0},{128,64},{192,128},{256,192},{320,256},{384,320},{4... | collective-permute-start | bytes 786440 | tf_op jit(solution)/shard_map/ppermute | solution.py:298
  23.5 10.6 %collective-permute-start.1 = (bf16[8,16,1024]{2,1,0:T(8,128)(2,1)S(1)}, bf16[8,16,1024]{2,1,0:T(8,128)(2,1)S(1)}, u32[]{:S(2)}, u32[]{:S(2)}) collective-permute-start(bf16[8,16,1024]{2,1,0:T(8,128)(2,1)S(1)} %added.9), channel_id=1, source_target_pairs={{0,64},{64,128},{128,192},{192,256},{256,320},{320,384},{384,448},... | collective-permute-start | bytes 786440 | tf_op jit(solution)/shard_map/ppermute | solution.py:294
  25.5 10.6 %collective-permute-start.7 = (bf16[8,16,1024]{2,1,0:T(8,128)(2,1)S(1)}, bf16[8,16,1024]{2,1,0:T(8,128)(2,1)S(1)}, u32[]{:S(2)}, u32[]{:S(2)}) collective-permute-start(bf16[8,16,1024]{2,1,0:T(8,128)(2,1)S(1)} %added.14), channel_id=1, source_target_pairs={{0,704},{64,0},{128,64},{192,128},{256,192},{320,256},{384,320},{4... | collective-permute-start | bytes 786440 | tf_op jit(solution)/shard_map/ppermute | solution.py:298
  34.2 9.7 %collective-permute-start.2 = (bf16[8,16,1024]{2,1,0:T(8,128)(2,1)S(1)}, bf16[8,16,1024]{2,1,0:T(8,128)(2,1)S(1)}, u32[]{:S(2)}, u32[]{:S(2)}) collective-permute-start(bf16[8,16,1024]{2,1,0:T(8,128)(2,1)S(1)} %added.10), channel_id=1, source_target_pairs={{0,64},{64,128},{128,192},{192,256},{256,320},{320,384},{384,448},... | collective-permute-start | bytes 786440 | tf_op jit(solution)/shard_map/ppermute | solution.py:294
  36.2 9.7 %collective-permute-start.8 = (bf16[8,16,1024]{2,1,0:T(8,128)(2,1)S(1)}, bf16[8,16,1024]{2,1,0:T(8,128)(2,1)S(1)}, u32[]{:S(2)}, u32[]{:S(2)}) collective-permute-start(bf16[8,16,1024]{2,1,0:T(8,128)(2,1)S(1)} %added.15), channel_id=1, source_target_pairs={{0,704},{64,0},{128,64},{192,128},{256,192},{320,256},{384,320},{4... | collective-permute-start | bytes 786440 | tf_op jit(solution)/shard_map/ppermute | solution.py:298
  43.9 9.5 %collective-permute-start.3 = (bf16[8,16,1024]{2,1,0:T(8,128)(2,1)S(1)}, bf16[8,16,1024]{2,1,0:T(8,128)(2,1)S(1)}, u32[]{:S(2)}, u32[]{:S(2)}) collective-permute-start(bf16[8,16,1024]{2,1,0:T(8,128)(2,1)S(1)} %added.11), channel_id=1, source_target_pairs={{0,64},{64,128},{128,192},{192,256},{256,320},{320,384},{384,448},... | collective-permute-start | bytes 786440 | tf_op jit(solution)/shard_map/ppermute | solution.py:294
  46.0 9.7 %collective-permute-start.9 = (bf16[8,16,1024]{2,1,0:T(8,128)(2,1)S(1)}, bf16[8,16,1024]{2,1,0:T(8,128)(2,1)S(1)}, u32[]{:S(2)}, u32[]{:S(2)}) collective-permute-start(bf16[8,16,1024]{2,1,0:T(8,128)(2,1)S(1)} %added.16), channel_id=1, source_target_pairs={{0,704},{64,0},{128,64},{192,128},{256,192},{320,256},{384,320},{4... | collective-permute-start | bytes 786440 | tf_op jit(solution)/shard_map/ppermute | solution.py:298
  53.5 20.3 %copy-start.1 = (bf16[1,12,8,16,1024]{4,3,2,1,0:T(8,128)(2,1)S(1)}, bf16[1,12,8,16,1024]{4,3,2,1,0:T(8,128)(2,1)}, u32[]{:S(2)}) copy-start(bf16[1,12,8,16,1024]{4,3,2,1,0:T(8,128)(2,1)} %param.2) | copy-start | bytes 9437188
  53.5 9.7 %collective-permute-start.4 = (bf16[8,16,1024]{2,1,0:T(8,128)(2,1)S(1)}, bf16[8,16,1024]{2,1,0:T(8,128)(2,1)S(1)}, u32[]{:S(2)}, u32[]{:S(2)}) collective-permute-start(bf16[8,16,1024]{2,1,0:T(8,128)(2,1)S(1)} %added.12), channel_id=1, source_target_pairs={{0,64},{64,128},{128,192},{192,256},{256,320},{320,384},{384,448},... | collective-permute-start | bytes 786440 | tf_op jit(solution)/shard_map/ppermute | solution.py:294
  56.5 11.8 %collective-permute-start.10 = (bf16[8,16,1024]{2,1,0:T(8,128)(2,1)}, bf16[8,16,1024]{2,1,0:T(8,128)(2,1)S(1)}, u32[]{:S(2)}, u32[]{:S(2)}) collective-permute-start(bf16[8,16,1024]{2,1,0:T(8,128)(2,1)} %added.17), channel_id=1, source_target_pairs={{0,704},{64,0},{128,64},{192,128},{256,192},{320,256},{384,320},{4... | collective-permute-start | bytes 786440 | tf_op jit(solution)/shard_map/ppermute | solution.py:298
  64.0 9.8 %collective-permute-start.5 = (bf16[8,16,1024]{2,1,0:T(8,128)(2,1)}, bf16[8,16,1024]{2,1,0:T(8,128)(2,1)}, u32[]{:S(2)}, u32[]{:S(2)}) collective-permute-start(bf16[8,16,1024]{2,1,0:T(8,128)(2,1)} %added.13), channel_id=1, source_target_pairs={{0,64},{64,128},{128,192},{192,256},{256,320},{320,384},{384,448},... | collective-permute-start | bytes 786440 | tf_op jit(solution)/shard_map/ppermute | solution.py:294
  98.7 3.8 %collective-permute-start.11 = (bf16[32,2,8,512]{3,2,1,0:T(8,128)(2,1)S(1)}, bf16[32,2,8,512]{3,2,1,0:T(8,128)(2,1)S(1)}, u32[]{:S(2)}, u32[]{:S(2)}) collective-permute-start(bf16[32,2,8,512]{3,2,1,0:T(8,128)(2,1)S(1)} %all_to_all.10.mine_ref), channel_id=1, source_target_pairs={{0,1},{1,0},{2,3},{3,2},{4,5},{5,4},{6,7},{7,6},{8,9},{9,8},{10,11... | collective-permute-start | bytes 1572872 | tf_op jit(solution)/shard_map/ppermute | solution.py:324
  108.8 17.3 %all-to-all-start.1 = ((bf16[32,8,512]{2,1,0:T(8,128)(2,1)}), bf16[32,8,512]{2,1,0:T(8,128)(2,1)S(1)}, u32[]{:S(2)}, u32[]{:S(2)}) async-start(bf16[32,8,512]{2,1,0:T(8,128)(2,1)} %get-tuple-element.12), calls=%async_computation.1 | async-start | bytes 524288 | tf_op jit(solution)/shard_map/all_to_all | solution.py:311

commit v6 on v5

v6 whole, which is shorter than its diff:
```python
import jax
import jax.numpy as jnp
from jax import lax
from jax.experimental import pallas as pl
from jax.experimental.pallas import tpu as pltpu
from jax.sharding import PartitionSpec as P

BLK = 512
LANES = 128
PER_BLK = BLK // LANES
STRIP = 64
ITERS = 2
DAMPING = 0.1
F32 = jnp.float32
BF16 = jnp.bfloat16
VMEM_LIMIT = 24 * 1024 * 1024
PICK_LIMIT = 61 * 1024 * 1024
STAGE_LIMIT = 50 * 1024 * 1024


def cost(flops, nbytes):
    return pl.CostEstimate(flops=flops, bytes_accessed=nbytes, transcendentals=0)


def vmem():
    return pl.BlockSpec(memory_space=pltpu.VMEM)


def smem():
    return pl.BlockSpec(memory_space=pltpu.SMEM)


def params(limit=VMEM_LIMIT):
    return pltpu.CompilerParams(vmem_limit_bytes=limit)


def assigned(here, slot, slot_block):
    chips = slot_block.shape[1] // 2

    def kernel(here_ref, slot_ref, table_ref, first_ref, second_ref, mode_ref, spare):
        row = here_ref[0]

        def collect(p, count):
            low, high = table_ref[row, 2 * p], table_ref[row, 2 * p + 1]
            two = jnp.logical_and(low < chips, high < chips)
            first_ref[p] = jnp.minimum(jnp.where(low < chips, low, high), chips)
            second_ref[p] = jnp.where(two, high, chips)
            spare[count] = high
            return count + two.astype(jnp.int32)

        def fill(p, count):
            empty = first_ref[p] == chips
            first_ref[p] = jnp.where(empty, spare[count], first_ref[p])
            return count + empty.astype(jnp.int32)

        lax.fori_loop(0, chips, collect, jnp.int32(0))
        lax.fori_loop(0, chips, fill, jnp.int32(0))
        kept = table_ref[row, slot_ref[0]]
        same = kept == first_ref[lax.div(slot_ref[0], 2)]
        mode_ref[0] = jnp.where(kept < chips, jnp.where(same, 1, 2), 0)

    return pl.pallas_call(
        kernel,
        out_shape=[jax.ShapeDtypeStruct((n,), jnp.int32) for n in (chips, chips, 1)],
        in_specs=[smem(), smem(), smem()],
        out_specs=[smem(), smem(), smem()],
        scratch_shapes=[pltpu.SMEM((chips + 1,), jnp.int32)],
        compiler_params=params(),
        cost_estimate=cost(0, 1024),
        name="assigned",
    )(here, slot, slot_block)


def outgoing_pieces(first, second, terms):
    rows, row_blocks, cols = terms[0].shape
    col_blocks = cols // BLK
    group = row_blocks * col_blocks
    chips = first.shape[0]

    def kernel(
        first_ref, second_ref, below_ref, above_ref, own_ref, out_ref, wide, pieces
    ):
        for k in range(cols // LANES):
            at = (slice(None), slice(None), slice(k * LANES, (k + 1) * LANES))
            lanes = below_ref[at].astype(F32) + above_ref[at].astype(F32)
            lanes = lanes + own_ref[at].astype(F32)
            wide[k] = lanes.reshape(rows * row_blocks, LANES)
        for rb in range(row_blocks):
            for k in range(cols // LANES):
                v, at = rb * col_blocks + k // PER_BLK, k % PER_BLK * LANES
                part = wide[k, pl.ds(rb, rows, stride=row_blocks), :]
                pieces[v, :, at : at + LANES] = part.astype(BF16)
        pieces[group] = jnp.zeros((rows, BLK), BF16)

        def place(p, carry):
            out_ref[p, 0] = pieces[first_ref[p]]
            out_ref[p, 1] = pieces[second_ref[p]]
            return carry

        lax.fori_loop(0, chips, place, 0, unroll=4)

    return pl.pallas_call(
        kernel,
        out_shape=jax.ShapeDtypeStruct((chips, 2, rows, BLK), BF16),
        in_specs=[smem(), smem(), vmem(), vmem(), vmem()],
        out_specs=vmem(),
        scratch_shapes=[
            pltpu.VMEM((cols // LANES, rows * row_blocks, LANES), F32),
            pltpu.VMEM((group + 1, rows, BLK), BF16),
        ],
        compiler_params=params(),
        cost_estimate=cost(0, 6 * chips * rows * BLK * 2),
        name="outgoing",
    )(first, second, *terms)


def incoming_update(first, returned, row_blocks, col_blocks):
    chips, rows, _ = returned.shape
    cols = col_blocks * BLK

    def kernel(first_ref, x_ref, out_ref, wide, pieces):
        def place(s, carry):
            pieces[first_ref[s]] = x_ref[s]
            return carry

        lax.fori_loop(0, chips, place, 0, unroll=4)
        for rb in range(row_blocks):
            for k in range(cols // LANES):
                v, at = rb * col_blocks + k // PER_BLK, k % PER_BLK * LANES
                part = pieces[v, :, at : at + LANES].astype(F32)
                wide[k, pl.ds(rb, rows, stride=row_blocks), :] = part
        for k in range(cols // LANES):
            lanes = wide[k].reshape(rows, row_blocks, LANES)
            out_ref[:, :, k * LANES : (k + 1) * LANES] = lanes.astype(BF16)

    return pl.pallas_call(
        kernel,
        out_shape=jax.ShapeDtypeStruct((rows, row_blocks, cols), BF16),
        in_specs=[smem(), vmem()],
        out_specs=vmem(),
        scratch_shapes=[
            pltpu.VMEM((cols // LANES, rows * row_blocks, LANES), F32),
            pltpu.VMEM((chips, rows, BLK), BF16),
        ],
        compiler_params=params(),
        cost_estimate=cost(0, 3 * chips * rows * BLK * 2),
        name="incoming",
    )(first, returned)


def dot(a, b, contract=((1,), (0,))):
    return lax.dot_general(a, b, (contract, ((), ())), preferred_element_type=F32)


def strips(rows=BLK):
    return [slice(at, at + STRIP) for at in range(0, rows, STRIP)]


def folded(x):
    return jnp.sum(x.reshape(-1, 8, x.shape[-1]), axis=0)


def put_linear(out_ref, in_ref, times, diagonal):
    row = lax.broadcasted_iota(jnp.int32, (STRIP, LANES), 0)
    lane = lax.broadcasted_iota(jnp.int32, (STRIP, LANES), 1)
    for at in strips():
        x = in_ref[at, :] * times
        out_ref[at, :] = x.astype(BF16)
        left = at.start // LANES * LANES
        lanes = slice(left, left + LANES)
        eye = jnp.where(row + (at.start - left) == lane, diagonal, 0.0)
        out_ref[at, lanes] = (x[:, lanes] + eye).astype(BF16)


def newton_root(gram, total, scale, low, rest, root):
    shift = DAMPING * total / BLK + 1e-06
    squares = sum(folded(gram[at, :] * gram[at, :]) for at in strips())
    squares = jnp.sum(squares) * (scale * scale)
    norm = jnp.sqrt(squares + 2.0 * shift * total + BLK * shift * shift) / 4.0
    times, diagonal = scale / norm, shift / norm
    start = lax.rsqrt(jnp.sqrt(norm))
    for iteration in range(ITERS):
        put_linear(low, gram, -0.25 * times, 1.25 - 0.25 * diagonal)
        if iteration == 0:
            put_linear(root, gram, -0.25 * times * start, (1.25 - 0.25 * diagonal) * start)
        else:
            root[...] = dot(root[...], low[...]).astype(BF16)
        if iteration + 1 < ITERS:
            put_linear(rest, gram, times, diagonal)
            square = dot(low[...], low[...]).astype(BF16)
            fourth = dot(square, square).astype(BF16)
            gram[...] = dot(fourth, rest[...])
            times, diagonal = 1.0, 0.0


def whole_block(core_ref, mine_ref, other_ref, which, halves, block):
    halves[:, core_ref[0]] = mine_ref[:, which].astype(F32)
    halves[:, 1 - core_ref[0]] = other_ref[:, which].astype(F32)
    chips, _, rows, _ = halves.shape
    per_strip = STRIP // (2 * rows)
    squares = 0.0
    for k, at in enumerate(strips()):
        x = halves[k * per_strip : (k + 1) * per_strip].reshape(STRIP, BLK)
        block[at, :] = x.astype(BF16)
        squares += folded(x * x)
    return jnp.sum(squares)


def buffers(chips, rows):
    return [
        pltpu.VMEM((chips, 2, rows, BLK), F32),
        pltpu.VMEM((BLK, BLK), F32),
        pltpu.VMEM((BLK, BLK), BF16),
        pltpu.VMEM((BLK, BLK), BF16),
        pltpu.VMEM((BLK, BLK), BF16),
    ]


def first_work(core, mine, other, replicas):
    chips, _, rows, _ = mine.shape
    scale = 1.0 / (replicas * replicas)

    def kernel(core_ref, mine_ref, other_ref, right, update_ref, halves, gram, block, low, rest):
        total = whole_block(core_ref, mine_ref, other_ref, 0, halves, block) * scale
        gram[...] = dot(block[...], block[...], ((0,), (0,)))
        newton_root(gram, total, scale, low, rest, right)
        low[...] = (dot(block[...], right[...]) * (1.0 / replicas)).astype(BF16)
        halves[...] = dot(low[...], right[...]).reshape(halves.shape)
        squares = sum(folded(halves[p] * halves[p]) for p in range(chips))
        count = BLK * BLK
        grad_rms = jnp.sqrt(total / count)
        dir_rms = jnp.sqrt(jnp.sum(squares) / count + 1e-06)
        factor = -(grad_rms / dir_rms)
        for p in range(0, chips, 4):
            update_ref[p : p + 4] = (halves[p : p + 4, core_ref[0]] * factor).astype(BF16)

    return pl.pallas_call(
        kernel,
        out_shape=(
            jax.ShapeDtypeStruct((BLK, BLK), BF16),
            jax.ShapeDtypeStruct((chips, rows, BLK), BF16),
        ),
        in_specs=[smem(), vmem(), vmem()],
        out_specs=(vmem(), vmem()),
        scratch_shapes=buffers(chips, rows),
        compiler_params=params(),
        cost_estimate=cost(14 * BLK**3, 8 * BLK * BLK),
        name="first_work",
    )(core, mine, other)


def slot_work(mode, core, mine, other, first_right, replicas):
    chips, _, rows, _ = mine.shape
    scale = 1.0 / (replicas * replicas)

    def kernel(mode_ref, core_ref, mine_ref, other_ref, right_ref, out_ref, halves, gram, block, low, rest):
        def left_root(which):
            total = whole_block(core_ref, mine_ref, other_ref, which, halves, block) * scale
            gram[...] = dot(block[...], block[...], ((1,), (1,)))
            newton_root(gram, total, scale, low, rest, out_ref.at[0])
            return total

        @pl.when(mode_ref[0] == 0)
        def _():
            out_ref[...] = jnp.zeros_like(out_ref)

        @pl.when(mode_ref[0] == 1)
        def _():
            left_root(0)
            out_ref[1] = right_ref[...]

        @pl.when(mode_ref[0] == 2)
        def _():
            total = left_root(1)
            gram[...] = dot(block[...], block[...], ((0,), (0,)))
            newton_root(gram, total, scale, low, rest, out_ref.at[1])

    return pl.pallas_call(
        kernel,
        out_shape=jax.ShapeDtypeStruct((2, BLK, BLK), BF16),
        in_specs=[smem(), smem(), vmem(), vmem(), vmem()],
        out_specs=vmem(),
        scratch_shapes=buffers(chips, rows),
        compiler_params=params(),
        cost_estimate=cost(20 * BLK**3, 8 * BLK * BLK),
        name="slot_work",
    )(mode, core, mine, other, first_right)


def part_of(parts_ref, here_ref, offset):
    return parts_ref.at[lax.rem(here_ref[0] + offset, parts_ref.shape[0])]


def picked(here, parts, offsets):
    def kernel(here_ref, parts_ref, *refs):
        outs, sems = refs[: len(offsets)], refs[len(offsets)]
        copies = [
            pltpu.make_async_copy(part_of(parts_ref, here_ref, offset), out, sems.at[k])
            for k, (offset, out) in enumerate(zip(offsets, outs))
        ]
        for copy in copies:
            copy.start()
        for copy in copies:
            copy.wait()

    return pl.pallas_call(
        kernel,
        out_shape=[jax.ShapeDtypeStruct(parts.shape[1:], BF16)] * len(offsets),
        in_specs=[smem(), pl.BlockSpec(memory_space=pltpu.HBM)],
        out_specs=[vmem()] * len(offsets),
        scratch_shapes=[pltpu.SemaphoreType.DMA((len(offsets),))],
        compiler_params=params(PICK_LIMIT),
        cost_estimate=cost(0, 4 * parts[0].size * len(offsets)),
        name="picked",
    )(here, parts)


def staged(parts):
    def kernel(parts_ref, out_ref, sem):
        copy = pltpu.make_async_copy(parts_ref, out_ref, sem.at[0])
        copy.start()
        copy.wait()

    return pl.pallas_call(
        kernel,
        out_shape=jax.ShapeDtypeStruct(parts.shape, BF16),
        in_specs=[pl.BlockSpec(memory_space=pltpu.HBM)],
        out_specs=vmem(),
        scratch_shapes=[pltpu.SemaphoreType.DMA((1,))],
        compiler_params=params(STAGE_LIMIT),
        cost_estimate=cost(0, 4 * parts.size),
        name="staged",
    )(parts)


def added(here, total, parts, offset):
    def kernel(here_ref, total_ref, parts_ref, out_ref):
        own = part_of(parts_ref, here_ref, offset)[...].astype(F32)
        out_ref[...] = (total_ref[...].astype(F32) + own).astype(BF16)

    return pl.pallas_call(
        kernel,
        out_shape=jax.ShapeDtypeStruct(total.shape, BF16),
        in_specs=[smem(), vmem(), vmem()],
        out_specs=vmem(),
        compiler_params=params(),
        cost_estimate=cost(total.size, 6 * total.size),
        name="added",
    )(here, total, parts)


def ring_terms(here, parts, axis):
    n = parts.shape[0]
    raising = [(i, (i + 1) % n) for i in range(n)]
    lowering = [(i, (i - 1) % n) for i in range(n)]
    hops = n // 2
    first = 2 * hops + 1 - n
    below, above, own = picked(here, parts, (hops, (first - hops) % n, 0))
    below, parts = lax.optimization_barrier((below, parts))
    parts = staged(parts)
    for step in range(hops):
        if step > 0:
            below = added(here, below, parts, hops - step)
        below = lax.ppermute(below, axis, raising)
        if step > first:
            above = added(here, above, parts, (step - hops) % n)
        if step >= first:
            above = lax.ppermute(above, axis, lowering)
    return below, above, own


def local(grads, slot_block):
    replicas = lax.axis_size("dp")
    here, slot = lax.axis_index("dp")[None], lax.axis_index("fsdp")[None]
    core = slot % 2
    chips = slot_block.shape[1] // 2
    same_core = [[2 * p + c for p in range(chips)] for c in range(2)]
    across = [(i, i ^ 1) for i in range(2 * chips)]

    def exchanged(x):
        return lax.all_to_all(
            x, "fsdp", split_axis=0, concat_axis=0, axis_index_groups=same_core, tiled=True
        )

    first, second, mode = assigned(here, slot, slot_block)
    terms = ring_terms(here, grads[0], "dp")
    _, row_blocks, cols = terms[0].shape
    mine = exchanged(outgoing_pieces(first, second, terms))
    other = lax.ppermute(mine, "fsdp", across)
    right, update = first_work(core, mine, other, replicas)
    returned = exchanged(update)
    roots = slot_work(mode, core, mine, other, right, replicas)
    result = incoming_update(first, returned, row_blocks, cols // BLK)
    return result[None], roots[None, None]


def solution(mesh):
    return jax.shard_map(
        local,
        mesh=mesh,
        in_specs=(P("dp", None, "fsdp", None, None), P()),
        out_specs=(P("dp", "fsdp", None, None), P("dp", "fsdp", None, None, None)),
        check_vma=False,
    )
```

time: 128 us -> 125 us (0.977)
  local copies, waits for them, and re-layouts: 4.52 us -> 0.01 us
  waiting for transfers between devices: 29.2 us -> 31.7 us
  between operations: 2.89 us -> 0.89 us
    all_to_all x1, waiting for transfers between devices: 7.56 us -> 11 us  [exchanged(): lax.all_to_all(x, 'fsdp', split_axis=0, concat_axis=0, axis_index_groups=...]
    pallas_call x1, Pallas kernels: 0.03 us -> 2.02 us  [picked(): pl.pallas_call(kernel, out_shape=[jax.ShapeDtypeStruct(parts.shape[1:], B...]
    dynamic_slice x2 -> x0, local copies, waits for them, and re-layouts: 1.93 us -> none  [the longest x1 1.27 us: local(): kept = lax.dynamic_slice_in_dim(table, slot, 1, 0)]
    unnamed x4, local copies, waits for them, and re-layouts: 1.89 us -> 0.01 us
    pallas_call x9, Pallas kernels: 2.04 us -> 0.65 us  [added(): pl.pallas_call(kernel, out_shape=jax.ShapeDtypeStruct(total.shape, BF16),...]
    pallas_call x3 -> x4, Pallas kernels: 9 us -> 9.48 us  [the longest x1 4.07 us: first_work(): pl.pallas_call(kernel, out_shape=(jax.ShapeDtypeStruct((BLK, BLK), BF16),...]
  transfers between devices with their start and end apart: 13 -> 13, of which waited for: 8 -> 8; matrix products, arithmetic and copies ran while one was open for 2% -> 0% of each run, Pallas kernels for 4% -> 5%
where the time goes in v6:
time: 125 us; the launch traced here: 124 us
  starting transfers between devices  53.3 us (43%)
  waiting for transfers between devices  31.7 us (25%)
  blocking collectives  23.6 us (19%)
  Pallas kernels  14.7 us (12%)
    ppermute x5, starting transfers between devices, ring_terms(): above = lax.ppermute(above, axis, lowering)  32.8 us
    all_to_all x1, blocking collectives, exchanged(): lax.all_to_all(x, 'fsdp', split_axis=0, concat_axis=0, axis_index_groups=...  23.6 us
    ppermute x6, waiting for transfers between devices, ring_terms(): below = lax.ppermute(below, axis, raising)  18.9 us
    ppermute x6, starting transfers between devices, ring_terms(): below = lax.ppermute(below, axis, raising)  14 us
    all_to_all x1, waiting for transfers between devices, exchanged(): lax.all_to_all(x, 'fsdp', split_axis=0, concat_axis=0, axis_index_groups=...  11 us
    all_to_all x1, starting transfers between devices, exchanged(): lax.all_to_all(x, 'fsdp', split_axis=0, concat_axis=0, axis_index_groups=...  4.66 us
    pallas_call x1, Pallas kernels, first_work(): pl.pallas_call(kernel, out_shape=(jax.ShapeDtypeStruct((BLK, BLK), BF16),...  4.07 us
  transfers between devices with their start and end apart: 13, of which 8 were waited for; matrix products, arithmetic and copies ran while one was open for 0% of the time, Pallas kernels for 5%

profile of v6, /device:TPU:8, one launch (start us, length us, event | category | flops | bytes accessed | tf_op | source)
XLA Modules:
  0.0 124.2 jit_solution(15774623340469724468)
XLA Ops:
  0.6 2.0 %picked.1 = (bf16[8,16,1024]{2,1,0:T(8,128)(2,1)}, bf16[8,16,1024]{2,1,0:T(8,128)(2,1)}, bf16[8,16,1024]{2,1,0:T(8,128)(2,1)}) custom-call(s32[1]{0:T(128)} %bitcast.here_ref, bf16[12,8,16,1024]{3,2,1,0:T(8,128)(2,1)} %bitcast.5), custom_call_target="tpu_custom_call" | custom-call | bytes 1572864 | tf_op jit(solution)/shard_map/picked/pallas_call | solution.py:306
  2.7 4.3 %collective-permute-start = (bf16[8,16,1024]{2,1,0:T(8,128)(2,1)}, bf16[8,16,1024]{2,1,0:T(8,128)(2,1)S(1)}, u32[]{:S(2)}, u32[]{:S(2)}) collective-permute-start(bf16[8,16,1024]{2,1,0:T(8,128)(2,1)} %get-tuple-element.15), channel_id=1, source_target_pairs={{0,64},{64,128},{128,192},{192,256},{256,320},{320,384},{384,448},... | collective-permute-start | bytes 786440 | tf_op jit(solution)/shard_map/ppermute | solution.py:364
  7.0 12.2 %collective-permute-start.6 = (bf16[8,16,1024]{2,1,0:T(8,128)(2,1)}, bf16[8,16,1024]{2,1,0:T(8,128)(2,1)S(1)}, u32[]{:S(2)}, u32[]{:S(2)}) collective-permute-start(bf16[8,16,1024]{2,1,0:T(8,128)(2,1)} %get-tuple-element.17), channel_id=1, source_target_pairs={{0,704},{64,0},{128,64},{192,128},{256,192},{320,256},{384,320},{4... | collective-permute-start | bytes 786440 | tf_op jit(solution)/shard_map/ppermute | solution.py:368
  19.2 1.9 %staged.1.parts_ref = bf16[12,8,16,1024]{3,2,1,0:T(8,128)(2,1)S(1)} custom-call(bf16[12,8,16,1024]{3,2,1,0:T(8,128)(2,1)} %bitcast.6), custom_call_target="tpu_custom_call" | custom-call | bytes 6291456 | tf_op jit(solution)/shard_map/staged/pallas_call | solution.py:324
  21.1 2.7 %collective-permute-done.total_ref = bf16[8,16,1024]{2,1,0:T(8,128)(2,1)S(1)} collective-permute-done((bf16[8,16,1024]{2,1,0:T(8,128)(2,1)}, bf16[8,16,1024]{2,1,0:T(8,128)(2,1)S(1)}, u32[]{:S(2)}, u32[]{:S(2)}) %collective-permute-start) | collective-permute-done | bytes 262176 | tf_op jit(solution)/shard_map/ppermute | solution.py:364
  23.8 1.9 %collective-permute-start.1 = (bf16[8,16,1024]{2,1,0:T(8,128)(2,1)S(1)}, bf16[8,16,1024]{2,1,0:T(8,128)(2,1)S(1)}, u32[]{:S(2)}, u32[]{:S(2)}) collective-permute-start(bf16[8,16,1024]{2,1,0:T(8,128)(2,1)S(1)} %added.9), channel_id=1, source_target_pairs={{0,64},{64,128},{128,192},{192,256},{256,320},{320,384},{384,448},... | collective-permute-start | bytes 786440 | tf_op jit(solution)/shard_map/ppermute | solution.py:364
  25.9 5.1 %collective-permute-start.7 = (bf16[8,16,1024]{2,1,0:T(8,128)(2,1)S(1)}, bf16[8,16,1024]{2,1,0:T(8,128)(2,1)S(1)}, u32[]{:S(2)}, u32[]{:S(2)}) collective-permute-start(bf16[8,16,1024]{2,1,0:T(8,128)(2,1)S(1)} %added.14), channel_id=1, source_target_pairs={{0,704},{64,0},{128,64},{192,128},{256,192},{320,256},{384,320},{4... | collective-permute-start | bytes 786440 | tf_op jit(solution)/shard_map/ppermute | solution.py:368
  31.0 3.4 %collective-permute-done.1.total_ref = bf16[8,16,1024]{2,1,0:T(8,128)(2,1)S(1)} collective-permute-done((bf16[8,16,1024]{2,1,0:T(8,128)(2,1)S(1)}, bf16[8,16,1024]{2,1,0:T(8,128)(2,1)S(1)}, u32[]{:S(2)}, u32[]{:S(2)}) %collective-permute-start.1) | collective-permute-done | bytes 262176 | tf_op jit(solution)/shard_map/ppermute | solution.py:364
  34.5 1.9 %collective-permute-start.2 = (bf16[8,16,1024]{2,1,0:T(8,128)(2,1)S(1)}, bf16[8,16,1024]{2,1,0:T(8,128)(2,1)S(1)}, u32[]{:S(2)}, u32[]{:S(2)}) collective-permute-start(bf16[8,16,1024]{2,1,0:T(8,128)(2,1)S(1)} %added.10), channel_id=1, source_target_pairs={{0,64},{64,128},{128,192},{192,256},{256,320},{320,384},{384,448},... | collective-permute-start | bytes 786440 | tf_op jit(solution)/shard_map/ppermute | solution.py:364
  36.5 5.1 %collective-permute-start.8 = (bf16[8,16,1024]{2,1,0:T(8,128)(2,1)S(1)}, bf16[8,16,1024]{2,1,0:T(8,128)(2,1)S(1)}, u32[]{:S(2)}, u32[]{:S(2)}) collective-permute-start(bf16[8,16,1024]{2,1,0:T(8,128)(2,1)S(1)} %added.15), channel_id=1, source_target_pairs={{0,704},{64,0},{128,64},{192,128},{256,192},{320,256},{384,320},{4... | collective-permute-start | bytes 786440 | tf_op jit(solution)/shard_map/ppermute | solution.py:368
  41.7 2.5 %collective-permute-done.2.total_ref = bf16[8,16,1024]{2,1,0:T(8,128)(2,1)S(1)} collective-permute-done((bf16[8,16,1024]{2,1,0:T(8,128)(2,1)S(1)}, bf16[8,16,1024]{2,1,0:T(8,128)(2,1)S(1)}, u32[]{:S(2)}, u32[]{:S(2)}) %collective-permute-start.2) | collective-permute-done | bytes 262176 | tf_op jit(solution)/shard_map/ppermute | solution.py:364
  44.3 1.9 %collective-permute-start.3 = (bf16[8,16,1024]{2,1,0:T(8,128)(2,1)S(1)}, bf16[8,16,1024]{2,1,0:T(8,128)(2,1)S(1)}, u32[]{:S(2)}, u32[]{:S(2)}) collective-permute-start(bf16[8,16,1024]{2,1,0:T(8,128)(2,1)S(1)} %added.11), channel_id=1, source_target_pairs={{0,64},{64,128},{128,192},{192,256},{256,320},{320,384},{384,448},... | collective-permute-start | bytes 786440 | tf_op jit(solution)/shard_map/ppermute | solution.py:364
  46.3 5.1 %collective-permute-start.9 = (bf16[8,16,1024]{2,1,0:T(8,128)(2,1)S(1)}, bf16[8,16,1024]{2,1,0:T(8,128)(2,1)S(1)}, u32[]{:S(2)}, u32[]{:S(2)}) collective-permute-start(bf16[8,16,1024]{2,1,0:T(8,128)(2,1)S(1)} %added.16), channel_id=1, source_target_pairs={{0,704},{64,0},{128,64},{192,128},{256,192},{320,256},{384,320},{4... | collective-permute-start | bytes 786440 | tf_op jit(solution)/shard_map/ppermute | solution.py:368
  51.4 2.3 %collective-permute-done.3.total_ref = bf16[8,16,1024]{2,1,0:T(8,128)(2,1)S(1)} collective-permute-done((bf16[8,16,1024]{2,1,0:T(8,128)(2,1)S(1)}, bf16[8,16,1024]{2,1,0:T(8,128)(2,1)S(1)}, u32[]{:S(2)}, u32[]{:S(2)}) %collective-permute-start.3) | collective-permute-done | bytes 262176 | tf_op jit(solution)/shard_map/ppermute | solution.py:364
  53.8 2.1 %collective-permute-start.4 = (bf16[8,16,1024]{2,1,0:T(8,128)(2,1)S(1)}, bf16[8,16,1024]{2,1,0:T(8,128)(2,1)S(1)}, u32[]{:S(2)}, u32[]{:S(2)}) collective-permute-start(bf16[8,16,1024]{2,1,0:T(8,128)(2,1)S(1)} %added.12), channel_id=1, source_target_pairs={{0,64},{64,128},{128,192},{192,256},{256,320},{320,384},{384,448},... | collective-permute-start | bytes 786440 | tf_op jit(solution)/shard_map/ppermute | solution.py:364
  56.0 5.1 %collective-permute-start.10 = (bf16[8,16,1024]{2,1,0:T(8,128)(2,1)S(1)}, bf16[8,16,1024]{2,1,0:T(8,128)(2,1)S(1)}, u32[]{:S(2)}, u32[]{:S(2)}) collective-permute-start(bf16[8,16,1024]{2,1,0:T(8,128)(2,1)S(1)} %added.17), channel_id=1, source_target_pairs={{0,704},{64,0},{128,64},{192,128},{256,192},{320,256},{384,320},{4... | collective-permute-start | bytes 786440 | tf_op jit(solution)/shard_map/ppermute | solution.py:368
  61.1 2.3 %collective-permute-done.4.total_ref = bf16[8,16,1024]{2,1,0:T(8,128)(2,1)S(1)} collective-permute-done((bf16[8,16,1024]{2,1,0:T(8,128)(2,1)S(1)}, bf16[8,16,1024]{2,1,0:T(8,128)(2,1)S(1)}, u32[]{:S(2)}, u32[]{:S(2)}) %collective-permute-start.4) | collective-permute-done | bytes 262176 | tf_op jit(solution)/shard_map/ppermute | solution.py:364
  63.5 1.9 %collective-permute-start.5 = (bf16[8,16,1024]{2,1,0:T(8,128)(2,1)S(1)}, bf16[8,16,1024]{2,1,0:T(8,128)(2,1)S(1)}, u32[]{:S(2)}, u32[]{:S(2)}) collective-permute-start(bf16[8,16,1024]{2,1,0:T(8,128)(2,1)S(1)} %added.13), channel_id=1, source_target_pairs={{0,64},{64,128},{128,192},{192,256},{256,320},{320,384},{384,448},... | collective-permute-start | bytes 786440 | tf_op jit(solution)/shard_map/ppermute | solution.py:364
  67.4 5.6 %collective-permute-done.5.below_ref = bf16[8,16,1024]{2,1,0:T(8,128)(2,1)S(1)} collective-permute-done((bf16[8,16,1024]{2,1,0:T(8,128)(2,1)S(1)}, bf16[8,16,1024]{2,1,0:T(8,128)(2,1)S(1)}, u32[]{:S(2)}, u32[]{:S(2)}) %collective-permute-start.5) | collective-permute-done | bytes 262176 | tf_op jit(solution)/shard_map/ppermute | solution.py:364
  73.9 23.6 %all_to_all.10.mine_ref = bf16[32,2,8,512]{3,2,1,0:T(8,128)(2,1)S(1)} all-to-all(bf16[32,2,8,512]{3,2,1,0:T(8,128)(2,1)S(1)} %outgoing.1), channel_id=1, replica_groups={{0,2,4,6,8,10,12,14,16,18,20,22,24,26,28,30,32,34,36,38,40,42,44,46,48,..., dimensions={0} | all-to-all | bytes 1048576 | tf_op jit(solution)/shard_map/all_to_all | solution.py:381
  97.5 1.9 %collective-permute-start.11 = (bf16[32,2,8,512]{3,2,1,0:T(8,128)(2,1)S(1)}, bf16[32,2,8,512]{3,2,1,0:T(8,128)(2,1)S(1)}, u32[]{:S(2)}, u32[]{:S(2)}) collective-permute-start(bf16[32,2,8,512]{3,2,1,0:T(8,128)(2,1)S(1)} %all_to_all.10.mine_ref), channel_id=1, source_target_pairs={{0,1},{1,0},{2,3},{3,2},{4,5},{5,4},{6,7},{7,6},{8,9},{9,8},{10,11... | collective-permute-start | bytes 1572872 | tf_op jit(solution)/shard_map/ppermute | solution.py:389
  101.3 4.1 %first_work.1 = (bf16[512,512]{1,0:T(8,128)(2,1)S(1)}, bf16[32,8,512]{2,1,0:T(8,128)(2,1)}) custom-call(s32[1]{0:T(128)S(6)} %select_n.7.core_ref, bf16[32,2,8,512]{3,2,1,0:T(8,128)(2,1)S(1)} %all_to_all.10.mine_ref, bf16[32,2,8,512]{3,2,1,0:T(8,128)(2,1)S(1)} %collective-permute-done.11.other_ref), custom_call_target="tpu_custom_call" | custom-call | flops 1879048192 | bytes 2097152 | tf_op jit(solution)/shard_map/first_work/pallas_call | solution.py:237
  105.4 4.7 %all-to-all-start.1 = ((bf16[32,8,512]{2,1,0:T(8,128)(2,1)}), bf16[32,8,512]{2,1,0:T(8,128)(2,1)S(1)}, u32[]{:S(2)}, u32[]{:S(2)}) async-start(bf16[32,8,512]{2,1,0:T(8,128)(2,1)} %get-tuple-element.19), calls=%async_computation.1 | async-start | bytes 524288 | tf_op jit(solution)/shard_map/all_to_all | solution.py:381
  111.6 11.0 %all-to-all-done.1.x_ref = bf16[32,8,512]{2,1,0:T(8,128)(2,1)S(1)} async-done(((bf16[32,8,512]{2,1,0:T(8,128)(2,1)}), bf16[32,8,512]{2,1,0:T(8,128)(2,1)S(1)}, u32[]{:S(2)}, u32[]{:S(2)}) %all-to-all-start.1) | async-done | bytes 262176 | tf_op jit(solution)/shard_map/all_to_all | solution.py:381
  (23 shorter events, 8.6 us)
Async XLA Ops:
  2.7 21.1 %collective-permute-start = (bf16[8,16,1024]{2,1,0:T(8,128)(2,1)}, bf16[8,16,1024]{2,1,0:T(8,128)(2,1)S(1)}, u32[]{:S(2)}, u32[]{:S(2)}) collective-permute-start(bf16[8,16,1024]{2,1,0:T(8,128)(2,1)} %get-tuple-element.15), channel_id=1, source_target_pairs={{0,64},{64,128},{128,192},{192,256},{256,320},{320,384},{384,448},... | collective-permute-start | bytes 786440 | tf_op jit(solution)/shard_map/ppermute | solution.py:364
  7.0 18.8 %collective-permute-start.6 = (bf16[8,16,1024]{2,1,0:T(8,128)(2,1)}, bf16[8,16,1024]{2,1,0:T(8,128)(2,1)S(1)}, u32[]{:S(2)}, u32[]{:S(2)}) collective-permute-start(bf16[8,16,1024]{2,1,0:T(8,128)(2,1)} %get-tuple-element.17), channel_id=1, source_target_pairs={{0,704},{64,0},{128,64},{192,128},{256,192},{320,256},{384,320},{4... | collective-permute-start | bytes 786440 | tf_op jit(solution)/shard_map/ppermute | solution.py:368
  23.8 10.6 %collective-permute-start.1 = (bf16[8,16,1024]{2,1,0:T(8,128)(2,1)S(1)}, bf16[8,16,1024]{2,1,0:T(8,128)(2,1)S(1)}, u32[]{:S(2)}, u32[]{:S(2)}) collective-permute-start(bf16[8,16,1024]{2,1,0:T(8,128)(2,1)S(1)} %added.9), channel_id=1, source_target_pairs={{0,64},{64,128},{128,192},{192,256},{256,320},{320,384},{384,448},... | collective-permute-start | bytes 786440 | tf_op jit(solution)/shard_map/ppermute | solution.py:364
  25.9 10.6 %collective-permute-start.7 = (bf16[8,16,1024]{2,1,0:T(8,128)(2,1)S(1)}, bf16[8,16,1024]{2,1,0:T(8,128)(2,1)S(1)}, u32[]{:S(2)}, u32[]{:S(2)}) collective-permute-start(bf16[8,16,1024]{2,1,0:T(8,128)(2,1)S(1)} %added.14), channel_id=1, source_target_pairs={{0,704},{64,0},{128,64},{192,128},{256,192},{320,256},{384,320},{4... | collective-permute-start | bytes 786440 | tf_op jit(solution)/shard_map/ppermute | solution.py:368
  34.5 9.7 %collective-permute-start.2 = (bf16[8,16,1024]{2,1,0:T(8,128)(2,1)S(1)}, bf16[8,16,1024]{2,1,0:T(8,128)(2,1)S(1)}, u32[]{:S(2)}, u32[]{:S(2)}) collective-permute-start(bf16[8,16,1024]{2,1,0:T(8,128)(2,1)S(1)} %added.10), channel_id=1, source_target_pairs={{0,64},{64,128},{128,192},{192,256},{256,320},{320,384},{384,448},... | collective-permute-start | bytes 786440 | tf_op jit(solution)/shard_map/ppermute | solution.py:364
  36.5 9.7 %collective-permute-start.8 = (bf16[8,16,1024]{2,1,0:T(8,128)(2,1)S(1)}, bf16[8,16,1024]{2,1,0:T(8,128)(2,1)S(1)}, u32[]{:S(2)}, u32[]{:S(2)}) collective-permute-start(bf16[8,16,1024]{2,1,0:T(8,128)(2,1)S(1)} %added.15), channel_id=1, source_target_pairs={{0,704},{64,0},{128,64},{192,128},{256,192},{320,256},{384,320},{4... | collective-permute-start | bytes 786440 | tf_op jit(solution)/shard_map/ppermute | solution.py:368
  44.3 9.5 %collective-permute-start.3 = (bf16[8,16,1024]{2,1,0:T(8,128)(2,1)S(1)}, bf16[8,16,1024]{2,1,0:T(8,128)(2,1)S(1)}, u32[]{:S(2)}, u32[]{:S(2)}) collective-permute-start(bf16[8,16,1024]{2,1,0:T(8,128)(2,1)S(1)} %added.11), channel_id=1, source_target_pairs={{0,64},{64,128},{128,192},{192,256},{256,320},{320,384},{384,448},... | collective-permute-start | bytes 786440 | tf_op jit(solution)/shard_map/ppermute | solution.py:364
  46.3 9.6 %collective-permute-start.9 = (bf16[8,16,1024]{2,1,0:T(8,128)(2,1)S(1)}, bf16[8,16,1024]{2,1,0:T(8,128)(2,1)S(1)}, u32[]{:S(2)}, u32[]{:S(2)}) collective-permute-start(bf16[8,16,1024]{2,1,0:T(8,128)(2,1)S(1)} %added.16), channel_id=1, source_target_pairs={{0,704},{64,0},{128,64},{192,128},{256,192},{320,256},{384,320},{4... | collective-permute-start | bytes 786440 | tf_op jit(solution)/shard_map/ppermute | solution.py:368
  53.8 11.6 %copy-start.1 = (s32[12,64]{1,0:T(8,128)S(1)}, s32[12,64]{1,0:T(8,128)}, u32[]{:S(2)}) copy-start(s32[12,64]{1,0:T(8,128)} %table_ref.1) | copy-start | bytes 9220
  53.8 19.2 %copy-start = (bf16[8,16,1024]{2,1,0:T(8,128)(2,1)S(1)}, bf16[8,16,1024]{2,1,0:T(8,128)(2,1)}, u32[]{:S(2)}) copy-start(bf16[8,16,1024]{2,1,0:T(8,128)(2,1)} %get-tuple-element.18.own_ref) | copy-start | bytes 786436
  53.8 9.6 %collective-permute-start.4 = (bf16[8,16,1024]{2,1,0:T(8,128)(2,1)S(1)}, bf16[8,16,1024]{2,1,0:T(8,128)(2,1)S(1)}, u32[]{:S(2)}, u32[]{:S(2)}) collective-permute-start(bf16[8,16,1024]{2,1,0:T(8,128)(2,1)S(1)} %added.12), channel_id=1, source_target_pairs={{0,64},{64,128},{128,192},{192,256},{256,320},{320,384},{384,448},... | collective-permute-start | bytes 786440 | tf_op jit(solution)/shard_map/ppermute | solution.py:364
  56.0 11.4 %collective-permute-start.10 = (bf16[8,16,1024]{2,1,0:T(8,128)(2,1)S(1)}, bf16[8,16,1024]{2,1,0:T(8,128)(2,1)S(1)}, u32[]{:S(2)}, u32[]{:S(2)}) collective-permute-start(bf16[8,16,1024]{2,1,0:T(8,128)(2,1)S(1)} %added.17), channel_id=1, source_target_pairs={{0,704},{64,0},{128,64},{192,128},{256,192},{320,256},{384,320},{4... | collective-permute-start | bytes 786440 | tf_op jit(solution)/shard_map/ppermute | solution.py:368
  63.5 9.5 %collective-permute-start.5 = (bf16[8,16,1024]{2,1,0:T(8,128)(2,1)S(1)}, bf16[8,16,1024]{2,1,0:T(8,128)(2,1)S(1)}, u32[]{:S(2)}, u32[]{:S(2)}) collective-permute-start(bf16[8,16,1024]{2,1,0:T(8,128)(2,1)S(1)} %added.13), channel_id=1, source_target_pairs={{0,64},{64,128},{128,192},{192,256},{256,320},{320,384},{384,448},... | collective-permute-start | bytes 786440 | tf_op jit(solution)/shard_map/ppermute | solution.py:364
  97.5 3.8 %collective-permute-start.11 = (bf16[32,2,8,512]{3,2,1,0:T(8,128)(2,1)S(1)}, bf16[32,2,8,512]{3,2,1,0:T(8,128)(2,1)S(1)}, u32[]{:S(2)}, u32[]{:S(2)}) collective-permute-start(bf16[32,2,8,512]{3,2,1,0:T(8,128)(2,1)S(1)} %all_to_all.10.mine_ref), channel_id=1, source_target_pairs={{0,1},{1,0},{2,3},{3,2},{4,5},{5,4},{6,7},{7,6},{8,9},{9,8},{10,11... | collective-permute-start | bytes 1572872 | tf_op jit(solution)/shard_map/ppermute | solution.py:389
  105.4 17.3 %all-to-all-start.1 = ((bf16[32,8,512]{2,1,0:T(8,128)(2,1)}), bf16[32,8,512]{2,1,0:T(8,128)(2,1)S(1)}, u32[]{:S(2)}, u32[]{:S(2)}) async-start(bf16[32,8,512]{2,1,0:T(8,128)(2,1)} %get-tuple-element.19), calls=%async_computation.1 | async-start | bytes 524288 | tf_op jit(solution)/shard_map/all_to_all | solution.py:381

commit v7 on v6

--- a/solution.py
+++ b/solution.py
@@ -291,12 +291,29 @@
     return parts_ref.at[lax.rem(here_ref[0] + offset, parts_ref.shape[0])]
 
 
-def picked(here, parts, offsets):
-    def kernel(here_ref, parts_ref, *refs):
-        outs, sems = refs[: len(offsets)], refs[len(offsets)]
+def picked(here, parts, offset):
+    def kernel(here_ref, parts_ref, out_ref, sem):
+        copy = pltpu.make_async_copy(part_of(parts_ref, here_ref, offset), out_ref, sem.at[0])
+        copy.start()
+        copy.wait()
+
+    return pl.pallas_call(
+        kernel,
+        out_shape=jax.ShapeDtypeStruct(parts.shape[1:], BF16),
+        in_specs=[smem(), pl.BlockSpec(memory_space=pltpu.HBM)],
+        out_specs=vmem(),
+        scratch_shapes=[pltpu.SemaphoreType.DMA((1,))],
+        compiler_params=params(PICK_LIMIT),
+        cost_estimate=cost(0, 4 * parts[0].size),
+        name="picked",
+    )(here, parts)
+
+
+def staged(here, parts):
+    def kernel(here_ref, parts_ref, all_ref, own_ref, sems):
         copies = [
-            pltpu.make_async_copy(part_of(parts_ref, here_ref, offset), out, sems.at[k])
-            for k, (offset, out) in enumerate(zip(offsets, outs))
+            pltpu.make_async_copy(parts_ref, all_ref, sems.at[0]),
+            pltpu.make_async_copy(part_of(parts_ref, here_ref, 0), own_ref, sems.at[1]),
         ]
         for copy in copies:
             copy.start()
@@ -305,32 +322,17 @@
 
     return pl.pallas_call(
         kernel,
-        out_shape=[jax.ShapeDtypeStruct(parts.shape[1:], BF16)] * len(offsets),
+        out_shape=[
+            jax.ShapeDtypeStruct(parts.shape, BF16),
+            jax.ShapeDtypeStruct(parts.shape[1:], BF16),
+        ],
         in_specs=[smem(), pl.BlockSpec(memory_space=pltpu.HBM)],
-        out_specs=[vmem()] * len(offsets),
-        scratch_shapes=[pltpu.SemaphoreType.DMA((len(offsets),))],
-        compiler_params=params(PICK_LIMIT),
-        cost_estimate=cost(0, 4 * parts[0].size * len(offsets)),
-        name="picked",
-    )(here, parts)
-
-
-def staged(parts):
-    def kernel(parts_ref, out_ref, sem):
-        copy = pltpu.make_async_copy(parts_ref, out_ref, sem.at[0])
-        copy.start()
-        copy.wait()
-
-    return pl.pallas_call(
-        kernel,
-        out_shape=jax.ShapeDtypeStruct(parts.shape, BF16),
-        in_specs=[pl.BlockSpec(memory_space=pltpu.HBM)],
-        out_specs=vmem(),
-        scratch_shapes=[pltpu.SemaphoreType.DMA((1,))],
+        out_specs=[vmem(), vmem()],
+        scratch_shapes=[pltpu.SemaphoreType.DMA((2,))],
         compiler_params=params(STAGE_LIMIT),
         cost_estimate=cost(0, 4 * parts.size),
         name="staged",
-    )(parts)
+    )(here, parts)
 
 
 def added(here, total, parts, offset):
@@ -355,9 +357,11 @@
     lowering = [(i, (i - 1) % n) for i in range(n)]
     hops = n // 2
     first = 2 * hops + 1 - n
-    below, above, own = picked(here, parts, (hops, (first - hops) % n, 0))
+    below = picked(here, parts, hops)
     below, parts = lax.optimization_barrier((below, parts))
-    parts = staged(parts)
+    above = picked(here, parts, (first - hops) % n)
+    above, parts = lax.optimization_barrier((above, parts))
+    parts, own = staged(here, parts)
     for step in range(hops):
         if step > 0:
             below = added(here, below, parts, hops - step)

time: 125 us -> 124 us (level)
  waiting for transfers between devices: 31.7 us -> 28.2 us
  starting transfers between devices: 53.3 us -> 55 us
  Pallas kernels: 14.7 us -> 16.1 us
    ppermute x6, waiting for transfers between devices: 18.9 us -> 13.3 us  [ring_terms(): below = lax.ppermute(below, axis, raising)]
    ppermute x5, waiting for transfers between devices: 0.01 us -> 2.18 us  [ring_terms(): above = lax.ppermute(above, axis, lowering)]
    ppermute x5, starting transfers between devices: 32.8 us -> 34.5 us  [ring_terms(): above = lax.ppermute(above, axis, lowering)]
    pallas_call x2 -> x3, Pallas kernels: 3.92 us -> 5.26 us  [the longest x2 3.34 us: picked(): pl.pallas_call(kernel, out_shape=jax.ShapeDtypeStruct(parts.shape[1:], BF...]
  transfers between devices with their start and end apart: 13 -> 13, of which waited for: 8 -> 12; matrix products, arithmetic and copies ran while one was open for 0% -> 0% of each run, Pallas kernels for 5% -> 6%
where the time goes in v7:
time: 124 us
  starting transfers between devices  55 us (44%)
  waiting for transfers between devices  28.2 us (23%)
  blocking collectives  23.6 us (19%)
  Pallas kernels  16.1 us (13%)
    ppermute x5, starting transfers between devices, ring_terms(): above = lax.ppermute(above, axis, lowering)  34.5 us
    all_to_all x1, blocking collectives, exchanged(): lax.all_to_all(x, 'fsdp', split_axis=0, concat_axis=0, axis_index_groups=...  23.6 us
    ppermute x6, starting transfers between devices, ring_terms(): below = lax.ppermute(below, axis, raising)  13.9 us
    ppermute x6, waiting for transfers between devices, ring_terms(): below = lax.ppermute(below, axis, raising)  13.3 us
    all_to_all x1, waiting for transfers between devices, exchanged(): lax.all_to_all(x, 'fsdp', split_axis=0, concat_axis=0, axis_index_groups=...  10.8 us
    all_to_all x1, starting transfers between devices, exchanged(): lax.all_to_all(x, 'fsdp', split_axis=0, concat_axis=0, axis_index_groups=...  4.67 us
    pallas_call x1, Pallas kernels, first_work(): pl.pallas_call(kernel, out_shape=(jax.ShapeDtypeStruct((BLK, BLK), BF16),...  4.07 us
    pallas_call x2, Pallas kernels, picked(): pl.pallas_call(kernel, out_shape=jax.ShapeDtypeStruct(parts.shape[1:], BF...  3.34 us
  transfers between devices with their start and end apart: 13, of which 12 were waited for; matrix products, arithmetic and copies ran while one was open for 0% of the time, Pallas kernels for 6%

profile of v7, /device:TPU:8, one launch (start us, length us, event | category | flops | bytes accessed | tf_op | source)
XLA Modules:
  0.0 123.7 jit_solution(6198161061749143446)
XLA Ops:
  0.6 1.7 %picked.2 = bf16[8,16,1024]{2,1,0:T(8,128)(2,1)} custom-call(s32[1]{0:T(128)} %bitcast.here_ref, bf16[12,8,16,1024]{3,2,1,0:T(8,128)(2,1)} %bitcast.5), custom_call_target="tpu_custom_call" | custom-call | bytes 524288 | tf_op jit(solution)/shard_map/picked/pallas_call | solution.py:300
  2.3 4.3 %collective-permute-start = (bf16[8,16,1024]{2,1,0:T(8,128)(2,1)}, bf16[8,16,1024]{2,1,0:T(8,128)(2,1)S(1)}, u32[]{:S(2)}, u32[]{:S(2)}) collective-permute-start(bf16[8,16,1024]{2,1,0:T(8,128)(2,1)} %picked.2), channel_id=1, source_target_pairs={{0,64},{64,128},{128,192},{192,256},{256,320},{320,384},{384,448},... | collective-permute-start | bytes 786440 | tf_op jit(solution)/shard_map/ppermute | solution.py:368
  6.6 1.7 %picked.3 = bf16[8,16,1024]{2,1,0:T(8,128)(2,1)} custom-call(s32[1]{0:T(128)} %bitcast.here_ref, bf16[12,8,16,1024]{3,2,1,0:T(8,128)(2,1)} %bitcast.6), custom_call_target="tpu_custom_call" | custom-call | bytes 524288 | tf_op jit(solution)/shard_map/picked/pallas_call | solution.py:300
  8.3 12.2 %collective-permute-start.6 = (bf16[8,16,1024]{2,1,0:T(8,128)(2,1)}, bf16[8,16,1024]{2,1,0:T(8,128)(2,1)S(1)}, u32[]{:S(2)}, u32[]{:S(2)}) collective-permute-start(bf16[8,16,1024]{2,1,0:T(8,128)(2,1)} %picked.3), channel_id=1, source_target_pairs={{0,704},{64,0},{128,64},{192,128},{256,192},{320,256},{384,320},{4... | collective-permute-start | bytes 786440 | tf_op jit(solution)/shard_map/ppermute | solution.py:372
  20.5 1.9 %staged.1 = (bf16[12,8,16,1024]{3,2,1,0:T(8,128)(2,1)S(1)}, bf16[8,16,1024]{2,1,0:T(8,128)(2,1)S(1)}) custom-call(s32[1]{0:T(128)} %bitcast.here_ref, bf16[12,8,16,1024]{3,2,1,0:T(8,128)(2,1)} %bitcast.7), custom_call_target="tpu_custom_call" | custom-call | bytes 6291456 | tf_op jit(solution)/shard_map/staged/pallas_call | solution.py:323
  23.5 1.9 %collective-permute-start.1 = (bf16[8,16,1024]{2,1,0:T(8,128)(2,1)S(1)}, bf16[8,16,1024]{2,1,0:T(8,128)(2,1)S(1)}, u32[]{:S(2)}, u32[]{:S(2)}) collective-permute-start(bf16[8,16,1024]{2,1,0:T(8,128)(2,1)S(1)} %added.9), channel_id=1, source_target_pairs={{0,64},{64,128},{128,192},{192,256},{256,320},{320,384},{384,448},... | collective-permute-start | bytes 786440 | tf_op jit(solution)/shard_map/ppermute | solution.py:368
  26.4 5.5 %collective-permute-start.7 = (bf16[8,16,1024]{2,1,0:T(8,128)(2,1)S(1)}, bf16[8,16,1024]{2,1,0:T(8,128)(2,1)S(1)}, u32[]{:S(2)}, u32[]{:S(2)}) collective-permute-start(bf16[8,16,1024]{2,1,0:T(8,128)(2,1)S(1)} %added.14), channel_id=1, source_target_pairs={{0,704},{64,0},{128,64},{192,128},{256,192},{320,256},{384,320},{4... | collective-permute-start | bytes 786440 | tf_op jit(solution)/shard_map/ppermute | solution.py:372
  31.9 2.1 %collective-permute-done.1.total_ref = bf16[8,16,1024]{2,1,0:T(8,128)(2,1)S(1)} collective-permute-done((bf16[8,16,1024]{2,1,0:T(8,128)(2,1)S(1)}, bf16[8,16,1024]{2,1,0:T(8,128)(2,1)S(1)}, u32[]{:S(2)}, u32[]{:S(2)}) %collective-permute-start.1) | collective-permute-done | bytes 262176 | tf_op jit(solution)/shard_map/ppermute | solution.py:368
  34.1 1.9 %collective-permute-start.2 = (bf16[8,16,1024]{2,1,0:T(8,128)(2,1)S(1)}, bf16[8,16,1024]{2,1,0:T(8,128)(2,1)S(1)}, u32[]{:S(2)}, u32[]{:S(2)}) collective-permute-start(bf16[8,16,1024]{2,1,0:T(8,128)(2,1)S(1)} %added.10), channel_id=1, source_target_pairs={{0,64},{64,128},{128,192},{192,256},{256,320},{320,384},{384,448},... | collective-permute-start | bytes 786440 | tf_op jit(solution)/shard_map/ppermute | solution.py:368
  36.7 5.6 %collective-permute-start.8 = (bf16[8,16,1024]{2,1,0:T(8,128)(2,1)S(1)}, bf16[8,16,1024]{2,1,0:T(8,128)(2,1)S(1)}, u32[]{:S(2)}, u32[]{:S(2)}) collective-permute-start(bf16[8,16,1024]{2,1,0:T(8,128)(2,1)S(1)} %added.15), channel_id=1, source_target_pairs={{0,704},{64,0},{128,64},{192,128},{256,192},{320,256},{384,320},{4... | collective-permute-start | bytes 786440 | tf_op jit(solution)/shard_map/ppermute | solution.py:372
  43.9 1.9 %collective-permute-start.3 = (bf16[8,16,1024]{2,1,0:T(8,128)(2,1)S(1)}, bf16[8,16,1024]{2,1,0:T(8,128)(2,1)S(1)}, u32[]{:S(2)}, u32[]{:S(2)}) collective-permute-start(bf16[8,16,1024]{2,1,0:T(8,128)(2,1)S(1)} %added.11), channel_id=1, source_target_pairs={{0,64},{64,128},{128,192},{192,256},{256,320},{320,384},{384,448},... | collective-permute-start | bytes 786440 | tf_op jit(solution)/shard_map/ppermute | solution.py:368
  46.2 5.6 %collective-permute-start.9 = (bf16[8,16,1024]{2,1,0:T(8,128)(2,1)S(1)}, bf16[8,16,1024]{2,1,0:T(8,128)(2,1)S(1)}, u32[]{:S(2)}, u32[]{:S(2)}) collective-permute-start(bf16[8,16,1024]{2,1,0:T(8,128)(2,1)S(1)} %added.16), channel_id=1, source_target_pairs={{0,704},{64,0},{128,64},{192,128},{256,192},{320,256},{384,320},{4... | collective-permute-start | bytes 786440 | tf_op jit(solution)/shard_map/ppermute | solution.py:372
  53.5 1.9 %collective-permute-start.4 = (bf16[8,16,1024]{2,1,0:T(8,128)(2,1)S(1)}, bf16[8,16,1024]{2,1,0:T(8,128)(2,1)S(1)}, u32[]{:S(2)}, u32[]{:S(2)}) collective-permute-start(bf16[8,16,1024]{2,1,0:T(8,128)(2,1)S(1)} %added.12), channel_id=1, source_target_pairs={{0,64},{64,128},{128,192},{192,256},{256,320},{320,384},{384,448},... | collective-permute-start | bytes 786440 | tf_op jit(solution)/shard_map/ppermute | solution.py:368
  55.8 5.6 %collective-permute-start.10 = (bf16[8,16,1024]{2,1,0:T(8,128)(2,1)S(1)}, bf16[8,16,1024]{2,1,0:T(8,128)(2,1)S(1)}, u32[]{:S(2)}, u32[]{:S(2)}) collective-permute-start(bf16[8,16,1024]{2,1,0:T(8,128)(2,1)S(1)} %added.17), channel_id=1, source_target_pairs={{0,704},{64,0},{128,64},{192,128},{256,192},{320,256},{384,320},{4... | collective-permute-start | bytes 786440 | tf_op jit(solution)/shard_map/ppermute | solution.py:372
  63.0 1.9 %collective-permute-start.5 = (bf16[8,16,1024]{2,1,0:T(8,128)(2,1)S(1)}, bf16[8,16,1024]{2,1,0:T(8,128)(2,1)S(1)}, u32[]{:S(2)}, u32[]{:S(2)}) collective-permute-start(bf16[8,16,1024]{2,1,0:T(8,128)(2,1)S(1)} %added.13), channel_id=1, source_target_pairs={{0,64},{64,128},{128,192},{192,256},{256,320},{320,384},{384,448},... | collective-permute-start | bytes 786440 | tf_op jit(solution)/shard_map/ppermute | solution.py:368
  64.9 1.9 %assigned.1 = (s32[32]{0:T(128)S(1)}, s32[32]{0:T(128)S(1)}, s32[1]{0:T(128)}) custom-call(s32[1]{0:T(128)} %bitcast.here_ref, s32[1]{0:T(128)} %bitcast.1.slot_ref, s32[12,64]{1,0:T(8,128)S(1)} %copy-done), custom_call_target="tpu_custom_call" | custom-call | bytes 1024 | tf_op jit(solution)/shard_map/assigned/pallas_call | solution.py:62
  66.9 5.6 %collective-permute-done.5.below_ref = bf16[8,16,1024]{2,1,0:T(8,128)(2,1)S(1)} collective-permute-done((bf16[8,16,1024]{2,1,0:T(8,128)(2,1)S(1)}, bf16[8,16,1024]{2,1,0:T(8,128)(2,1)S(1)}, u32[]{:S(2)}, u32[]{:S(2)}) %collective-permute-start.5) | collective-permute-done | bytes 262176 | tf_op jit(solution)/shard_map/ppermute | solution.py:368
  73.4 23.6 %all_to_all.10.mine_ref = bf16[32,2,8,512]{3,2,1,0:T(8,128)(2,1)S(1)} all-to-all(bf16[32,2,8,512]{3,2,1,0:T(8,128)(2,1)S(1)} %outgoing.1), channel_id=1, replica_groups={{0,2,4,6,8,10,12,14,16,18,20,22,24,26,28,30,32,34,36,38,40,42,44,46,48,..., dimensions={0} | all-to-all | bytes 1048576 | tf_op jit(solution)/shard_map/all_to_all | solution.py:385
  97.0 1.9 %collective-permute-start.11 = (bf16[32,2,8,512]{3,2,1,0:T(8,128)(2,1)S(1)}, bf16[32,2,8,512]{3,2,1,0:T(8,128)(2,1)S(1)}, u32[]{:S(2)}, u32[]{:S(2)}) collective-permute-start(bf16[32,2,8,512]{3,2,1,0:T(8,128)(2,1)S(1)} %all_to_all.10.mine_ref), channel_id=1, source_target_pairs={{0,1},{1,0},{2,3},{3,2},{4,5},{5,4},{6,7},{7,6},{8,9},{9,8},{10,11... | collective-permute-start | bytes 1572872 | tf_op jit(solution)/shard_map/ppermute | solution.py:393
  98.9 1.9 %collective-permute-done.11.other_ref = bf16[32,2,8,512]{3,2,1,0:T(8,128)(2,1)S(1)} collective-permute-done((bf16[32,2,8,512]{3,2,1,0:T(8,128)(2,1)S(1)}, bf16[32,2,8,512]{3,2,1,0:T(8,128)(2,1)S(1)}, u32[]{:S(2)}, u32[]{:S(2)}) %collective-permute-start.11) | collective-permute-done | bytes 524320 | tf_op jit(solution)/shard_map/ppermute | solution.py:393
  100.8 4.1 %first_work.1 = (bf16[512,512]{1,0:T(8,128)(2,1)S(1)}, bf16[32,8,512]{2,1,0:T(8,128)(2,1)}) custom-call(s32[1]{0:T(128)S(6)} %select_n.7.core_ref, bf16[32,2,8,512]{3,2,1,0:T(8,128)(2,1)S(1)} %all_to_all.10.mine_ref, bf16[32,2,8,512]{3,2,1,0:T(8,128)(2,1)S(1)} %collective-permute-done.11.other_ref), custom_call_target="tpu_custom_call" | custom-call | flops 1879048192 | bytes 2097152 | tf_op jit(solution)/shard_map/first_work/pallas_call | solution.py:237
  104.9 4.7 %all-to-all-start.1 = ((bf16[32,8,512]{2,1,0:T(8,128)(2,1)}), bf16[32,8,512]{2,1,0:T(8,128)(2,1)S(1)}, u32[]{:S(2)}, u32[]{:S(2)}) async-start(bf16[32,8,512]{2,1,0:T(8,128)(2,1)} %get-tuple-element.21), calls=%async_computation.1 | async-start | bytes 524288 | tf_op jit(solution)/shard_map/all_to_all | solution.py:385
  109.5 1.7 %slot_work.1 = bf16[2,512,512]{2,1,0:T(8,128)(2,1)} custom-call(s32[1]{0:T(128)} %get-tuple-element.22.mode_ref, s32[1]{0:T(128)S(6)} %select_n.7.core_ref, bf16[32,2,8,512]{3,2,1,0:T(8,128)(2,1)S(1)} %all_to_all.10.mine_ref, bf16[32,2,8,512]{3,2,1,0:T(8,128)(2,1)S(1)} %collective-permute-done.11.other_ref, bf16[512,512]{1,0:T(8,128)(2,1)S(1)} %get-tuple-element.23.right_ref), custom_call_target="tpu_custom_call" | custom-call | flops 2684354560 | bytes 2097152 | tf_op jit(solution)/shard_map/slot_work/pallas_call | solution.py:278
  111.3 10.8 %all-to-all-done.1.x_ref = bf16[32,8,512]{2,1,0:T(8,128)(2,1)S(1)} async-done(((bf16[32,8,512]{2,1,0:T(8,128)(2,1)}), bf16[32,8,512]{2,1,0:T(8,128)(2,1)S(1)}, u32[]{:S(2)}, u32[]{:S(2)}) %all-to-all-start.1) | async-done | bytes 262176 | tf_op jit(solution)/shard_map/all_to_all | solution.py:385
  (22 shorter events, 10.9 us)
Async XLA Ops:
  2.3 21.1 %collective-permute-start = (bf16[8,16,1024]{2,1,0:T(8,128)(2,1)}, bf16[8,16,1024]{2,1,0:T(8,128)(2,1)S(1)}, u32[]{:S(2)}, u32[]{:S(2)}) collective-permute-start(bf16[8,16,1024]{2,1,0:T(8,128)(2,1)} %picked.2), channel_id=1, source_target_pairs={{0,64},{64,128},{128,192},{192,256},{256,320},{320,384},{384,448},... | collective-permute-start | bytes 786440 | tf_op jit(solution)/shard_map/ppermute | solution.py:368
  8.3 18.1 %collective-permute-start.6 = (bf16[8,16,1024]{2,1,0:T(8,128)(2,1)}, bf16[8,16,1024]{2,1,0:T(8,128)(2,1)S(1)}, u32[]{:S(2)}, u32[]{:S(2)}) collective-permute-start(bf16[8,16,1024]{2,1,0:T(8,128)(2,1)} %picked.3), channel_id=1, source_target_pairs={{0,704},{64,0},{128,64},{192,128},{256,192},{320,256},{384,320},{4... | collective-permute-start | bytes 786440 | tf_op jit(solution)/shard_map/ppermute | solution.py:372
  23.5 10.6 %collective-permute-start.1 = (bf16[8,16,1024]{2,1,0:T(8,128)(2,1)S(1)}, bf16[8,16,1024]{2,1,0:T(8,128)(2,1)S(1)}, u32[]{:S(2)}, u32[]{:S(2)}) collective-permute-start(bf16[8,16,1024]{2,1,0:T(8,128)(2,1)S(1)} %added.9), channel_id=1, source_target_pairs={{0,64},{64,128},{128,192},{192,256},{256,320},{320,384},{384,448},... | collective-permute-start | bytes 786440 | tf_op jit(solution)/shard_map/ppermute | solution.py:368
  26.4 10.2 %collective-permute-start.7 = (bf16[8,16,1024]{2,1,0:T(8,128)(2,1)S(1)}, bf16[8,16,1024]{2,1,0:T(8,128)(2,1)S(1)}, u32[]{:S(2)}, u32[]{:S(2)}) collective-permute-start(bf16[8,16,1024]{2,1,0:T(8,128)(2,1)S(1)} %added.14), channel_id=1, source_target_pairs={{0,704},{64,0},{128,64},{192,128},{256,192},{320,256},{384,320},{4... | collective-permute-start | bytes 786440 | tf_op jit(solution)/shard_map/ppermute | solution.py:372
  34.1 9.7 %collective-permute-start.2 = (bf16[8,16,1024]{2,1,0:T(8,128)(2,1)S(1)}, bf16[8,16,1024]{2,1,0:T(8,128)(2,1)S(1)}, u32[]{:S(2)}, u32[]{:S(2)}) collective-permute-start(bf16[8,16,1024]{2,1,0:T(8,128)(2,1)S(1)} %added.10), channel_id=1, source_target_pairs={{0,64},{64,128},{128,192},{192,256},{256,320},{320,384},{384,448},... | collective-permute-start | bytes 786440 | tf_op jit(solution)/shard_map/ppermute | solution.py:368
  36.7 9.5 %collective-permute-start.8 = (bf16[8,16,1024]{2,1,0:T(8,128)(2,1)S(1)}, bf16[8,16,1024]{2,1,0:T(8,128)(2,1)S(1)}, u32[]{:S(2)}, u32[]{:S(2)}) collective-permute-start(bf16[8,16,1024]{2,1,0:T(8,128)(2,1)S(1)} %added.15), channel_id=1, source_target_pairs={{0,704},{64,0},{128,64},{192,128},{256,192},{320,256},{384,320},{4... | collective-permute-start | bytes 786440 | tf_op jit(solution)/shard_map/ppermute | solution.py:372
  43.9 9.5 %collective-permute-start.3 = (bf16[8,16,1024]{2,1,0:T(8,128)(2,1)S(1)}, bf16[8,16,1024]{2,1,0:T(8,128)(2,1)S(1)}, u32[]{:S(2)}, u32[]{:S(2)}) collective-permute-start(bf16[8,16,1024]{2,1,0:T(8,128)(2,1)S(1)} %added.11), channel_id=1, source_target_pairs={{0,64},{64,128},{128,192},{192,256},{256,320},{320,384},{384,448},... | collective-permute-start | bytes 786440 | tf_op jit(solution)/shard_map/ppermute | solution.py:368
  46.2 9.5 %collective-permute-start.9 = (bf16[8,16,1024]{2,1,0:T(8,128)(2,1)S(1)}, bf16[8,16,1024]{2,1,0:T(8,128)(2,1)S(1)}, u32[]{:S(2)}, u32[]{:S(2)}) collective-permute-start(bf16[8,16,1024]{2,1,0:T(8,128)(2,1)S(1)} %added.16), channel_id=1, source_target_pairs={{0,704},{64,0},{128,64},{192,128},{256,192},{320,256},{384,320},{4... | collective-permute-start | bytes 786440 | tf_op jit(solution)/shard_map/ppermute | solution.py:372
  53.4 11.5 %copy-start = (s32[12,64]{1,0:T(8,128)S(1)}, s32[12,64]{1,0:T(8,128)}, u32[]{:S(2)}) copy-start(s32[12,64]{1,0:T(8,128)} %table_ref.1) | copy-start | bytes 9220
  53.5 9.5 %collective-permute-start.4 = (bf16[8,16,1024]{2,1,0:T(8,128)(2,1)S(1)}, bf16[8,16,1024]{2,1,0:T(8,128)(2,1)S(1)}, u32[]{:S(2)}, u32[]{:S(2)}) collective-permute-start(bf16[8,16,1024]{2,1,0:T(8,128)(2,1)S(1)} %added.12), channel_id=1, source_target_pairs={{0,64},{64,128},{128,192},{192,256},{256,320},{320,384},{384,448},... | collective-permute-start | bytes 786440 | tf_op jit(solution)/shard_map/ppermute | solution.py:368
  55.8 11.1 %collective-permute-start.10 = (bf16[8,16,1024]{2,1,0:T(8,128)(2,1)S(1)}, bf16[8,16,1024]{2,1,0:T(8,128)(2,1)S(1)}, u32[]{:S(2)}, u32[]{:S(2)}) collective-permute-start(bf16[8,16,1024]{2,1,0:T(8,128)(2,1)S(1)} %added.17), channel_id=1, source_target_pairs={{0,704},{64,0},{128,64},{192,128},{256,192},{320,256},{384,320},{4... | collective-permute-start | bytes 786440 | tf_op jit(solution)/shard_map/ppermute | solution.py:372
  63.0 9.5 %collective-permute-start.5 = (bf16[8,16,1024]{2,1,0:T(8,128)(2,1)S(1)}, bf16[8,16,1024]{2,1,0:T(8,128)(2,1)S(1)}, u32[]{:S(2)}, u32[]{:S(2)}) collective-permute-start(bf16[8,16,1024]{2,1,0:T(8,128)(2,1)S(1)} %added.13), channel_id=1, source_target_pairs={{0,64},{64,128},{128,192},{192,256},{256,320},{320,384},{384,448},... | collective-permute-start | bytes 786440 | tf_op jit(solution)/shard_map/ppermute | solution.py:368
  97.0 3.8 %collective-permute-start.11 = (bf16[32,2,8,512]{3,2,1,0:T(8,128)(2,1)S(1)}, bf16[32,2,8,512]{3,2,1,0:T(8,128)(2,1)S(1)}, u32[]{:S(2)}, u32[]{:S(2)}) collective-permute-start(bf16[32,2,8,512]{3,2,1,0:T(8,128)(2,1)S(1)} %all_to_all.10.mine_ref), channel_id=1, source_target_pairs={{0,1},{1,0},{2,3},{3,2},{4,5},{5,4},{6,7},{7,6},{8,9},{9,8},{10,11... | collective-permute-start | bytes 1572872 | tf_op jit(solution)/shard_map/ppermute | solution.py:393
  104.9 17.3 %all-to-all-start.1 = ((bf16[32,8,512]{2,1,0:T(8,128)(2,1)}), bf16[32,8,512]{2,1,0:T(8,128)(2,1)S(1)}, u32[]{:S(2)}, u32[]{:S(2)}) async-start(bf16[32,8,512]{2,1,0:T(8,128)(2,1)} %get-tuple-element.21), calls=%async_computation.1 | async-start | bytes 524288 | tf_op jit(solution)/shard_map/all_to_all | solution.py:385

commit v8 on v7

--- a/solution.py
+++ b/solution.py
@@ -14,7 +14,7 @@
 F32 = jnp.float32
 BF16 = jnp.bfloat16
 VMEM_LIMIT = 24 * 1024 * 1024
-PICK_LIMIT = 61 * 1024 * 1024
+PICK_LIMIT = 53 * 1024 * 1024
 STAGE_LIMIT = 50 * 1024 * 1024
 
 

time: 124 us -> 123 us (level)
  Pallas kernels: 16.1 us -> 14.6 us
  waiting for transfers between devices: 28.2 us -> 29.6 us
    ppermute x6, waiting for transfers between devices: 13.3 us -> 16.6 us  [ring_terms(): below = lax.ppermute(below, axis, raising)]
    ppermute x5, waiting for transfers between devices: 2.18 us -> 0.17 us  [ring_terms(): above = lax.ppermute(above, axis, lowering)]
    pallas_call x2, Pallas kernels: 3.34 us -> 1.94 us  [picked(): pl.pallas_call(kernel, out_shape=jax.ShapeDtypeStruct(parts.shape[1:], BF...]
  transfers between devices with their start and end apart: 13 -> 13, of which waited for: 12 -> 9; matrix products, arithmetic and copies ran while one was open for 0% -> 0% of each run, Pallas kernels for 6% -> 6%
where the time goes in v8:
time: 123 us
  starting transfers between devices  54.1 us (44%)
  waiting for transfers between devices  29.6 us (24%)
  blocking collectives  23.6 us (19%)
  Pallas kernels  14.6 us (12%)
    ppermute x5, starting transfers between devices, ring_terms(): above = lax.ppermute(above, axis, lowering)  33.7 us
    all_to_all x1, blocking collectives, exchanged(): lax.all_to_all(x, 'fsdp', split_axis=0, concat_axis=0, axis_index_groups=...  23.6 us
    ppermute x6, waiting for transfers between devices, ring_terms(): below = lax.ppermute(below, axis, raising)  16.6 us
    ppermute x6, starting transfers between devices, ring_terms(): below = lax.ppermute(below, axis, raising)  13.9 us
    all_to_all x1, waiting for transfers between devices, exchanged(): lax.all_to_all(x, 'fsdp', split_axis=0, concat_axis=0, axis_index_groups=...  11 us
    all_to_all x1, starting transfers between devices, exchanged(): lax.all_to_all(x, 'fsdp', split_axis=0, concat_axis=0, axis_index_groups=...  4.67 us
    pallas_call x1, Pallas kernels, first_work(): pl.pallas_call(kernel, out_shape=(jax.ShapeDtypeStruct((BLK, BLK), BF16),...  4.06 us
  transfers between devices with their start and end apart: 13, of which 9 were waited for; matrix products, arithmetic and copies ran while one was open for 0% of the time, Pallas kernels for 6%

profile of v8, /device:TPU:8, one launch (start us, length us, event | category | flops | bytes accessed | tf_op | source)
XLA Modules:
  0.0 122.8 jit_solution(6850266784270861764)
XLA Ops:
  1.6 4.3 %collective-permute-start = (bf16[8,16,1024]{2,1,0:T(8,128)(2,1)S(1)}, bf16[8,16,1024]{2,1,0:T(8,128)(2,1)S(1)}, u32[]{:S(2)}, u32[]{:S(2)}) collective-permute-start(bf16[8,16,1024]{2,1,0:T(8,128)(2,1)S(1)} %picked.2), channel_id=1, source_target_pairs={{0,64},{64,128},{128,192},{192,256},{256,320},{320,384},{384,448},... | collective-permute-start | bytes 786440 | tf_op jit(solution)/shard_map/ppermute | solution.py:368
  6.9 12.2 %collective-permute-start.6 = (bf16[8,16,1024]{2,1,0:T(8,128)(2,1)S(1)}, bf16[8,16,1024]{2,1,0:T(8,128)(2,1)S(1)}, u32[]{:S(2)}, u32[]{:S(2)}) collective-permute-start(bf16[8,16,1024]{2,1,0:T(8,128)(2,1)S(1)} %picked.3), channel_id=1, source_target_pairs={{0,704},{64,0},{128,64},{192,128},{256,192},{320,256},{384,320},{4... | collective-permute-start | bytes 786440 | tf_op jit(solution)/shard_map/ppermute | solution.py:372
  19.1 1.9 %staged.1 = (bf16[12,8,16,1024]{3,2,1,0:T(8,128)(2,1)S(1)}, bf16[8,16,1024]{2,1,0:T(8,128)(2,1)S(1)}) custom-call(s32[1]{0:T(128)} %bitcast.here_ref, bf16[12,8,16,1024]{3,2,1,0:T(8,128)(2,1)} %bitcast.7), custom_call_target="tpu_custom_call" | custom-call | bytes 6291456 | tf_op jit(solution)/shard_map/staged/pallas_call | solution.py:323
  22.6 1.9 %collective-permute-start.1 = (bf16[8,16,1024]{2,1,0:T(8,128)(2,1)S(1)}, bf16[8,16,1024]{2,1,0:T(8,128)(2,1)S(1)}, u32[]{:S(2)}, u32[]{:S(2)}) collective-permute-start(bf16[8,16,1024]{2,1,0:T(8,128)(2,1)S(1)} %added.9), channel_id=1, source_target_pairs={{0,64},{64,128},{128,192},{192,256},{256,320},{320,384},{384,448},... | collective-permute-start | bytes 786440 | tf_op jit(solution)/shard_map/ppermute | solution.py:368
  24.7 5.6 %collective-permute-start.7 = (bf16[8,16,1024]{2,1,0:T(8,128)(2,1)S(1)}, bf16[8,16,1024]{2,1,0:T(8,128)(2,1)S(1)}, u32[]{:S(2)}, u32[]{:S(2)}) collective-permute-start(bf16[8,16,1024]{2,1,0:T(8,128)(2,1)S(1)} %added.14), channel_id=1, source_target_pairs={{0,704},{64,0},{128,64},{192,128},{256,192},{320,256},{384,320},{4... | collective-permute-start | bytes 786440 | tf_op jit(solution)/shard_map/ppermute | solution.py:372
  30.3 2.8 %collective-permute-done.1.total_ref = bf16[8,16,1024]{2,1,0:T(8,128)(2,1)S(1)} collective-permute-done((bf16[8,16,1024]{2,1,0:T(8,128)(2,1)S(1)}, bf16[8,16,1024]{2,1,0:T(8,128)(2,1)S(1)}, u32[]{:S(2)}, u32[]{:S(2)}) %collective-permute-start.1) | collective-permute-done | bytes 262176 | tf_op jit(solution)/shard_map/ppermute | solution.py:368
  33.2 1.9 %collective-permute-start.2 = (bf16[8,16,1024]{2,1,0:T(8,128)(2,1)S(1)}, bf16[8,16,1024]{2,1,0:T(8,128)(2,1)S(1)}, u32[]{:S(2)}, u32[]{:S(2)}) collective-permute-start(bf16[8,16,1024]{2,1,0:T(8,128)(2,1)S(1)} %added.10), channel_id=1, source_target_pairs={{0,64},{64,128},{128,192},{192,256},{256,320},{320,384},{384,448},... | collective-permute-start | bytes 786440 | tf_op jit(solution)/shard_map/ppermute | solution.py:368
  35.3 5.4 %collective-permute-start.8 = (bf16[8,16,1024]{2,1,0:T(8,128)(2,1)S(1)}, bf16[8,16,1024]{2,1,0:T(8,128)(2,1)S(1)}, u32[]{:S(2)}, u32[]{:S(2)}) collective-permute-start(bf16[8,16,1024]{2,1,0:T(8,128)(2,1)S(1)} %added.15), channel_id=1, source_target_pairs={{0,704},{64,0},{128,64},{192,128},{256,192},{320,256},{384,320},{4... | collective-permute-start | bytes 786440 | tf_op jit(solution)/shard_map/ppermute | solution.py:372
  40.7 2.2 %collective-permute-done.2.total_ref = bf16[8,16,1024]{2,1,0:T(8,128)(2,1)S(1)} collective-permute-done((bf16[8,16,1024]{2,1,0:T(8,128)(2,1)S(1)}, bf16[8,16,1024]{2,1,0:T(8,128)(2,1)S(1)}, u32[]{:S(2)}, u32[]{:S(2)}) %collective-permute-start.2) | collective-permute-done | bytes 262176 | tf_op jit(solution)/shard_map/ppermute | solution.py:368
  43.0 1.9 %collective-permute-start.3 = (bf16[8,16,1024]{2,1,0:T(8,128)(2,1)S(1)}, bf16[8,16,1024]{2,1,0:T(8,128)(2,1)S(1)}, u32[]{:S(2)}, u32[]{:S(2)}) collective-permute-start(bf16[8,16,1024]{2,1,0:T(8,128)(2,1)S(1)} %added.11), channel_id=1, source_target_pairs={{0,64},{64,128},{128,192},{192,256},{256,320},{320,384},{384,448},... | collective-permute-start | bytes 786440 | tf_op jit(solution)/shard_map/ppermute | solution.py:368
  45.0 5.2 %collective-permute-start.9 = (bf16[8,16,1024]{2,1,0:T(8,128)(2,1)S(1)}, bf16[8,16,1024]{2,1,0:T(8,128)(2,1)S(1)}, u32[]{:S(2)}, u32[]{:S(2)}) collective-permute-start(bf16[8,16,1024]{2,1,0:T(8,128)(2,1)S(1)} %added.16), channel_id=1, source_target_pairs={{0,704},{64,0},{128,64},{192,128},{256,192},{320,256},{384,320},{4... | collective-permute-start | bytes 786440 | tf_op jit(solution)/shard_map/ppermute | solution.py:372
  50.2 2.2 %collective-permute-done.3.total_ref = bf16[8,16,1024]{2,1,0:T(8,128)(2,1)S(1)} collective-permute-done((bf16[8,16,1024]{2,1,0:T(8,128)(2,1)S(1)}, bf16[8,16,1024]{2,1,0:T(8,128)(2,1)S(1)}, u32[]{:S(2)}, u32[]{:S(2)}) %collective-permute-start.3) | collective-permute-done | bytes 262176 | tf_op jit(solution)/shard_map/ppermute | solution.py:368
  52.5 1.9 %collective-permute-start.4 = (bf16[8,16,1024]{2,1,0:T(8,128)(2,1)S(1)}, bf16[8,16,1024]{2,1,0:T(8,128)(2,1)S(1)}, u32[]{:S(2)}, u32[]{:S(2)}) collective-permute-start(bf16[8,16,1024]{2,1,0:T(8,128)(2,1)S(1)} %added.12), channel_id=1, source_target_pairs={{0,64},{64,128},{128,192},{192,256},{256,320},{320,384},{384,448},... | collective-permute-start | bytes 786440 | tf_op jit(solution)/shard_map/ppermute | solution.py:368
  54.6 5.2 %collective-permute-start.10 = (bf16[8,16,1024]{2,1,0:T(8,128)(2,1)S(1)}, bf16[8,16,1024]{2,1,0:T(8,128)(2,1)S(1)}, u32[]{:S(2)}, u32[]{:S(2)}) collective-permute-start(bf16[8,16,1024]{2,1,0:T(8,128)(2,1)S(1)} %added.17), channel_id=1, source_target_pairs={{0,704},{64,0},{128,64},{192,128},{256,192},{320,256},{384,320},{4... | collective-permute-start | bytes 786440 | tf_op jit(solution)/shard_map/ppermute | solution.py:372
  59.8 2.2 %collective-permute-done.4.total_ref = bf16[8,16,1024]{2,1,0:T(8,128)(2,1)S(1)} collective-permute-done((bf16[8,16,1024]{2,1,0:T(8,128)(2,1)S(1)}, bf16[8,16,1024]{2,1,0:T(8,128)(2,1)S(1)}, u32[]{:S(2)}, u32[]{:S(2)}) %collective-permute-start.4) | collective-permute-done | bytes 262176 | tf_op jit(solution)/shard_map/ppermute | solution.py:368
  62.1 1.9 %collective-permute-start.5 = (bf16[8,16,1024]{2,1,0:T(8,128)(2,1)S(1)}, bf16[8,16,1024]{2,1,0:T(8,128)(2,1)S(1)}, u32[]{:S(2)}, u32[]{:S(2)}) collective-permute-start(bf16[8,16,1024]{2,1,0:T(8,128)(2,1)S(1)} %added.13), channel_id=1, source_target_pairs={{0,64},{64,128},{128,192},{192,256},{256,320},{320,384},{384,448},... | collective-permute-start | bytes 786440 | tf_op jit(solution)/shard_map/ppermute | solution.py:368
  64.0 1.9 %assigned.1 = (s32[32]{0:T(128)S(1)}, s32[32]{0:T(128)S(1)}, s32[1]{0:T(128)}) custom-call(s32[1]{0:T(128)} %bitcast.here_ref, s32[1]{0:T(128)} %bitcast.1.slot_ref, s32[12,64]{1,0:T(8,128)S(1)} %copy-done), custom_call_target="tpu_custom_call" | custom-call | bytes 1024 | tf_op jit(solution)/shard_map/assigned/pallas_call | solution.py:62
  65.9 5.6 %collective-permute-done.5.below_ref = bf16[8,16,1024]{2,1,0:T(8,128)(2,1)S(1)} collective-permute-done((bf16[8,16,1024]{2,1,0:T(8,128)(2,1)S(1)}, bf16[8,16,1024]{2,1,0:T(8,128)(2,1)S(1)}, u32[]{:S(2)}, u32[]{:S(2)}) %collective-permute-start.5) | collective-permute-done | bytes 262176 | tf_op jit(solution)/shard_map/ppermute | solution.py:368
  72.5 23.6 %all_to_all.10.mine_ref = bf16[32,2,8,512]{3,2,1,0:T(8,128)(2,1)S(1)} all-to-all(bf16[32,2,8,512]{3,2,1,0:T(8,128)(2,1)S(1)} %outgoing.1), channel_id=1, replica_groups={{0,2,4,6,8,10,12,14,16,18,20,22,24,26,28,30,32,34,36,38,40,42,44,46,48,..., dimensions={0} | all-to-all | bytes 1048576 | tf_op jit(solution)/shard_map/all_to_all | solution.py:385
  96.1 1.9 %collective-permute-start.11 = (bf16[32,2,8,512]{3,2,1,0:T(8,128)(2,1)S(1)}, bf16[32,2,8,512]{3,2,1,0:T(8,128)(2,1)S(1)}, u32[]{:S(2)}, u32[]{:S(2)}) collective-permute-start(bf16[32,2,8,512]{3,2,1,0:T(8,128)(2,1)S(1)} %all_to_all.10.mine_ref), channel_id=1, source_target_pairs={{0,1},{1,0},{2,3},{3,2},{4,5},{5,4},{6,7},{7,6},{8,9},{9,8},{10,11... | collective-permute-start | bytes 1572872 | tf_op jit(solution)/shard_map/ppermute | solution.py:393
  98.0 1.9 %collective-permute-done.11.other_ref = bf16[32,2,8,512]{3,2,1,0:T(8,128)(2,1)S(1)} collective-permute-done((bf16[32,2,8,512]{3,2,1,0:T(8,128)(2,1)S(1)}, bf16[32,2,8,512]{3,2,1,0:T(8,128)(2,1)S(1)}, u32[]{:S(2)}, u32[]{:S(2)}) %collective-permute-start.11) | collective-permute-done | bytes 524320 | tf_op jit(solution)/shard_map/ppermute | solution.py:393
  99.9 4.1 %first_work.1 = (bf16[512,512]{1,0:T(8,128)(2,1)S(1)}, bf16[32,8,512]{2,1,0:T(8,128)(2,1)}) custom-call(s32[1]{0:T(128)S(6)} %select_n.7.core_ref, bf16[32,2,8,512]{3,2,1,0:T(8,128)(2,1)S(1)} %all_to_all.10.mine_ref, bf16[32,2,8,512]{3,2,1,0:T(8,128)(2,1)S(1)} %collective-permute-done.11.other_ref), custom_call_target="tpu_custom_call" | custom-call | flops 1879048192 | bytes 2097152 | tf_op jit(solution)/shard_map/first_work/pallas_call | solution.py:237
  103.9 4.7 %all-to-all-start.1 = ((bf16[32,8,512]{2,1,0:T(8,128)(2,1)}), bf16[32,8,512]{2,1,0:T(8,128)(2,1)S(1)}, u32[]{:S(2)}, u32[]{:S(2)}) async-start(bf16[32,8,512]{2,1,0:T(8,128)(2,1)} %get-tuple-element.21), calls=%async_computation.1 | async-start | bytes 524288 | tf_op jit(solution)/shard_map/all_to_all | solution.py:385
  110.2 11.0 %all-to-all-done.1.x_ref = bf16[32,8,512]{2,1,0:T(8,128)(2,1)S(1)} async-done(((bf16[32,8,512]{2,1,0:T(8,128)(2,1)}), bf16[32,8,512]{2,1,0:T(8,128)(2,1)S(1)}, u32[]{:S(2)}, u32[]{:S(2)}) %all-to-all-start.1) | async-done | bytes 262176 | tf_op jit(solution)/shard_map/all_to_all | solution.py:385
  (22 shorter events, 8.3 us)
Async XLA Ops:
  1.6 20.9 %collective-permute-start = (bf16[8,16,1024]{2,1,0:T(8,128)(2,1)S(1)}, bf16[8,16,1024]{2,1,0:T(8,128)(2,1)S(1)}, u32[]{:S(2)}, u32[]{:S(2)}) collective-permute-start(bf16[8,16,1024]{2,1,0:T(8,128)(2,1)S(1)} %picked.2), channel_id=1, source_target_pairs={{0,64},{64,128},{128,192},{192,256},{256,320},{320,384},{384,448},... | collective-permute-start | bytes 786440 | tf_op jit(solution)/shard_map/ppermute | solution.py:368
  6.9 17.8 %collective-permute-start.6 = (bf16[8,16,1024]{2,1,0:T(8,128)(2,1)S(1)}, bf16[8,16,1024]{2,1,0:T(8,128)(2,1)S(1)}, u32[]{:S(2)}, u32[]{:S(2)}) collective-permute-start(bf16[8,16,1024]{2,1,0:T(8,128)(2,1)S(1)} %picked.3), channel_id=1, source_target_pairs={{0,704},{64,0},{128,64},{192,128},{256,192},{320,256},{384,320},{4... | collective-permute-start | bytes 786440 | tf_op jit(solution)/shard_map/ppermute | solution.py:372
  22.6 10.6 %collective-permute-start.1 = (bf16[8,16,1024]{2,1,0:T(8,128)(2,1)S(1)}, bf16[8,16,1024]{2,1,0:T(8,128)(2,1)S(1)}, u32[]{:S(2)}, u32[]{:S(2)}) collective-permute-start(bf16[8,16,1024]{2,1,0:T(8,128)(2,1)S(1)} %added.9), channel_id=1, source_target_pairs={{0,64},{64,128},{128,192},{192,256},{256,320},{320,384},{384,448},... | collective-permute-start | bytes 786440 | tf_op jit(solution)/shard_map/ppermute | solution.py:368
  24.7 10.4 %collective-permute-start.7 = (bf16[8,16,1024]{2,1,0:T(8,128)(2,1)S(1)}, bf16[8,16,1024]{2,1,0:T(8,128)(2,1)S(1)}, u32[]{:S(2)}, u32[]{:S(2)}) collective-permute-start(bf16[8,16,1024]{2,1,0:T(8,128)(2,1)S(1)} %added.14), channel_id=1, source_target_pairs={{0,704},{64,0},{128,64},{192,128},{256,192},{320,256},{384,320},{4... | collective-permute-start | bytes 786440 | tf_op jit(solution)/shard_map/ppermute | solution.py:372
  33.2 9.7 %collective-permute-start.2 = (bf16[8,16,1024]{2,1,0:T(8,128)(2,1)S(1)}, bf16[8,16,1024]{2,1,0:T(8,128)(2,1)S(1)}, u32[]{:S(2)}, u32[]{:S(2)}) collective-permute-start(bf16[8,16,1024]{2,1,0:T(8,128)(2,1)S(1)} %added.10), channel_id=1, source_target_pairs={{0,64},{64,128},{128,192},{192,256},{256,320},{320,384},{384,448},... | collective-permute-start | bytes 786440 | tf_op jit(solution)/shard_map/ppermute | solution.py:368
  35.3 9.7 %collective-permute-start.8 = (bf16[8,16,1024]{2,1,0:T(8,128)(2,1)S(1)}, bf16[8,16,1024]{2,1,0:T(8,128)(2,1)S(1)}, u32[]{:S(2)}, u32[]{:S(2)}) collective-permute-start(bf16[8,16,1024]{2,1,0:T(8,128)(2,1)S(1)} %added.15), channel_id=1, source_target_pairs={{0,704},{64,0},{128,64},{192,128},{256,192},{320,256},{384,320},{4... | collective-permute-start | bytes 786440 | tf_op jit(solution)/shard_map/ppermute | solution.py:372
  43.0 9.5 %collective-permute-start.3 = (bf16[8,16,1024]{2,1,0:T(8,128)(2,1)S(1)}, bf16[8,16,1024]{2,1,0:T(8,128)(2,1)S(1)}, u32[]{:S(2)}, u32[]{:S(2)}) collective-permute-start(bf16[8,16,1024]{2,1,0:T(8,128)(2,1)S(1)} %added.11), channel_id=1, source_target_pairs={{0,64},{64,128},{128,192},{192,256},{256,320},{320,384},{384,448},... | collective-permute-start | bytes 786440 | tf_op jit(solution)/shard_map/ppermute | solution.py:368
  45.0 9.5 %collective-permute-start.9 = (bf16[8,16,1024]{2,1,0:T(8,128)(2,1)S(1)}, bf16[8,16,1024]{2,1,0:T(8,128)(2,1)S(1)}, u32[]{:S(2)}, u32[]{:S(2)}) collective-permute-start(bf16[8,16,1024]{2,1,0:T(8,128)(2,1)S(1)} %added.16), channel_id=1, source_target_pairs={{0,704},{64,0},{128,64},{192,128},{256,192},{320,256},{384,320},{4... | collective-permute-start | bytes 786440 | tf_op jit(solution)/shard_map/ppermute | solution.py:372
  52.5 11.5 %copy-start = (s32[12,64]{1,0:T(8,128)S(1)}, s32[12,64]{1,0:T(8,128)}, u32[]{:S(2)}) copy-start(s32[12,64]{1,0:T(8,128)} %table_ref.1) | copy-start | bytes 9220
  52.5 9.5 %collective-permute-start.4 = (bf16[8,16,1024]{2,1,0:T(8,128)(2,1)S(1)}, bf16[8,16,1024]{2,1,0:T(8,128)(2,1)S(1)}, u32[]{:S(2)}, u32[]{:S(2)}) collective-permute-start(bf16[8,16,1024]{2,1,0:T(8,128)(2,1)S(1)} %added.12), channel_id=1, source_target_pairs={{0,64},{64,128},{128,192},{192,256},{256,320},{320,384},{384,448},... | collective-permute-start | bytes 786440 | tf_op jit(solution)/shard_map/ppermute | solution.py:368
  54.6 11.4 %collective-permute-start.10 = (bf16[8,16,1024]{2,1,0:T(8,128)(2,1)S(1)}, bf16[8,16,1024]{2,1,0:T(8,128)(2,1)S(1)}, u32[]{:S(2)}, u32[]{:S(2)}) collective-permute-start(bf16[8,16,1024]{2,1,0:T(8,128)(2,1)S(1)} %added.17), channel_id=1, source_target_pairs={{0,704},{64,0},{128,64},{192,128},{256,192},{320,256},{384,320},{4... | collective-permute-start | bytes 786440 | tf_op jit(solution)/shard_map/ppermute | solution.py:372
  62.1 9.5 %collective-permute-start.5 = (bf16[8,16,1024]{2,1,0:T(8,128)(2,1)S(1)}, bf16[8,16,1024]{2,1,0:T(8,128)(2,1)S(1)}, u32[]{:S(2)}, u32[]{:S(2)}) collective-permute-start(bf16[8,16,1024]{2,1,0:T(8,128)(2,1)S(1)} %added.13), channel_id=1, source_target_pairs={{0,64},{64,128},{128,192},{192,256},{256,320},{320,384},{384,448},... | collective-permute-start | bytes 786440 | tf_op jit(solution)/shard_map/ppermute | solution.py:368
  96.1 3.8 %collective-permute-start.11 = (bf16[32,2,8,512]{3,2,1,0:T(8,128)(2,1)S(1)}, bf16[32,2,8,512]{3,2,1,0:T(8,128)(2,1)S(1)}, u32[]{:S(2)}, u32[]{:S(2)}) collective-permute-start(bf16[32,2,8,512]{3,2,1,0:T(8,128)(2,1)S(1)} %all_to_all.10.mine_ref), channel_id=1, source_target_pairs={{0,1},{1,0},{2,3},{3,2},{4,5},{5,4},{6,7},{7,6},{8,9},{9,8},{10,11... | collective-permute-start | bytes 1572872 | tf_op jit(solution)/shard_map/ppermute | solution.py:393
  103.9 17.3 %all-to-all-start.1 = ((bf16[32,8,512]{2,1,0:T(8,128)(2,1)}), bf16[32,8,512]{2,1,0:T(8,128)(2,1)S(1)}, u32[]{:S(2)}, u32[]{:S(2)}) async-start(bf16[32,8,512]{2,1,0:T(8,128)(2,1)} %get-tuple-element.21), calls=%async_computation.1 | async-start | bytes 524288 | tf_op jit(solution)/shard_map/all_to_all | solution.py:385

commit v9 on v8

--- a/solution.py
+++ b/solution.py
@@ -335,20 +335,23 @@
     )(here, parts)
 
 
-def added(here, total, parts, offset):
-    def kernel(here_ref, total_ref, parts_ref, out_ref):
+def added(here, total, parts, offset, more=None):
+    given = (total,) if more is None else (total, more)
+
+    def kernel(here_ref, parts_ref, *refs):
+        out_ref = refs[-1]
         own = part_of(parts_ref, here_ref, offset)[...].astype(F32)
-        out_ref[...] = (total_ref[...].astype(F32) + own).astype(BF16)
+        out_ref[...] = sum((x[...].astype(F32) for x in refs[:-1]), own).astype(BF16)
 
     return pl.pallas_call(
         kernel,
         out_shape=jax.ShapeDtypeStruct(total.shape, BF16),
-        in_specs=[smem(), vmem(), vmem()],
+        in_specs=[smem(), vmem()] + [vmem()] * len(given),
         out_specs=vmem(),
         compiler_params=params(),
         cost_estimate=cost(total.size, 6 * total.size),
         name="added",
-    )(here, total, parts)
+    )(here, parts, *given)
 
 
 def ring_terms(here, parts, axis):
@@ -357,19 +360,23 @@
     lowering = [(i, (i - 1) % n) for i in range(n)]
     hops = n // 2
     first = 2 * hops + 1 - n
-    below = picked(here, parts, hops)
-    below, parts = lax.optimization_barrier((below, parts))
-    above = picked(here, parts, (first - hops) % n)
-    above, parts = lax.optimization_barrier((above, parts))
+    skipping = [(i, (i + 2) % n) for i in range(n)]
+    near = picked(here, parts, hops - 1)
+    near, parts = lax.optimization_barrier((near, parts))
+    far, above = picked(here, parts, hops), picked(here, parts, (first - hops) % n)
+    far, above, parts = lax.optimization_barrier((far, above, parts))
     parts, own = staged(here, parts)
-    for step in range(hops):
-        if step > 0:
-            below = added(here, below, parts, hops - step)
-        below = lax.ppermute(below, axis, raising)
+    near = lax.ppermute(near, axis, raising)
+    far = lax.ppermute(far, axis, skipping)
+    below = added(here, near, parts, hops - 2, far)
+    for step in range(first, hops):
         if step > first:
             above = added(here, above, parts, (step - hops) % n)
-        if step >= first:
-            above = lax.ppermute(above, axis, lowering)
+        above = lax.ppermute(above, axis, lowering)
+        if step > first:
+            if step > first + 1:
+                below = added(here, below, parts, hops - step)
+            below = lax.ppermute(below, axis, raising)
     return below, above, own
 
 

time: 123 us -> 133 us (1.081)
  waiting for transfers between devices: 29.6 us -> 34.9 us
  Pallas kernels: 14.6 us -> 17.9 us
    ppermute x0 -> x2, waiting for transfers between devices: none -> 8.53 us  [the longest x1 6.33 us: ring_terms(): far = lax.ppermute(far, axis, skipping)]
    ppermute x6 -> x4, starting transfers between devices: 13.9 us -> 9.09 us  [ring_terms(): below = lax.ppermute(below, axis, raising)]
    ppermute x0 -> x2, starting transfers between devices: none -> 3.84 us  [the longest x1 1.92 us: ring_terms(): far = lax.ppermute(far, axis, skipping)]
    pallas_call x1, Pallas kernels: 1.6 us -> 3.94 us  [slot_work(): pl.pallas_call(kernel, out_shape=jax.ShapeDtypeStruct((2, BLK, BLK), BF16...]
    all_to_all x1, waiting for transfers between devices: 11 us -> 8.66 us  [exchanged(): lax.all_to_all(x, 'fsdp', split_axis=0, concat_axis=0, axis_index_groups=...]
    pallas_call x2 -> x3, Pallas kernels: 1.94 us -> 2.91 us  [picked(): pl.pallas_call(kernel, out_shape=jax.ShapeDtypeStruct(parts.shape[1:], BF...]
    ppermute x6 -> x4, waiting for transfers between devices: 16.6 us -> 15.9 us  [ring_terms(): below = lax.ppermute(below, axis, raising)]
  transfers between devices with their start and end apart: 13 -> 13, of which waited for: 9 -> 8; matrix products, arithmetic and copies ran while one was open for 0% -> 0% of each run, Pallas kernels for 6% -> 6%
where the time goes in v9:
time: 133 us; the launch traced here: 132 us
  starting transfers between devices  53.7 us (40%)
  waiting for transfers between devices  34.9 us (26%)
  blocking collectives  24.5 us (18%)
  Pallas kernels  17.9 us (13%)
    ppermute x5, starting transfers between devices, ring_terms(): above = lax.ppermute(above, axis, lowering)  34.4 us
    all_to_all x1, blocking collectives, exchanged(): lax.all_to_all(x, 'fsdp', split_axis=0, concat_axis=0, axis_index_groups=...  24.5 us
    ppermute x4, waiting for transfers between devices, ring_terms(): below = lax.ppermute(below, axis, raising)  15.9 us
    ppermute x4, starting transfers between devices, ring_terms(): below = lax.ppermute(below, axis, raising)  9.09 us
    all_to_all x1, waiting for transfers between devices, exchanged(): lax.all_to_all(x, 'fsdp', split_axis=0, concat_axis=0, axis_index_groups=...  8.66 us
    ppermute x1, waiting for transfers between devices, ring_terms(): far = lax.ppermute(far, axis, skipping)  6.33 us
    all_to_all x1, starting transfers between devices, exchanged(): lax.all_to_all(x, 'fsdp', split_axis=0, concat_axis=0, axis_index_groups=...  4.5 us
    pallas_call x1, Pallas kernels, first_work(): pl.pallas_call(kernel, out_shape=(jax.ShapeDtypeStruct((BLK, BLK), BF16),...  4.07 us
  transfers between devices with their start and end apart: 13, of which 8 were waited for; matrix products, arithmetic and copies ran while one was open for 0% of the time, Pallas kernels for 6%

profile of v9, /device:TPU:8, one launch (start us, length us, event | category | flops | bytes accessed | tf_op | source)
XLA Modules:
  0.0 132.0 jit_solution(15843540356553171297)
XLA Ops:
  3.6 14.6 %collective-permute-start.6 = (bf16[8,16,1024]{2,1,0:T(8,128)(2,1)S(1)}, bf16[8,16,1024]{2,1,0:T(8,128)(2,1)S(1)}, u32[]{:S(2)}, u32[]{:S(2)}) collective-permute-start(bf16[8,16,1024]{2,1,0:T(8,128)(2,1)S(1)} %picked.5), channel_id=1, source_target_pairs={{0,704},{64,0},{128,64},{192,128},{256,192},{320,256},{384,320},{4... | collective-permute-start | bytes 786440 | tf_op jit(solution)/shard_map/ppermute | solution.py:375
  18.2 1.9 %collective-permute-start.1 = (bf16[8,16,1024]{2,1,0:T(8,128)(2,1)S(1)}, bf16[8,16,1024]{2,1,0:T(8,128)(2,1)S(1)}, u32[]{:S(2)}, u32[]{:S(2)}) collective-permute-start(bf16[8,16,1024]{2,1,0:T(8,128)(2,1)S(1)} %picked.4), channel_id=1, source_target_pairs={{0,128},{64,192},{128,256},{192,320},{256,384},{320,448},{384,512}... | collective-permute-start | bytes 786440 | tf_op jit(solution)/shard_map/ppermute | solution.py:370
  20.1 1.9 %collective-permute-start = (bf16[8,16,1024]{2,1,0:T(8,128)(2,1)S(1)}, bf16[8,16,1024]{2,1,0:T(8,128)(2,1)S(1)}, u32[]{:S(2)}, u32[]{:S(2)}) collective-permute-start(bf16[8,16,1024]{2,1,0:T(8,128)(2,1)S(1)} %picked.3), channel_id=1, source_target_pairs={{0,64},{64,128},{128,192},{192,256},{256,320},{320,384},{384,448},... | collective-permute-start | bytes 786440 | tf_op jit(solution)/shard_map/ppermute | solution.py:369
  22.0 1.9 %staged.1 = (bf16[12,8,16,1024]{3,2,1,0:T(8,128)(2,1)S(1)}, bf16[8,16,1024]{2,1,0:T(8,128)(2,1)S(1)}) custom-call(s32[1]{0:T(128)} %bitcast.here_ref, bf16[12,8,16,1024]{3,2,1,0:T(8,128)(2,1)} %bitcast.8), custom_call_target="tpu_custom_call" | custom-call | bytes 6291456 | tf_op jit(solution)/shard_map/staged/pallas_call | solution.py:323
  24.0 5.3 %collective-permute-start.7 = (bf16[8,16,1024]{2,1,0:T(8,128)(2,1)S(1)}, bf16[8,16,1024]{2,1,0:T(8,128)(2,1)S(1)}, u32[]{:S(2)}, u32[]{:S(2)}) collective-permute-start(bf16[8,16,1024]{2,1,0:T(8,128)(2,1)S(1)} %added.12), channel_id=1, source_target_pairs={{0,704},{64,0},{128,64},{192,128},{256,192},{320,256},{384,320},{4... | collective-permute-start | bytes 786440 | tf_op jit(solution)/shard_map/ppermute | solution.py:375
  29.4 6.3 %collective-permute-done.1.refs_1_ = bf16[8,16,1024]{2,1,0:T(8,128)(2,1)S(1)} collective-permute-done((bf16[8,16,1024]{2,1,0:T(8,128)(2,1)S(1)}, bf16[8,16,1024]{2,1,0:T(8,128)(2,1)S(1)}, u32[]{:S(2)}, u32[]{:S(2)}) %collective-permute-start.1) | collective-permute-done | bytes 262176 | tf_op jit(solution)/shard_map/ppermute | solution.py:370
  35.7 2.2 %collective-permute-done.refs_0_ = bf16[8,16,1024]{2,1,0:T(8,128)(2,1)S(1)} collective-permute-done((bf16[8,16,1024]{2,1,0:T(8,128)(2,1)S(1)}, bf16[8,16,1024]{2,1,0:T(8,128)(2,1)S(1)}, u32[]{:S(2)}, u32[]{:S(2)}) %collective-permute-start) | collective-permute-done | bytes 262176 | tf_op jit(solution)/shard_map/ppermute | solution.py:369
  38.0 3.3 %collective-permute-start.2 = (bf16[8,16,1024]{2,1,0:T(8,128)(2,1)S(1)}, bf16[8,16,1024]{2,1,0:T(8,128)(2,1)S(1)}, u32[]{:S(2)}, u32[]{:S(2)}) collective-permute-start(bf16[8,16,1024]{2,1,0:T(8,128)(2,1)S(1)} %added.8), channel_id=1, source_target_pairs={{0,64},{64,128},{128,192},{192,256},{256,320},{320,384},{384,448},... | collective-permute-start | bytes 786440 | tf_op jit(solution)/shard_map/ppermute | solution.py:379
  41.5 4.2 %collective-permute-start.8 = (bf16[8,16,1024]{2,1,0:T(8,128)(2,1)S(1)}, bf16[8,16,1024]{2,1,0:T(8,128)(2,1)S(1)}, u32[]{:S(2)}, u32[]{:S(2)}) collective-permute-start(bf16[8,16,1024]{2,1,0:T(8,128)(2,1)S(1)} %added.13), channel_id=1, source_target_pairs={{0,704},{64,0},{128,64},{192,128},{256,192},{320,256},{384,320},{4... | collective-permute-start | bytes 786440 | tf_op jit(solution)/shard_map/ppermute | solution.py:375
  45.7 4.3 %collective-permute-done.2.refs_0_ = bf16[8,16,1024]{2,1,0:T(8,128)(2,1)S(1)} collective-permute-done((bf16[8,16,1024]{2,1,0:T(8,128)(2,1)S(1)}, bf16[8,16,1024]{2,1,0:T(8,128)(2,1)S(1)}, u32[]{:S(2)}, u32[]{:S(2)}) %collective-permute-start.2) | collective-permute-done | bytes 262176 | tf_op jit(solution)/shard_map/ppermute | solution.py:379
  50.0 1.9 %collective-permute-start.3 = (bf16[8,16,1024]{2,1,0:T(8,128)(2,1)S(1)}, bf16[8,16,1024]{2,1,0:T(8,128)(2,1)S(1)}, u32[]{:S(2)}, u32[]{:S(2)}) collective-permute-start(bf16[8,16,1024]{2,1,0:T(8,128)(2,1)S(1)} %added.9), channel_id=1, source_target_pairs={{0,64},{64,128},{128,192},{192,256},{256,320},{320,384},{384,448},... | collective-permute-start | bytes 786440 | tf_op jit(solution)/shard_map/ppermute | solution.py:379
  52.0 5.1 %collective-permute-start.9 = (bf16[8,16,1024]{2,1,0:T(8,128)(2,1)S(1)}, bf16[8,16,1024]{2,1,0:T(8,128)(2,1)S(1)}, u32[]{:S(2)}, u32[]{:S(2)}) collective-permute-start(bf16[8,16,1024]{2,1,0:T(8,128)(2,1)S(1)} %added.14), channel_id=1, source_target_pairs={{0,704},{64,0},{128,64},{192,128},{256,192},{320,256},{384,320},{4... | collective-permute-start | bytes 786440 | tf_op jit(solution)/shard_map/ppermute | solution.py:375
  57.2 3.4 %collective-permute-done.3.refs_0_ = bf16[8,16,1024]{2,1,0:T(8,128)(2,1)S(1)} collective-permute-done((bf16[8,16,1024]{2,1,0:T(8,128)(2,1)S(1)}, bf16[8,16,1024]{2,1,0:T(8,128)(2,1)S(1)}, u32[]{:S(2)}, u32[]{:S(2)}) %collective-permute-start.3) | collective-permute-done | bytes 262176 | tf_op jit(solution)/shard_map/ppermute | solution.py:379
  60.7 1.9 %collective-permute-start.4 = (bf16[8,16,1024]{2,1,0:T(8,128)(2,1)S(1)}, bf16[8,16,1024]{2,1,0:T(8,128)(2,1)S(1)}, u32[]{:S(2)}, u32[]{:S(2)}) collective-permute-start(bf16[8,16,1024]{2,1,0:T(8,128)(2,1)S(1)} %added.10), channel_id=1, source_target_pairs={{0,64},{64,128},{128,192},{192,256},{256,320},{320,384},{384,448},... | collective-permute-start | bytes 786440 | tf_op jit(solution)/shard_map/ppermute | solution.py:379
  62.7 5.1 %collective-permute-start.10 = (bf16[8,16,1024]{2,1,0:T(8,128)(2,1)S(1)}, bf16[8,16,1024]{2,1,0:T(8,128)(2,1)S(1)}, u32[]{:S(2)}, u32[]{:S(2)}) collective-permute-start(bf16[8,16,1024]{2,1,0:T(8,128)(2,1)S(1)} %added.15), channel_id=1, source_target_pairs={{0,704},{64,0},{128,64},{192,128},{256,192},{320,256},{384,320},{4... | collective-permute-start | bytes 786440 | tf_op jit(solution)/shard_map/ppermute | solution.py:375
  67.9 2.5 %collective-permute-done.4.refs_0_ = bf16[8,16,1024]{2,1,0:T(8,128)(2,1)S(1)} collective-permute-done((bf16[8,16,1024]{2,1,0:T(8,128)(2,1)S(1)}, bf16[8,16,1024]{2,1,0:T(8,128)(2,1)S(1)}, u32[]{:S(2)}, u32[]{:S(2)}) %collective-permute-start.4) | collective-permute-done | bytes 262176 | tf_op jit(solution)/shard_map/ppermute | solution.py:379
  70.5 1.9 %collective-permute-start.5 = (bf16[8,16,1024]{2,1,0:T(8,128)(2,1)S(1)}, bf16[8,16,1024]{2,1,0:T(8,128)(2,1)S(1)}, u32[]{:S(2)}, u32[]{:S(2)}) collective-permute-start(bf16[8,16,1024]{2,1,0:T(8,128)(2,1)S(1)} %added.11), channel_id=1, source_target_pairs={{0,64},{64,128},{128,192},{192,256},{256,320},{320,384},{384,448},... | collective-permute-start | bytes 786440 | tf_op jit(solution)/shard_map/ppermute | solution.py:379
  74.3 5.6 %collective-permute-done.5.below_ref = bf16[8,16,1024]{2,1,0:T(8,128)(2,1)S(1)} collective-permute-done((bf16[8,16,1024]{2,1,0:T(8,128)(2,1)S(1)}, bf16[8,16,1024]{2,1,0:T(8,128)(2,1)S(1)}, u32[]{:S(2)}, u32[]{:S(2)}) %collective-permute-start.5) | collective-permute-done | bytes 262176 | tf_op jit(solution)/shard_map/ppermute | solution.py:379
  80.9 24.5 %all_to_all.10.mine_ref = bf16[32,2,8,512]{3,2,1,0:T(8,128)(2,1)S(1)} all-to-all(bf16[32,2,8,512]{3,2,1,0:T(8,128)(2,1)S(1)} %outgoing.1), channel_id=1, replica_groups={{0,2,4,6,8,10,12,14,16,18,20,22,24,26,28,30,32,34,36,38,40,42,44,46,48,..., dimensions={0} | all-to-all | bytes 1048576 | tf_op jit(solution)/shard_map/all_to_all | solution.py:392
  105.4 1.9 %collective-permute-start.11 = (bf16[32,2,8,512]{3,2,1,0:T(8,128)(2,1)S(1)}, bf16[32,2,8,512]{3,2,1,0:T(8,128)(2,1)S(1)}, u32[]{:S(2)}, u32[]{:S(2)}) collective-permute-start(bf16[32,2,8,512]{3,2,1,0:T(8,128)(2,1)S(1)} %all_to_all.10.mine_ref), channel_id=1, source_target_pairs={{0,1},{1,0},{2,3},{3,2},{4,5},{5,4},{6,7},{7,6},{8,9},{9,8},{10,11... | collective-permute-start | bytes 1572872 | tf_op jit(solution)/shard_map/ppermute | solution.py:400
  109.2 4.1 %first_work.1 = (bf16[512,512]{1,0:T(8,128)(2,1)S(1)}, bf16[32,8,512]{2,1,0:T(8,128)(2,1)}) custom-call(s32[1]{0:T(128)S(6)} %select_n.7.core_ref, bf16[32,2,8,512]{3,2,1,0:T(8,128)(2,1)S(1)} %all_to_all.10.mine_ref, bf16[32,2,8,512]{3,2,1,0:T(8,128)(2,1)S(1)} %collective-permute-done.11.other_ref), custom_call_target="tpu_custom_call" | custom-call | flops 1879048192 | bytes 2097152 | tf_op jit(solution)/shard_map/first_work/pallas_call | solution.py:237
  113.3 4.5 %all-to-all-start.1 = ((bf16[32,8,512]{2,1,0:T(8,128)(2,1)}), bf16[32,8,512]{2,1,0:T(8,128)(2,1)S(1)}, u32[]{:S(2)}, u32[]{:S(2)}) async-start(bf16[32,8,512]{2,1,0:T(8,128)(2,1)} %get-tuple-element.23), calls=%async_computation.1 | async-start | bytes 524288 | tf_op jit(solution)/shard_map/all_to_all | solution.py:392
  117.8 3.9 %slot_work.1 = bf16[2,512,512]{2,1,0:T(8,128)(2,1)} custom-call(s32[1]{0:T(128)} %get-tuple-element.24.mode_ref, s32[1]{0:T(128)S(6)} %select_n.7.core_ref, bf16[32,2,8,512]{3,2,1,0:T(8,128)(2,1)S(1)} %all_to_all.10.mine_ref, bf16[32,2,8,512]{3,2,1,0:T(8,128)(2,1)S(1)} %collective-permute-done.11.other_ref, bf16[512,512]{1,0:T(8,128)(2,1)S(1)} %get-tuple-element.25.right_ref), custom_call_target="tpu_custom_call" | custom-call | flops 2684354560 | bytes 2097152 | tf_op jit(solution)/shard_map/slot_work/pallas_call | solution.py:278
  121.7 8.7 %all-to-all-done.1.x_ref = bf16[32,8,512]{2,1,0:T(8,128)(2,1)S(1)} async-done(((bf16[32,8,512]{2,1,0:T(8,128)(2,1)}), bf16[32,8,512]{2,1,0:T(8,128)(2,1)S(1)}, u32[]{:S(2)}, u32[]{:S(2)}) %all-to-all-start.1) | async-done | bytes 262176 | tf_op jit(solution)/shard_map/all_to_all | solution.py:392
  (22 shorter events, 9.8 us)
Async XLA Ops:
  3.6 20.4 %collective-permute-start.6 = (bf16[8,16,1024]{2,1,0:T(8,128)(2,1)S(1)}, bf16[8,16,1024]{2,1,0:T(8,128)(2,1)S(1)}, u32[]{:S(2)}, u32[]{:S(2)}) collective-permute-start(bf16[8,16,1024]{2,1,0:T(8,128)(2,1)S(1)} %picked.5), channel_id=1, source_target_pairs={{0,704},{64,0},{128,64},{192,128},{256,192},{320,256},{384,320},{4... | collective-permute-start | bytes 786440 | tf_op jit(solution)/shard_map/ppermute | solution.py:375
  18.2 17.6 %collective-permute-start.1 = (bf16[8,16,1024]{2,1,0:T(8,128)(2,1)S(1)}, bf16[8,16,1024]{2,1,0:T(8,128)(2,1)S(1)}, u32[]{:S(2)}, u32[]{:S(2)}) collective-permute-start(bf16[8,16,1024]{2,1,0:T(8,128)(2,1)S(1)} %picked.4), channel_id=1, source_target_pairs={{0,128},{64,192},{128,256},{192,320},{256,384},{320,448},{384,512}... | collective-permute-start | bytes 786440 | tf_op jit(solution)/shard_map/ppermute | solution.py:370
  20.1 17.8 %collective-permute-start = (bf16[8,16,1024]{2,1,0:T(8,128)(2,1)S(1)}, bf16[8,16,1024]{2,1,0:T(8,128)(2,1)S(1)}, u32[]{:S(2)}, u32[]{:S(2)}) collective-permute-start(bf16[8,16,1024]{2,1,0:T(8,128)(2,1)S(1)} %picked.3), channel_id=1, source_target_pairs={{0,64},{64,128},{128,192},{192,256},{256,320},{320,384},{384,448},... | collective-permute-start | bytes 786440 | tf_op jit(solution)/shard_map/ppermute | solution.py:369
  24.0 17.3 %collective-permute-start.7 = (bf16[8,16,1024]{2,1,0:T(8,128)(2,1)S(1)}, bf16[8,16,1024]{2,1,0:T(8,128)(2,1)S(1)}, u32[]{:S(2)}, u32[]{:S(2)}) collective-permute-start(bf16[8,16,1024]{2,1,0:T(8,128)(2,1)S(1)} %added.12), channel_id=1, source_target_pairs={{0,704},{64,0},{128,64},{192,128},{256,192},{320,256},{384,320},{4... | collective-permute-start | bytes 786440 | tf_op jit(solution)/shard_map/ppermute | solution.py:375
  38.0 11.9 %collective-permute-start.2 = (bf16[8,16,1024]{2,1,0:T(8,128)(2,1)S(1)}, bf16[8,16,1024]{2,1,0:T(8,128)(2,1)S(1)}, u32[]{:S(2)}, u32[]{:S(2)}) collective-permute-start(bf16[8,16,1024]{2,1,0:T(8,128)(2,1)S(1)} %added.8), channel_id=1, source_target_pairs={{0,64},{64,128},{128,192},{192,256},{256,320},{320,384},{384,448},... | collective-permute-start | bytes 786440 | tf_op jit(solution)/shard_map/ppermute | solution.py:379
  41.5 10.5 %collective-permute-start.8 = (bf16[8,16,1024]{2,1,0:T(8,128)(2,1)S(1)}, bf16[8,16,1024]{2,1,0:T(8,128)(2,1)S(1)}, u32[]{:S(2)}, u32[]{:S(2)}) collective-permute-start(bf16[8,16,1024]{2,1,0:T(8,128)(2,1)S(1)} %added.13), channel_id=1, source_target_pairs={{0,704},{64,0},{128,64},{192,128},{256,192},{320,256},{384,320},{4... | collective-permute-start | bytes 786440 | tf_op jit(solution)/shard_map/ppermute | solution.py:375
  50.0 10.6 %collective-permute-start.3 = (bf16[8,16,1024]{2,1,0:T(8,128)(2,1)S(1)}, bf16[8,16,1024]{2,1,0:T(8,128)(2,1)S(1)}, u32[]{:S(2)}, u32[]{:S(2)}) collective-permute-start(bf16[8,16,1024]{2,1,0:T(8,128)(2,1)S(1)} %added.9), channel_id=1, source_target_pairs={{0,64},{64,128},{128,192},{192,256},{256,320},{320,384},{384,448},... | collective-permute-start | bytes 786440 | tf_op jit(solution)/shard_map/ppermute | solution.py:379
  52.0 10.6 %collective-permute-start.9 = (bf16[8,16,1024]{2,1,0:T(8,128)(2,1)S(1)}, bf16[8,16,1024]{2,1,0:T(8,128)(2,1)S(1)}, u32[]{:S(2)}, u32[]{:S(2)}) collective-permute-start(bf16[8,16,1024]{2,1,0:T(8,128)(2,1)S(1)} %added.14), channel_id=1, source_target_pairs={{0,704},{64,0},{128,64},{192,128},{256,192},{320,256},{384,320},{4... | collective-permute-start | bytes 786440 | tf_op jit(solution)/shard_map/ppermute | solution.py:375
  60.7 11.7 %copy-start = (s32[12,64]{1,0:T(8,128)S(1)}, s32[12,64]{1,0:T(8,128)}, u32[]{:S(2)}) copy-start(s32[12,64]{1,0:T(8,128)} %table_ref.1) | copy-start | bytes 9220
  60.7 9.7 %collective-permute-start.4 = (bf16[8,16,1024]{2,1,0:T(8,128)(2,1)S(1)}, bf16[8,16,1024]{2,1,0:T(8,128)(2,1)S(1)}, u32[]{:S(2)}, u32[]{:S(2)}) collective-permute-start(bf16[8,16,1024]{2,1,0:T(8,128)(2,1)S(1)} %added.10), channel_id=1, source_target_pairs={{0,64},{64,128},{128,192},{192,256},{256,320},{320,384},{384,448},... | collective-permute-start | bytes 786440 | tf_op jit(solution)/shard_map/ppermute | solution.py:379
  62.7 11.6 %collective-permute-start.10 = (bf16[8,16,1024]{2,1,0:T(8,128)(2,1)S(1)}, bf16[8,16,1024]{2,1,0:T(8,128)(2,1)S(1)}, u32[]{:S(2)}, u32[]{:S(2)}) collective-permute-start(bf16[8,16,1024]{2,1,0:T(8,128)(2,1)S(1)} %added.15), channel_id=1, source_target_pairs={{0,704},{64,0},{128,64},{192,128},{256,192},{320,256},{384,320},{4... | collective-permute-start | bytes 786440 | tf_op jit(solution)/shard_map/ppermute | solution.py:375
  70.5 9.5 %collective-permute-start.5 = (bf16[8,16,1024]{2,1,0:T(8,128)(2,1)S(1)}, bf16[8,16,1024]{2,1,0:T(8,128)(2,1)S(1)}, u32[]{:S(2)}, u32[]{:S(2)}) collective-permute-start(bf16[8,16,1024]{2,1,0:T(8,128)(2,1)S(1)} %added.11), channel_id=1, source_target_pairs={{0,64},{64,128},{128,192},{192,256},{256,320},{320,384},{384,448},... | collective-permute-start | bytes 786440 | tf_op jit(solution)/shard_map/ppermute | solution.py:379
  105.4 3.8 %collective-permute-start.11 = (bf16[32,2,8,512]{3,2,1,0:T(8,128)(2,1)S(1)}, bf16[32,2,8,512]{3,2,1,0:T(8,128)(2,1)S(1)}, u32[]{:S(2)}, u32[]{:S(2)}) collective-permute-start(bf16[32,2,8,512]{3,2,1,0:T(8,128)(2,1)S(1)} %all_to_all.10.mine_ref), channel_id=1, source_target_pairs={{0,1},{1,0},{2,3},{3,2},{4,5},{5,4},{6,7},{7,6},{8,9},{9,8},{10,11... | collective-permute-start | bytes 1572872 | tf_op jit(solution)/shard_map/ppermute | solution.py:400
  113.3 17.1 %all-to-all-start.1 = ((bf16[32,8,512]{2,1,0:T(8,128)(2,1)}), bf16[32,8,512]{2,1,0:T(8,128)(2,1)S(1)}, u32[]{:S(2)}, u32[]{:S(2)}) async-start(bf16[32,8,512]{2,1,0:T(8,128)(2,1)} %get-tuple-element.23), calls=%async_computation.1 | async-start | bytes 524288 | tf_op jit(solution)/shard_map/all_to_all | solution.py:392
